TPU v7x, 128 devices: a whole 4x4x4 slice. The times are simulated.
128 devices in a mesh: blk: 16 (over z, y), sub: 8 (over x, core).
Axes of the slice: x: 4, y: 4, z: 4, core: 2. Of those that a mesh axis runs over, the one named last changes fastest.
Arguments:
- synthetic: bfloat16 [16384, 3, 1024], P(('blk', 'sub')), may hold values from -6 to 6
- observed: bfloat16 [16384, 3, 1024], P(('blk', 'sub')), may hold values from -6 to 6
- pair_first: int32 [256, 1024], P('blk', 'sub'), may hold values from 0 to 16383, as said below
- pair_second: int32 [256, 1024], P('blk', 'sub'), may hold values from 0 to 16383, as said below
- pair_mask: int32 [256, 1024], P('blk', 'sub'), may hold values 0 or 1
- pair_weight: float32 [256, 1024], P('blk', 'sub'), may hold values from 0.2 to 2
- station_owner: int32 [16384, 1], P(('blk', 'sub')), may hold values from 0 to 127; in each aligned block of 128 rows (0 to 127, 128 to 255, ...) at most 2 rows name the same one
- station_element: int32 [16384], P(('blk', 'sub')), may hold values from 0 to 127
Outputs:
- delivered: float32 [16384, 3, 1024], P(('blk', 'sub'))
Inputs may be any that keep to these rules, and one draw needn't show every extreme that they name: `pair_first`: the slots of block j name first stations of block j, stations j * 64 to j * 64 + 63. `pair_second`: the second station is the first plus 1 to 63; where that passes the last station it is taken modulo 64 inside the first station's block. `station_owner`: among the 128 stations of one device, at most 2 have the same owner, and some owner has exactly 2.
All inputs are finite; a program needn't handle non-finite values. No bound on the sum of `pair_mask` on one device may be relied on, other than what follows from the above.
Results may differ from a plain program's by a relative error of at most 0.0045.
Values may be sent and summed in bfloat16 or wider, within the bound.
A program may use at most 128 MiB of HBM per device.

v0:
```python
import math

import jax
import jax.numpy as jnp
from jax import lax
from jax.sharding import PartitionSpec as P

ELEM_DEV = 128
NF = 128
BLOCK = 64


def passed_along(x, axis, by):
    size = lax.axis_size(axis)
    pairs = [(i, i + by) for i in range(size) if 0 <= i + by < size]
    return lax.ppermute(x, axis, pairs)


def dft_tables(samples, freqs):
    sample_index = jnp.arange(samples, dtype=jnp.int32)
    orders = jnp.arange(freqs, dtype=jnp.int32)
    phase_index = sample_index[:, None] * orders[None, :] % samples
    angles = phase_index.astype(jnp.float32) * (2.0 * math.pi / samples)
    norm_scale = 1.0 / math.sqrt(samples)
    cosine = jnp.cos(angles) * norm_scale
    sine_part = jnp.sin(angles) * norm_scale
    forward_table = jnp.concatenate([cosine, -sine_part], axis=1).astype(jnp.bfloat16)
    doubled = jnp.where(orders == 0, 1.0, 2.0).astype(jnp.float32)
    inverse_table = jnp.concatenate(
        [cosine.T * doubled[:, None], -sine_part.T * doubled[:, None]], axis=0
    )
    return (forward_table, inverse_table)


def spectra(traces, forward_table):
    station_count = traces.shape[0]
    stacked = traces.reshape(station_count * 3, traces.shape[2])
    result = jnp.dot(stacked, forward_table, preferred_element_type=jnp.float32).astype(
        jnp.bfloat16
    )
    return result.reshape(station_count, 3, 2, forward_table.shape[1] // 2)


def pair_terms(first_rows, second_rows, weights):
    left_re = first_rows[:, :, 0]
    left_im = first_rows[:, :, 1]
    right_re = second_rows[:, :, 0]
    right_im = second_rows[:, :, 1]
    cross_re = left_re * right_re + left_im * right_im
    cross_im = left_im * right_re - left_re * right_im
    weighted = weights[:, None, None]
    resid_re = (cross_re[:, :3] - cross_re[:, 3:]) * weighted
    resid_im = (cross_im[:, :3] - cross_im[:, 3:]) * weighted
    first_re = resid_re * right_re[:, :3] - resid_im * right_im[:, :3]
    first_im = resid_re * right_im[:, :3] + resid_im * right_re[:, :3]
    second_re = resid_re * left_re[:, :3] + resid_im * left_im[:, :3]
    second_im = resid_re * left_im[:, :3] - resid_im * left_re[:, :3]
    return (jnp.stack([first_re, first_im], axis=2), jnp.stack([second_re, second_im], axis=2))


def group_fetch(rows):
    return passed_along(rows, "blk", -1)


def group_return(rows):
    return passed_along(rows, "blk", 1)


def pair_work(group_table, first_ids, second_ids, weights, group_start, fetch_rim, return_rim):
    group_rows = group_table.shape[0]
    block_count = first_ids.shape[0]
    slot_count = first_ids.shape[1]
    tail_shape = group_table.shape[1:]
    rim_rows = fetch_rim(group_table[:BLOCK])
    extended = jnp.concatenate([group_table, rim_rows], axis=0)
    lower = extended[:group_rows].reshape(block_count, BLOCK, -1)
    upper = extended[BLOCK:].reshape(block_count, BLOCK, -1)
    windows = jnp.concatenate([lower, upper], axis=1)
    base = group_start + jnp.arange(block_count, dtype=jnp.int32)[:, None] * BLOCK
    window_index = jnp.arange(2 * BLOCK, dtype=jnp.int32)
    first_match = (first_ids - base)[:, :, None] == window_index[None, None, :]
    second_match = (second_ids - base)[:, :, None] == window_index[None, None, :]
    first_rows = jnp.einsum(
        "bpw,bwf->bpf",
        first_match.astype(jnp.bfloat16),
        windows,
        preferred_element_type=jnp.float32,
    )
    second_rows = jnp.einsum(
        "bpw,bwf->bpf",
        second_match.astype(jnp.bfloat16),
        windows,
        preferred_element_type=jnp.float32,
    )
    first_terms, second_terms = pair_terms(
        first_rows.reshape((block_count * slot_count,) + tail_shape),
        second_rows.reshape((block_count * slot_count,) + tail_shape),
        weights.reshape(-1),
    )
    term_width = first_terms.shape[1] * first_terms.shape[2] * first_terms.shape[3]
    window_sums = jnp.einsum(
        "bpw,bpf->bwf",
        first_match.astype(jnp.float32),
        first_terms.reshape(block_count, slot_count, term_width),
        precision=lax.Precision.HIGHEST,
        preferred_element_type=jnp.float32,
    )
    window_sums = window_sums + jnp.einsum(
        "bpw,bpf->bwf",
        second_match.astype(jnp.float32),
        second_terms.reshape(block_count, slot_count, term_width),
        precision=lax.Precision.HIGHEST,
        preferred_element_type=jnp.float32,
    )
    lower_sums = window_sums[:, :BLOCK].reshape(group_rows, term_width)
    upper_sums = window_sums[:, BLOCK:].reshape(group_rows, term_width)
    accumulated = jnp.pad(lower_sums, ((0, BLOCK), (0, 0))) + jnp.pad(
        upper_sums, ((BLOCK, 0), (0, 0))
    )
    accumulated = accumulated.reshape((group_rows + BLOCK,) + first_terms.shape[1:])
    returned = return_rim(accumulated[group_rows:])
    padded_back = jnp.pad(returned, ((0, group_rows - BLOCK), (0, 0), (0, 0), (0, 0)))
    return accumulated[:group_rows] + padded_back


def on_device(
    synthetic,
    observed,
    pair_first,
    pair_second,
    pair_mask,
    pair_weight,
    station_owner,
    station_element,
):
    samples = synthetic.shape[2]
    stations_here = synthetic.shape[0]
    sub_count = lax.axis_size("sub")
    blk_count = lax.axis_size("blk")
    group_start = lax.axis_index("blk") * (stations_here * sub_count)
    forward_table, inverse_table = dft_tables(samples, NF)
    spectrum_table = jnp.concatenate(
        [spectra(synthetic, forward_table), spectra(observed, forward_table)], axis=1
    )
    effective = pair_weight * pair_mask.astype(jnp.float32)
    gathered = lax.all_gather(spectrum_table, "sub", axis=0, tiled=True)
    partial_sums = pair_work(
        gathered, pair_first, pair_second, effective, group_start, group_fetch, group_return
    )
    adjoint_spectra = lax.psum_scatter(partial_sums, "sub", scatter_dimension=0, tiled=True)
    payload = jnp.dot(
        adjoint_spectra.reshape(stations_here * 3, 2 * NF),
        inverse_table,
        precision=lax.Precision.HIGHEST,
        preferred_element_type=jnp.float32,
    ).reshape(stations_here, 3, samples)
    width = payload.shape[2]
    devices = blk_count * sub_count
    slots = max(2, (2 * stations_here + devices - 1) // devices)
    owners = station_owner[:, 0]
    positions = jnp.arange(stations_here, dtype=jnp.int32)
    same_owner = owners[:, None] == owners[None, :]
    earlier = positions[None, :] < positions[:, None]
    slot_rank = jnp.sum((same_owner & earlier).astype(jnp.int32), axis=1)
    target_slot = owners * slots + slot_rank
    slot_index = jnp.arange(devices * slots, dtype=jnp.int32)
    placement = slot_index[:, None] == target_slot[None, :]
    outgoing = jnp.dot(
        placement.astype(jnp.float32),
        payload.reshape(stations_here, 3 * width),
        precision=lax.Precision.HIGHEST,
        preferred_element_type=jnp.float32,
    ).reshape(devices, slots, 3, width)
    occupied = jnp.sum(placement.astype(jnp.int32), axis=1)
    labels = (
        jnp.sum(placement.astype(jnp.int32) * station_element[None, :], axis=1)
        + ELEM_DEV * (1 - occupied)
    ).reshape(devices, slots)
    received, received_labels = (
        lax.all_to_all(outgoing, ("blk", "sub"), split_axis=0, concat_axis=0, tiled=True),
        lax.all_to_all(labels, ("blk", "sub"), split_axis=0, concat_axis=0, tiled=True),
    )
    incoming = received.reshape(-1, 3 * width)
    incoming_labels = received_labels.reshape(-1)
    element_index = jnp.arange(ELEM_DEV, dtype=jnp.int32)
    collect = (element_index[:, None] == incoming_labels[None, :]).astype(jnp.float32)
    summed = jnp.dot(
        collect, incoming, precision=lax.Precision.HIGHEST, preferred_element_type=jnp.float32
    )
    delivered = summed.reshape(ELEM_DEV, 3, width)
    return delivered


def solution(mesh):
    return jax.shard_map(
        on_device,
        mesh=mesh,
        in_specs=(
            P(("blk", "sub"), None, None),
            P(("blk", "sub"), None, None),
            P("blk", "sub"),
            P("blk", "sub"),
            P("blk", "sub"),
            P("blk", "sub"),
            P(("blk", "sub"), None),
            P(("blk", "sub")),
        ),
        out_specs=P(("blk", "sub"), None, None),
        check_vma=False,
    )
```

profile of v0, /device:TPU:1, one launch (start us, length us, event | category | flops | bytes accessed | tf_op | source)
XLA Modules:
  0.0 442.0 jit_solution(3131575002965724886)
XLA Ops:
  6.5 2.2 negate_convert_fusion
  8.8 1.9 copy.68
  16.3 30.7 %all-gather.2.cloned.1.call-done = bf16[1024,6,2,128]{3,2,1,0:T(2,128)(2,1)} async-done(((bf16[128,6,2,128]{3,2,1,0:T(2,128)(2,1)}), bf16[1024,6,2,128]{3,2,1,0:T(2,128)(2,1)}) %all-gather.2.cloned.1.call-update) | async-done | bytes 3145744 | tf_op jit(solution)/shard_map/all_gather | solution.py:146
  48.1 1.5 collective-permute-start
  49.5 6.8 %reshape.131 = bf16[16,64,1536]{2,1,0:T(8,128)(2,1)S(1)} reshape(bf16[1024,6,2,128]{3,2,1,0:T(2,128)(2,1)} %all-gather.2.cloned.1.call-done) | data formatting | bytes 6291456 | tf_op jit(solution)/shard_map/reshape | solution.py:76
  56.3 2.0 constant_dynamic-update-slice_fusion.1
  59.3 4.0 pad_maximum_fusion.2
  63.4 2.7 reshape.132
  66.1 3.8 constant_dynamic-update-slice_fusion
  69.9 9.2 %fusion.9 = f32[16,128,1536]{2,1,0:T(8,128)} fusion(bf16[16,128,1536]{2,1,0:T(8,128)(2,1)} %constant_dynamic-update-slice_fusion, s32[16,128]{1,0:T(8,128)S(1)} %get-tuple-element.21), kind=kOutput, calls=%fused_computation.31 | convolution fusion | flops 805568512 | bytes 18882560 | tf_op jit(solution)/shard_map/bpw,bwf->bpf/dot_general | solution.py:89
  79.1 15.2 %reshape.134 = f32[2048,6,2,128]{3,2,1,0:T(2,128)} reshape(f32[16,128,1536]{2,1,0:T(8,128)} %fusion.9) | data formatting | bytes 25165824 | tf_op jit(solution)/shard_map/reshape | solution.py:97
  94.3 15.7 %fusion.45 = (f32[2048,6,1,128]{3,2,1,0:T(1,128)}, f32[2048,6,1,128]{3,2,1,0:T(1,128)}) fusion(f32[2048,6,2,128]{3,2,1,0:T(2,128)} %reshape.134), kind=kLoop, calls=%fused_computation.96 | loop fusion | bytes 25165824 | tf_op jit(solution)/shard_map/slice | solution.py:48
  110.1 6.4 %fusion.11 = f32[16,128,1536]{2,1,0:T(8,128)} fusion(bf16[16,128,1536]{2,1,0:T(8,128)(2,1)S(1)} %bitcast.80, s32[16,128]{1,0:T(8,128)S(1)} %get-tuple-element.22), kind=kOutput, calls=%fused_computation.34 | convolution fusion | flops 805568512 | bytes 18882560 | tf_op jit(solution)/shard_map/bpw,bwf->bpf/dot_general | solution.py:83
  116.5 15.1 %reshape.133 = f32[2048,6,2,128]{3,2,1,0:T(2,128)} reshape(f32[16,128,1536]{2,1,0:T(8,128)} %fusion.11) | data formatting | bytes 25165824 | tf_op jit(solution)/shard_map/reshape | solution.py:96
  131.6 12.8 %fusion.46 = (f32[2048,6,1,128]{3,2,1,0:T(1,128)S(1)}, f32[2048,6,1,128]{3,2,1,0:T(1,128)S(1)}) fusion(f32[2048,6,2,128]{3,2,1,0:T(2,128)} %reshape.133), kind=kLoop, calls=%fused_computation.97 | loop fusion | bytes 25165824 | tf_op jit(solution)/shard_map/slice | solution.py:45
  144.5 3.4 copy.118
  147.9 2.1 copy-done
  150.0 3.6 copy.120
  153.6 3.3 copy.117
  157.5 7.6 %multiply_subtract_fusion = (f32[2048,6,128]{2,0,1:T(8,128)}, f32[2048,6,128]{2,0,1:T(8,128)}) fusion(f32[2048,6,1,128]{3,2,1,0:T(1,128)S(1)} %get-tuple-element.16, f32[2048,6,1,128]{3,2,1,0:T(1,128)S(1)} %bitcast.82, f32[2048,6,1,128]{3,2,1,0:T(1,128)} %copy-done, f32[2048,6,1,128]{3,2,1,0:T(1,128)S(1)} %bitcast.84), kind=kLoop, calls=%fused_computation.6 | loop fusion | flops 9437184 | bytes 37748736 | tf_op jit(solution)/shard_map/sub | solution.py:50
  165.2 3.6 copy.119
  170.2 11.0 %add_bitcast_fusion = (f32[2048,3,1,128]{3,0,1,2:T(8,128)}, f32[2048,3,128]{2,0,1:T(8,128)}, f32[2048,3,128]{2,0,1:T(8,128)}) fusion(f32[2048,6,128]{2,0,1:T(8,128)} %bitcast.89, f32[2048,6,128]{2,0,1:T(8,128)S(1)} %bitcast.93, f32[2048]{0:T(1024)S(1)} %copy-done.7, f32[2048,6,128]{2,0,1:T(8,128)} %get-tuple-element.11, f32[2048,6,128]{2,0,1:T(8,128)} %get-tuple-element.10), kind=kLoop, calls=%fused_computation.18 | loop fusion | flops 5505024 | bytes 28319744 | tf_op jit(solution)/shard_map/stack | solution.py:58
  181.3 2.6 copy-done.3
  183.8 6.1 %subtract_bitcast_fusion.1 = (f32[2048,3,1,128]{3,0,1,2:T(8,128)}, f32[2048,3,1,128]{3,0,1,2:T(8,128)}, f32[2048,3,1,128]{3,0,1,2:T(8,128)}) fusion(f32[2048,3,128]{2,0,1:T(8,128)} %get-tuple-element.9, f32[2048,3,128]{2,0,1:T(8,128)} %get-tuple-element.8, f32[2048,6,128]{2,0,1:T(8,128)S(1)} %bitcast.100, f32[2048,6,128]{2,0,1:T(8,128)S(1)} %bitcast.101, ...), kind=kLoop, calls=%fused_computation.20 | loop fusion | flops 7077888 | bytes 28311552 | tf_op jit(solution)/shard_map/stack | solution.py:58
  189.9 3.2 pad_maximum_fusion.1
  193.1 25.9 %copy.79 = f32[2048,3,2,128]{3,2,1,0:T(2,128)} copy(f32[2048,3,2,128]{3,0,1,2:T(8,128)S(1)} %pad_maximum_fusion.1) | data formatting | bytes 12582912 | tf_op jit(solution)/shard_map/stack | solution.py:58
  219.1 9.1 %reshape.136 = f32[16,128,768]{2,1,0:T(8,128)} reshape(f32[2048,3,2,128]{3,2,1,0:T(2,128)} %copy.79) | data formatting | bytes 12582912 | tf_op jit(solution)/shard_map/reshape | solution.py:111
  228.2 2.3 pad_maximum_fusion
  230.5 25.5 %copy.78 = f32[2048,3,2,128]{3,2,1,0:T(2,128)} copy(f32[2048,3,2,128]{3,0,1,2:T(8,128)S(1)} %pad_maximum_fusion) | data formatting | bytes 12582912 | tf_op jit(solution)/shard_map/stack | solution.py:58
  256.0 9.3 %reshape.135 = f32[16,128,768]{2,1,0:T(8,128)} reshape(f32[2048,3,2,128]{3,2,1,0:T(2,128)} %copy.78) | data formatting | bytes 12582912 | tf_op jit(solution)/shard_map/reshape | solution.py:104
  265.3 5.7 %fusion.10 = f32[16,128,768]{2,1,0:T(8,128)S(1)} fusion(f32[16,128,768]{2,1,0:T(8,128)} %reshape.135, s32[16,128]{1,0:T(8,128)S(1)} %get-tuple-element.22), kind=kOutput, calls=%fused_computation.33 | convolution fusion | flops 2416181248 | bytes 12591104 | tf_op jit(solution)/shard_map/bpw,bpf->bwf/dot_general | solution.py:101
  271.1 4.3 convolution_add_fusion
  276.1 1.6 copy-done.1
  277.9 4.0 collective-permute-start.1
  281.9 4.0 fusion
  285.8 3.5 slice.81
  289.4 2.8 pad_add_fusion
  294.0 10.6 %all-to-all-start = ((s32[128,1,2]{2,1,0:T(1,128)}), s32[128,1,2]{2,1,0:T(1,128)S(1)}, u32[]{:S(2)}, u32[]{:S(2)}) async-start(s32[128,1,2]{2,1,0:T(1,128)} %bitcast.1), calls=%async_computation | async-start | bytes 131072 | tf_op jit(solution)/shard_map/all_to_all | solution.py:181
  306.0 2.1 negate_multiply_fusion
  308.2 54.1 %all-reduce.6.cloned.1.call-done = f32[1024,3,2,128]{3,2,1,0:T(2,128)} async-done(((f32[1024,3,2,128]{3,2,1,0:T(2,128)}), f32[1024,3,2,128]{3,2,1,0:T(2,128)}) %all-reduce.6.cloned.1.call-update) | async-done | bytes 3145744
  365.8 1.5 fusion.33
  367.3 4.1 copy.81
  371.4 10.3 %all-to-all-start.1 = ((f32[128,2,3,1024]{3,1,2,0:T(2,128)}), f32[128,2,3,1024]{3,1,2,0:T(2,128)S(1)}, u32[]{:S(2)}, u32[]{:S(2)}) async-start(f32[128,2,3,1024]{3,1,2,0:T(2,128)} %copy.81), calls=%async_computation.1 | async-start | bytes 6291456 | tf_op jit(solution)/shard_map/all_to_all | solution.py:180
  383.1 40.0 %all-to-all-done.1 = f32[128,2,3,1024]{3,1,2,0:T(2,128)S(1)} async-done(((f32[128,2,3,1024]{3,1,2,0:T(2,128)}), f32[128,2,3,1024]{3,1,2,0:T(2,128)S(1)}, u32[]{:S(2)}, u32[]{:S(2)}) %all-to-all-start.1) | async-done | bytes 3145760 | tf_op jit(solution)/shard_map/all_to_all | solution.py:180
  423.1 1.8 copy.82
  424.8 2.9 copy.92
  427.7 2.4 copy.83
  430.1 4.9 %fusion.31 = f32[128,3,1024]{2,0,1:T(8,128)} fusion(f32[3,1024,256]{2,1,0:T(8,128)} %bitcast.103, s32[256]{0:T(256)S(1)} %eq.105), kind=kOutput, calls=%fused_computation.71 | convolution fusion | flops 1207992320 | bytes 4719616 | tf_op jit(solution)/shard_map/dot_general | solution.py:187
  (97 shorter events, 18.0 us)
Async XLA Ops:
  6.5 40.5 %all-gather.2.cloned.1.call-start = ((), (), s32[]{:S(2)}) async-start(), calls=%async_computation.2 | async-start | bytes 3538944 | tf_op jit(solution)/shard_map/all_gather | solution.py:146
  8.8 3.3 copy-start.6
  12.7 2.8 copy-start.8
  12.8 2.8 copy-start.9
  12.8 3.4 copy-start.10
  12.8 3.4 copy-start.11
  15.5 346.7 %all-reduce.6.cloned.1.call-start = ((), (), s32[]{:S(2)}) async-start(), calls=%async_computation.3 | async-start | bytes 6291456
  48.1 10.2 %collective-permute-start = (bf16[64,6,2,128]{3,2,1,0:T(2,128)(2,1)S(1)}, bf16[64,6,2,128]{3,2,1,0:T(2,128)(2,1)S(1)}, u32[]{:S(2)}, u32[]{:S(2)}) collective-permute-start(bf16[64,6,2,128]{3,2,1,0:T(2,128)(2,1)S(1)} %slice.84), channel_id=1, source_target_pairs={{8,0},{16,8},{24,16},{32,24},{40,32},{48,40},{56,48},{64,56},{72,6... | collective-permute-start | bytes 589832 | tf_op jit(solution)/shard_map/ppermute | solution.py:16
  56.3 3.0 copy-start.4
  79.1 31.0 %slice-start = ((s8[6291456]{0:T(1024)(128)(4,1)}), s8[2097152]{0:T(1024)(128)(4,1)S(1)}, s32[]{:S(2)}) async-start(s8[6291456]{0:T(1024)(128)(4,1)} %bitcast.79), calls=%async_computation.4 | async-start | bytes 4194304
  94.3 15.7 %slice-start.1 = ((s8[6291456]{0:T(1024)(128)(4,1)}), s8[4194304]{0:T(1024)(128)(4,1)S(1)}, s32[]{:S(2)}) async-start(s8[6291456]{0:T(1024)(128)(4,1)} %bitcast.79), calls=%async_computation.5 | async-start | bytes 8388608
  144.4 5.5 %copy-start = (f32[2048,6,1,128]{3,2,1,0:T(1,128)}, f32[2048,6,1,128]{3,2,1,0:T(1,128)S(1)}, u32[]{:S(2)}) copy-start(f32[2048,6,1,128]{3,2,1,0:T(1,128)S(1)} %get-tuple-element.17) | copy-start | bytes 18874372
  144.4 9.1 %slice-start.4 = ((s8[6291456]{0:T(1024)(128)(4,1)}), s8[4194304]{0:T(1024)(128)(4,1)S(1)}, s32[]{:S(2)}) async-start(s8[6291456]{0:T(1024)(128)(4,1)} %bitcast.83), calls=%async_computation.8 | async-start | bytes 8388608
  149.9 3.6 slice-start.5
  150.0 6.9 %slice-start.2 = ((s8[6291456]{0:T(1024)(128)(4,1)}), s8[4194304]{0:T(1024)(128)(4,1)S(1)}, s32[]{:S(2)}) async-start(s8[6291456]{0:T(1024)(128)(4,1)} %bitcast.81), calls=%async_computation.6 | async-start | bytes 8388608
  153.6 4.0 slice-start.3
  157.5 11.2 %copy-start.7 = (f32[2048]{0:T(1024)S(1)}, f32[2048]{0:T(1024)}, u32[]{:S(2)}) copy-start(f32[2048]{0:T(1024)} %multiply_bitcast_fusion) | copy-start | bytes 24580
  165.2 5.1 %copy-start.2 = (f32[2048,6,1,128]{3,0,1,2:T(8,128)S(1)}, f32[2048,6,1,128]{3,0,1,2:T(8,128)}, u32[]{:S(2)}) copy-start(f32[2048,6,1,128]{3,0,1,2:T(8,128)} %copy.120) | copy-start | bytes 18874372
  165.2 16.1 %slice-start.6 = ((s8[6291456]{0:T(1024)(128)(4,1)}), s8[4194304]{0:T(1024)(128)(4,1)S(1)}, s32[]{:S(2)}) async-start(s8[6291456]{0:T(1024)(128)(4,1)} %bitcast.90), calls=%async_computation.10 | async-start | bytes 8388608
  165.2 16.1 %slice-start.10 = ((s8[6291456]{0:T(1024)(128)(4,1)}), s8[4194304]{0:T(1024)(128)(4,1)S(1)}, s32[]{:S(2)}) async-start(s8[6291456]{0:T(1024)(128)(4,1)} %bitcast.98), calls=%async_computation.14 | async-start | bytes 8388608
  170.2 11.0 %slice-start.7 = ((s8[6291456]{0:T(1024)(128)(4,1)}), s8[2097152]{0:T(1024)(128)(4,1)S(1)}, s32[]{:S(2)}) async-start(s8[6291456]{0:T(1024)(128)(4,1)} %bitcast.90), calls=%async_computation.11 | async-start | bytes 4194304
  170.2 11.0 %slice-start.11 = ((s8[6291456]{0:T(1024)(128)(4,1)}), s8[2097152]{0:T(1024)(128)(4,1)S(1)}, s32[]{:S(2)}) async-start(s8[6291456]{0:T(1024)(128)(4,1)} %bitcast.98), calls=%async_computation.15 | async-start | bytes 4194304
  170.2 13.6 %copy-start.3 = (f32[2048,6,1,128]{3,0,1,2:T(8,128)S(1)}, f32[2048,6,1,128]{3,0,1,2:T(8,128)}, u32[]{:S(2)}) copy-start(f32[2048,6,1,128]{3,0,1,2:T(8,128)} %copy.119) | copy-start | bytes 18874372
  219.1 9.1 %copy-start.5 = (f32[2048,3,1,128]{3,0,1,2:T(8,128)S(1)}, f32[2048,3,1,128]{3,0,1,2:T(8,128)}, u32[]{:S(2)}) copy-start(f32[2048,3,1,128]{3,0,1,2:T(8,128)} %get-tuple-element.12) | copy-start | bytes 9437188
  256.0 15.0 %slice-start.8 = ((s8[6291456]{0:T(1024)(128)(4,1)}), s8[2097152]{0:T(1024)(128)(4,1)S(1)}, s32[]{:S(2)}) async-start(s8[6291456]{0:T(1024)(128)(4,1)} %bitcast.95), calls=%async_computation.12 | async-start | bytes 4194304
  265.3 5.8 %slice-start.9 = ((s8[6291456]{0:T(1024)(128)(4,1)}), s8[4194304]{0:T(1024)(128)(4,1)S(1)}, s32[]{:S(2)}) async-start(s8[6291456]{0:T(1024)(128)(4,1)} %bitcast.95), calls=%async_computation.13 | async-start | bytes 8388608
  276.1 1.7 copy-start.1
  277.9 11.5 %collective-permute-start.1 = (f32[64,3,2,128]{3,2,1,0:T(2,128)S(1)}, f32[64,3,2,128]{3,2,1,0:T(2,128)S(1)}, u32[]{:S(2)}, u32[]{:S(2)}) collective-permute-start(f32[64,3,2,128]{3,2,1,0:T(2,128)S(1)} %slice.83), channel_id=1, source_target_pairs={{0,8},{8,16},{16,24},{24,32},{32,40},{40,48},{48,56},{56,64},{64,7... | collective-permute-start | bytes 589832 | tf_op jit(solution)/shard_map/ppermute | solution.py:16
  292.2 0.7 copy-start.13
  292.2 0.8 copy-start.12
  292.2 12.4 %copy-start.14 = (u32[128]{0:T(128)S(1)}, u32[128]{0:T(128)}, u32[]{:S(2)}) copy-start(u32[128]{0:T(128)} %constant.53) | copy-start | bytes 1540
  294.0 77.4 %all-to-all-start = ((s32[128,1,2]{2,1,0:T(1,128)}), s32[128,1,2]{2,1,0:T(1,128)S(1)}, u32[]{:S(2)}, u32[]{:S(2)}) async-start(s32[128,1,2]{2,1,0:T(1,128)} %bitcast.1), calls=%async_computation | async-start | bytes 131072 | tf_op jit(solution)/shard_map/all_to_all | solution.py:181
  371.4 51.7 %all-to-all-start.1 = ((f32[128,2,3,1024]{3,1,2,0:T(2,128)}), f32[128,2,3,1024]{3,1,2,0:T(2,128)S(1)}, u32[]{:S(2)}, u32[]{:S(2)}) async-start(f32[128,2,3,1024]{3,1,2,0:T(2,128)} %copy.81), calls=%async_computation.1 | async-start | bytes 6291456 | tf_op jit(solution)/shard_map/all_to_all | solution.py:180
Sparse Core Ops, SparseCore 0:
  15.6 31.3 all-gather.1
  292.3 69.8 all-reduce.5
where the time goes:
time: 448 us; the launch traced here: 442 us
  local copies, waits for them, and re-layouts  193 us (43%)
  waiting for transfers between devices  125 us (28%)
  other arithmetic  48.5 us (11%)
  matrix products  34.3 us (8%)
  starting transfers between devices  26.4 us (6%)
  between operations  14.9 us (3%)
    unnamed x3, waiting for transfers between devices  54.1 us
    all_to_all x1, waiting for transfers between devices, on_device(): lax.all_to_all(outgoing, ('blk', 'sub'), split_axis=0, concat_axis=0, til...  40 us
    unnamed x64, local copies, waits for them, and re-layouts  33.2 us
    all_gather x1, waiting for transfers between devices, on_device(): gathered = lax.all_gather(spectrum_table, 'sub', axis=0, tiled=True)  30.7 us
    another operation x1, local copies, waits for them, and re-layouts, pair_terms(): jnp.stack([second_re, second_im], axis=2)  25.9 us
    another operation x1, local copies, waits for them, and re-layouts, pair_terms(): jnp.stack([first_re, first_im], axis=2)  25.5 us
    slice x1, local copies, waits for them, and re-layouts, pair_terms(): right_im = second_rows[:, :, 1]  15.7 us
    reshape x1, local copies, waits for them, and re-layouts, pair_work(): second_rows.reshape((block_count * slot_count,) + tail_shape)  15.2 us
  transfers between devices with their start and end apart: 6, of which 3 were waited for; matrix products, arithmetic and copies ran while one was open for 7% of the time, Pallas kernels for 0%

commit v1 on v0

v1 whole, which is shorter than its diff:
```python
import functools
import math

import jax
import jax.numpy as jnp
import numpy as np
from jax import lax
from jax.experimental import pallas as pl
from jax.experimental.pallas import tpu as pltpu
from jax.sharding import PartitionSpec as P

MESH = pl.DeviceIdType.MESH
NF = 128
BLOCK = 64
F32 = jnp.float32
BF16 = jnp.bfloat16


def dft_tables(samples, freqs):
    phase = (np.arange(samples)[:, None] * np.arange(freqs)[None, :]) % samples
    angles = phase.astype(np.float64) * (2.0 * math.pi / samples)
    scale = 1.0 / math.sqrt(samples)
    cosine, sine = np.cos(angles) * scale, np.sin(angles) * scale
    forward = np.concatenate([cosine, -sine], axis=1).astype(np.float32)
    doubled = np.where(np.arange(freqs) == 0, 1.0, 2.0)[:, None]
    inverse = np.concatenate([cosine.T * doubled, -sine.T * doubled], axis=0)
    return forward.astype(jnp.bfloat16), inverse.astype(np.float32)


def in_two(x):
    high = x.astype(BF16)
    return high, (x - high.astype(F32)).astype(BF16)


def dot_rows(a, b):
    return lax.dot_general(a, b, (((1,), (1,)), ((), ())), preferred_element_type=F32)


def dot_plain(a, b):
    return jnp.dot(a, b, preferred_element_type=F32)


def features(pair):
    xr, xi = pair[0][:, :NF].astype(F32), pair[0][:, NF:].astype(F32)
    o_r, o_i = pair[1][:, :NF].astype(F32), pair[1][:, NF:].astype(F32)
    dr, di = xr - o_r, xi - o_i
    parts = [dr * xr + di * xi, dr * xi - di * xr, o_r * xr + o_i * xi, o_r * xi - o_i * xr]
    both = [in_two(p) for p in parts]
    return jnp.concatenate(
        [jnp.concatenate([b[i] for b in both], axis=1) for i in range(2)], axis=0
    )


def for_features(links):
    high, low = in_two(links)
    return jnp.concatenate(
        [jnp.concatenate([high, high], axis=1), jnp.concatenate([low, low], axis=1)], axis=0
    )


def linked(links, values):
    rows = links.shape[0] // 2
    both = dot_plain(links, values)
    return both[:rows] + both[rows:]


def spread(rows, count, shift):
    index = lax.broadcasted_iota(jnp.int32, (count, NF), 0) + shift
    return jnp.concatenate(
        [(index == rows[s : s + 1]).astype(F32).astype(BF16) for s in range(rows.shape[0])], axis=1
    )


def spread_weights(rows, weights, count, shift):
    index = lax.broadcasted_iota(jnp.int32, (count, NF), 0) + shift
    parts = []
    for part in in_two(weights):
        wide = part.astype(F32)
        parts.append(
            jnp.concatenate(
                [
                    jnp.where(index == rows[s : s + 1], wide[s : s + 1], 0.0).astype(BF16)
                    for s in range(rows.shape[0])
                ],
                axis=1,
            )
        )
    return jnp.concatenate(parts, axis=0)


def exchange_kernel(
    blks,
    subs,
    syn_hbm,
    obs_hbm,
    table_hbm,
    first_hbm,
    second_hbm,
    mask_hbm,
    weight_hbm,
    owner_hbm,
    element_hbm,
    summed,
    traces,
    table,
    first,
    second,
    mask,
    weight,
    owner,
    element,
    spec,
    halo,
    list_out,
    list_over,
    lists,
    lists_prev,
    near_out,
    near_labels,
    label_out,
    labels,
    group_out,
    group_in,
    far_out,
    far_in,
    load_sems,
    list_send,
    list_recv,
    over_send,
    over_recv,
    halo_send,
    halo_recv,
    near_send,
    near_recv,
    label_send,
    label_recv,
    group_send,
    group_recv,
    far_send,
    far_recv,
):
    devices = blks * subs
    blk, sub = lax.axis_index("blk"), lax.axis_index("sub")
    me = blk * subs + sub
    rows = spec.shape[1]
    blocks = first.shape[0]
    group_rows, far_rows = 2 * blks, 2 * subs

    def around(at, step, size):
        there = at + step
        return jnp.where(there >= size, there - size, there)

    subs_there = [around(sub, step, subs) for step in range(1, subs)]
    blks_there = [around(blk, step, blks) for step in range(1, blks)]
    blk_after, blk_before = blks_there[0], blks_there[-1]
    after = (jnp.where(sub == subs - 1, blk_after, blk), subs_there[0])
    before = (jnp.where(sub == 0, blk_before, blk), subs_there[-1])

    pairs = [
        (first_hbm, first),
        (second_hbm, second),
        (mask_hbm, mask),
        (weight_hbm, weight),
        (table_hbm, table),
        (syn_hbm.at[0], traces.at[0, pl.ds(0, rows)]),
        (obs_hbm.at[0], traces.at[0, pl.ds(rows, rows)]),
        (syn_hbm.at[1], traces.at[1, pl.ds(0, rows)]),
        (obs_hbm.at[1], traces.at[1, pl.ds(rows, rows)]),
        (syn_hbm.at[2], traces.at[2, pl.ds(0, rows)]),
        (obs_hbm.at[2], traces.at[2, pl.ds(rows, rows)]),
        (owner_hbm, owner),
        (element_hbm, element),
    ]
    loads = [
        pltpu.make_async_copy(src, dst, load_sems.at[i]) for i, (src, dst) in enumerate(pairs)
    ]
    for load in loads:
        load.start()

    barrier = pltpu.get_barrier_semaphore()

    def greet(there):
        pl.semaphore_signal(barrier, inc=1, device_id=there, device_id_type=MESH)

    for there in subs_there:
        greet((blk, there))
    for there in blks_there:
        greet((there, sub))

    @pl.when(sub == 0)
    def _():
        for s in range(1, subs):
            greet((blk_before, s))

    @pl.when(sub == subs - 1)
    def _():
        greet((blk_after, 0))

    for i in range(4):
        loads[i].wait()
    base = (blk * blocks + lax.broadcasted_iota(jnp.int32, (blocks, NF), 0)) * BLOCK
    code = ((first[...] - base) * (2 * BLOCK) + (second[...] - base)).astype(F32)
    slot_weight = weight[...] * mask[...].astype(F32)
    zero_row = jnp.zeros((1, NF), F32)
    for s in range(subs):
        lines = [max(2 * s - 1, 0), 2 * s, 2 * s + 1]
        list_out[s] = jnp.concatenate(
            [code[i : i + 1] for i in lines]
            + [slot_weight[i : i + 1] for i in lines]
            + [zero_row] * 2,
            axis=0,
        )
    list_over[...] = jnp.concatenate(
        [code[blocks - 1 : blocks]]
        + [zero_row] * 2
        + [slot_weight[blocks - 1 : blocks]]
        + [zero_row] * 4,
        axis=0,
    )
    lists[sub] = list_out[sub]

    def transform(c):
        both = dot_plain(traces[c], table[...]).astype(BF16)
        spec[2 * c] = both[:rows]
        spec[2 * c + 1] = both[rows:]

    for i in range(4, 7):
        loads[i].wait()
    transform(0)

    pl.semaphore_wait(barrier, subs + blks - 1)

    def halo_copies(c):
        q = pl.ds(2 * c, 2)
        return [
            pltpu.make_async_remote_copy(
                src_ref=spec.at[q, pl.ds(0, BLOCK)],
                dst_ref=halo.at[q, pl.ds(BLOCK, BLOCK)],
                send_sem=halo_send.at[0, c],
                recv_sem=halo_recv.at[0, c],
                device_id=before,
                device_id_type=MESH,
            ),
            pltpu.make_async_remote_copy(
                src_ref=spec.at[q, pl.ds(rows - BLOCK, BLOCK)],
                dst_ref=halo.at[q, pl.ds(0, BLOCK)],
                send_sem=halo_send.at[1, c],
                recv_sem=halo_recv.at[1, c],
                device_id=after,
                device_id_type=MESH,
            ),
        ]

    halos = [halo_copies(c) for c in range(3)]
    for there in subs_there:
        pltpu.make_async_remote_copy(
            src_ref=list_out.at[there],
            dst_ref=lists.at[sub],
            send_sem=list_send,
            recv_sem=list_recv,
            device_id=(blk, there),
            device_id_type=MESH,
        ).start()
    over = pltpu.make_async_remote_copy(
        src_ref=list_over,
        dst_ref=lists_prev.at[sub],
        send_sem=over_send,
        recv_sem=over_recv,
        device_id=(blk_after, 0),
        device_id_type=MESH,
    )
    over.start()
    for copy in halos[0]:
        copy.start()
    for c in (1, 2):
        loads[5 + 2 * c].wait()
        loads[6 + 2 * c].wait()
        transform(c)
        for copy in halos[c]:
            copy.start()

    loads[11].wait()
    loads[12].wait()
    lane = lax.broadcasted_iota(jnp.int32, (rows, rows), 1)
    line = lax.broadcasted_iota(jnp.int32, (rows, rows), 0)
    owner_row = owner[...]

    def column(row):
        return jnp.sum(jnp.where(lane == line, row, 0), axis=1, keepdims=True)

    owner_column, element_column = column(owner_row), column(element[...]).astype(F32)
    same = owner_column == owner_row
    rank_row = jnp.sum(jnp.where(same & (line < lane), 1, 0), axis=0, keepdims=True)
    rank_column = jnp.sum(jnp.where(same & (lane < line), 1, 0), axis=1, keepdims=True)
    label_rows = []
    for k in range(2):
        chosen = ((owner_column == lane) & (rank_column == k)).astype(F32)
        label_rows.append(
            jnp.sum(chosen * (element_column - rows), axis=0, keepdims=True) + float(rows)
        )
    near_out[...] = jnp.concatenate(label_rows + [zero_row] * 6, axis=0)
    near_labels[sub] = near_out[...]
    for there in subs_there:
        pltpu.make_async_remote_copy(
            src_ref=near_out,
            dst_ref=near_labels.at[sub],
            send_sem=near_send,
            recv_sem=near_recv,
            device_id=(blk, there),
            device_id_type=MESH,
        ).start()
    sub_bits, blk_bits = subs.bit_length() - 1, blks.bit_length() - 1
    target = (owner_row & (subs - 1)) * group_rows + rank_row * blks + (owner_row >> sub_bits)
    slot = lax.broadcasted_iota(jnp.int32, (2 * devices, rows), 0)
    placement = (slot == target).astype(F32).astype(BF16)

    def stations(c):
        return (spec[2 * c], spec[2 * c + 1])

    own = [features(stations(c)) for c in range(3)]

    others = pl.ds(0, subs - 1)
    pltpu.make_async_copy(lists.at[others], lists.at[others], list_recv).wait()

    @pl.when(sub == 0)
    def _():
        pltpu.make_async_copy(lists_prev, lists_prev, over_recv).wait()

    @pl.when(sub != 0)
    def _():
        lists_prev[...] = lists[...]

    def unpacked(ref, k):
        codes = ref[:, k, :].astype(jnp.int32)
        return codes >> 7, codes & 127, ref[:, 3 + k, :]

    first0, second0, weight0 = unpacked(lists_prev, 0)
    first1, second1, weight1 = unpacked(lists, 1)
    first2, second2, weight2 = unpacked(lists, 2)
    to_prev = dot_rows(spread_weights(second0, weight0, BLOCK, BLOCK), spread(first0, rows, 0))
    upper = dot_rows(spread(first1, BLOCK, 0), spread_weights(second1, weight1, rows, 0))
    lower = dot_rows(spread(first2, BLOCK, 0), spread_weights(second2, weight2, rows, 0))
    to_prev = to_prev[:BLOCK] + to_prev[BLOCK:]
    upper = upper[:, :rows] + upper[:, rows:]
    lower = lower[:, :rows] + lower[:, rows:]
    half = lax.broadcasted_iota(jnp.int32, (BLOCK, rows), 1) >= BLOCK
    inside = jnp.where(half, pltpu.roll(lower, BLOCK, 1), 0.0)
    one_way = jnp.concatenate([upper, inside], axis=0)
    link_own = for_features(one_way + one_way.T)
    link_halo = for_features(jnp.concatenate([to_prev, jnp.where(half, lower, 0.0)], axis=0))
    inner = [linked(link_own, own[c]) for c in range(3)]

    pltpu.make_async_copy(near_labels.at[others], near_labels.at[others], near_recv).wait()
    group_labels = jnp.concatenate([near_labels[:, 0, :], near_labels[:, 1, :]], axis=0)
    label_out[...] = group_labels
    labels[blk] = group_labels
    for there in blks_there:
        pltpu.make_async_remote_copy(
            src_ref=label_out,
            dst_ref=labels.at[blk],
            send_sem=label_send,
            recv_sem=label_recv,
            device_id=(there, sub),
            device_id_type=MESH,
        ).start()

    row_out = lax.broadcasted_iota(jnp.int32, (2 * devices, 2 * devices), 0)
    row_in = lax.broadcasted_iota(jnp.int32, (2 * devices, 2 * devices), 1)
    wanted = (
        ((row_out & (subs - 1)) << (blk_bits + 1))
        + (((row_out >> sub_bits) & 1) << blk_bits)
        + (row_out >> (sub_bits + 1))
    )
    turned = (row_in == wanted).astype(F32).astype(BF16)

    for c in range(3):
        for copy in halos[c]:
            copy.wait_recv()
        sums = inner[c] + linked(link_halo, features((halo[2 * c], halo[2 * c + 1])))
        g1r, g1i, g2r, g2i = (sums[:, i * NF : (i + 1) * NF] for i in range(4))
        x, o = stations(c)
        xr, xi = x[:, :NF].astype(F32), x[:, NF:].astype(F32)
        dr, di = xr - o[:, :NF].astype(F32), xi - o[:, NF:].astype(F32)
        real = (xr * g1r - xi * g1i) + (dr * g2r - di * g2i)
        imag = (xr * g1i + xi * g1r) + (dr * g2i + di * g2r)
        adjoint = jnp.concatenate([real, imag], axis=1).astype(BF16)
        group_out[c] = dot_plain(placement, adjoint).astype(BF16)
        mine = pl.ds(pl.multiple_of(sub * group_rows, group_rows), group_rows)
        group_in[c, mine] = group_out[c, mine]
        for there in subs_there:
            theirs = pl.ds(pl.multiple_of(there * group_rows, group_rows), group_rows)
            pltpu.make_async_remote_copy(
                src_ref=group_out.at[c, theirs],
                dst_ref=group_in.at[c, mine],
                send_sem=group_send.at[c],
                recv_sem=group_recv.at[c],
                device_id=(blk, there),
                device_id_type=MESH,
            ).start()

    some = pl.ds(0, blks - 1)
    pltpu.make_async_copy(labels.at[some], labels.at[some], label_recv).wait()
    table_of_labels = labels[...].reshape(2 * devices, NF)
    row_lane = lax.broadcasted_iota(jnp.int32, (2 * devices, NF), 1)
    label = jnp.sum(jnp.where(row_lane == me, table_of_labels, 0.0), axis=1, keepdims=True)
    collect = (label == row_lane.astype(F32)).astype(F32).T.astype(BF16)

    part = pl.ds(0, (subs - 1) * group_rows)
    here = pl.ds(pl.multiple_of(blk * far_rows, far_rows), far_rows)
    for c in range(3):
        pltpu.make_async_copy(group_in.at[c, part], group_in.at[c, part], group_recv.at[c]).wait()
        far_out[c] = dot_plain(turned, group_in[c]).astype(BF16)
        far_in[c, here] = far_out[c, here]
        for there in blks_there:
            theirs = pl.ds(pl.multiple_of(there * far_rows, far_rows), far_rows)
            pltpu.make_async_remote_copy(
                src_ref=far_out.at[c, theirs],
                dst_ref=far_in.at[c, here],
                send_sem=far_send.at[c],
                recv_sem=far_recv.at[c],
                device_id=(there, sub),
                device_id_type=MESH,
            ).start()

    far_part = pl.ds(0, (blks - 1) * far_rows)
    for c in range(3):
        pltpu.make_async_copy(far_in.at[c, far_part], far_in.at[c, far_part], far_recv.at[c]).wait()
        summed[c] = dot_plain(collect, far_in[c])

    for c in range(3):
        for copy in halos[c]:
            copy.wait_send()
        pltpu.make_async_copy(
            group_out.at[c, part], group_out.at[c, part], group_send.at[c]
        ).wait()
        pltpu.make_async_copy(
            far_out.at[c, far_part], far_out.at[c, far_part], far_send.at[c]
        ).wait()
    pltpu.make_async_copy(list_out.at[others], list_out.at[others], list_send).wait()
    pltpu.make_async_copy(near_labels.at[others], near_labels.at[others], near_send).wait()
    pltpu.make_async_copy(labels.at[some], labels.at[some], label_send).wait()
    over.wait_send()


def exchange(blks, subs, syn, obs, table, first, second, mask, weight, owner, element):
    devices = blks * subs
    samples, rows = syn.shape[2], syn.shape[1]
    in_hbm = pl.BlockSpec(memory_space=pltpu.HBM)
    dma = pltpu.SemaphoreType.DMA
    moved = pltpu.VMEM((3, 2 * devices, 2 * NF), BF16)
    return pl.pallas_call(
        functools.partial(exchange_kernel, blks, subs),
        out_shape=jax.ShapeDtypeStruct((3, rows, 2 * NF), F32),
        in_specs=[in_hbm] * 9,
        out_specs=pl.BlockSpec(memory_space=pltpu.VMEM),
        scratch_shapes=[
            pltpu.VMEM((3, 2 * rows, samples), BF16),
            pltpu.VMEM(table.shape, BF16),
            pltpu.VMEM(first.shape, jnp.int32),
            pltpu.VMEM(second.shape, jnp.int32),
            pltpu.VMEM(mask.shape, jnp.int32),
            pltpu.VMEM(weight.shape, F32),
            pltpu.VMEM(owner.shape, jnp.int32),
            pltpu.VMEM(element.shape, jnp.int32),
            pltpu.VMEM((6, rows, 2 * NF), BF16),
            pltpu.VMEM((6, 2 * BLOCK, 2 * NF), BF16),
            pltpu.VMEM((subs, 8, NF), F32),
            pltpu.VMEM((8, NF), F32),
            pltpu.VMEM((subs, 8, NF), F32),
            pltpu.VMEM((subs, 8, NF), F32),
            pltpu.VMEM((8, NF), F32),
            pltpu.VMEM((subs, 8, NF), F32),
            pltpu.VMEM((2 * subs, NF), F32),
            pltpu.VMEM((blks, 2 * subs, NF), F32),
            moved,
            moved,
            moved,
            moved,
            dma((13,)),
            dma,
            dma,
            dma,
            dma,
            dma((2, 3)),
            dma((2, 3)),
            dma,
            dma,
            dma,
            dma,
            dma((3,)),
            dma((3,)),
            dma((3,)),
            dma((3,)),
        ],
        compiler_params=pltpu.CompilerParams(
            collective_id=0, has_side_effects=True, vmem_limit_bytes=60 * 2**20
        ),
        cost_estimate=pl.CostEstimate(
            flops=2 * 10**9, bytes_accessed=3 * 10**6, transcendentals=0
        ),
        name="exchange",
    )(syn, obs, table, first, second, mask, weight, owner, element)


def finish_kernel(summed, table_high, table_low, out, result, sems):
    components, elements, width = summed.shape
    count = components * elements
    samples = result.shape[1]
    chunk = samples // sems.shape[0]
    high, low = in_two(summed[...].reshape(count, width))
    parts = jnp.concatenate([high, low], axis=0)
    copies = []
    for n in range(sems.shape[0]):
        columns = pl.ds(n * chunk, chunk)
        both = dot_plain(parts, table_high[:, columns])
        result[:, columns] = both[:count] + (
            both[count:] + dot_plain(high, table_low[:, columns])
        )
        copies.append(
            pltpu.make_async_copy(result.at[:, columns], out.at[:, columns], sems.at[n])
        )
        copies[-1].start()
    for copy in copies:
        copy.wait()


def finish(summed, table_high, table_low):
    components, elements, width = summed.shape
    samples = table_high.shape[1]
    in_vmem = pl.BlockSpec(memory_space=pltpu.VMEM)
    out = pl.pallas_call(
        finish_kernel,
        out_shape=jax.ShapeDtypeStruct((components * elements, samples), F32),
        in_specs=[in_vmem] * 3,
        out_specs=pl.BlockSpec(memory_space=pl.ANY),
        scratch_shapes=[
            pltpu.VMEM((components * elements, samples), F32),
            pltpu.SemaphoreType.DMA((4,)),
        ],
        compiler_params=pltpu.CompilerParams(vmem_limit_bytes=40 * 2**20),
        cost_estimate=pl.CostEstimate(
            flops=7 * 10**8, bytes_accessed=3 * 10**6, transcendentals=0
        ),
        name="finish",
    )(summed, table_high, table_low)
    return out.reshape(components, elements, samples)


def on_device(
    blks,
    subs,
    synthetic,
    observed,
    pair_first,
    pair_second,
    pair_mask,
    pair_weight,
    station_owner,
    station_element,
):
    rows, _, samples = synthetic.shape
    forward, inverse = dft_tables(samples, NF)
    inverse_high = inverse.astype(jnp.bfloat16)
    inverse_low = (inverse - inverse_high.astype(np.float32)).astype(jnp.bfloat16)
    summed = exchange(
        blks,
        subs,
        jnp.transpose(synthetic, (1, 0, 2)),
        jnp.transpose(observed, (1, 0, 2)),
        jnp.asarray(forward),
        pair_first,
        pair_second,
        pair_mask,
        pair_weight,
        station_owner.reshape(1, rows),
        station_element.reshape(1, rows),
    )
    out = finish(summed, jnp.asarray(inverse_high), jnp.asarray(inverse_low))
    return jnp.transpose(out, (1, 0, 2))


def solution(mesh):
    blks, subs = mesh.shape["blk"], mesh.shape["sub"]
    return jax.shard_map(
        functools.partial(on_device, blks, subs),
        mesh=mesh,
        in_specs=(
            P(("blk", "sub"), None, None),
            P(("blk", "sub"), None, None),
            P("blk", "sub"),
            P("blk", "sub"),
            P("blk", "sub"),
            P("blk", "sub"),
            P(("blk", "sub"), None),
            P(("blk", "sub")),
        ),
        out_specs=P(("blk", "sub"), None, None),
        check_vma=False,
    )
```

time: 448 us -> 30.9 us (0.07); the launches traced: 442 us -> 30.6 us
  local copies, waits for them, and re-layouts: 193 us -> 1 us
  waiting for transfers between devices: 125 us -> 0 us
  other arithmetic: 48.5 us -> 0 us
  matrix products: 34.3 us -> 0 us
  Pallas kernels: 0 us -> 29.5 us
  starting transfers between devices: 26.4 us -> 0 us
  between operations: 14.9 us -> 0.03 us
    reshape x10 -> x0, local copies, waits for them, and re-layouts: 59.7 us -> none  [the longest x1 15.2 us: pair_work(): second_rows.reshape((block_count * slot_count,) + tail_shape)]
    unnamed x3 -> x0, waiting for transfers between devices: 54.1 us -> none
    another operation x3 -> x0, local copies, waits for them, and re-layouts: 52 us -> none  [the longest x1 25.9 us: pair_terms(): jnp.stack([second_re, second_im], axis=2)]
    all_to_all x2 -> x0, waiting for transfers between devices: 40 us -> none  [the longest x1 40 us: on_device(): lax.all_to_all(outgoing, ('blk', 'sub'), split_axis=0, concat_axis=0, til...]
    dot_general x9 -> x0, matrix products: 34.3 us -> none  [the longest x1 9.15 us: pair_work(): jnp.einsum('bpw,bwf->bpf', second_match.astype(jnp.bfloat16), windows, pr...]
    slice x6 -> x0, local copies, waits for them, and re-layouts: 34 us -> none  [the longest x1 15.7 us: pair_terms(): right_im = second_rows[:, :, 1]]
    unnamed x64 -> x6, local copies, waits for them, and re-layouts: 33.2 us -> 1 us
    all_gather x1 -> x0, waiting for transfers between devices: 30.7 us -> none  [on_device(): gathered = lax.all_gather(spectrum_table, 'sub', axis=0, tiled=True)]
  transfers between devices with their start and end apart: 6 -> 0, of which waited for: 3 -> 0; matrix products, arithmetic and copies ran while one was open for 7% -> 0% of each run, Pallas kernels for 0% -> 0%
where the time goes in v1:
time: 30.9 us; the launch traced here: 30.6 us
  Pallas kernels  29.5 us (95%)
  local copies, waits for them, and re-layouts  1 us (3%)
    pallas_call x1, Pallas kernels, exchange(): pl.pallas_call(functools.partial(exchange_kernel, blks, subs), out_shape=...  27.8 us
    pallas_call x1, Pallas kernels, finish(): pl.pallas_call(finish_kernel, out_shape=jax.ShapeDtypeStruct((components...  1.71 us
    unnamed x6, local copies, waits for them, and re-layouts  1 us

profile of v1, /device:TPU:1, one launch (start us, length us, event | category | flops | bytes accessed | tf_op | source)
XLA Modules:
  0.0 30.6 jit_solution(6790960931311720520)
XLA Ops:
  0.0 0.0 copy-start
  0.0 0.0 copy-start.1
  0.0 27.8 %exchange.1.summed = f32[3,128,256]{2,1,0:T(8,128)} custom-call(bf16[3,128,1024]{2,1,0:T(8,128)(2,1)} %bitcast.7, bf16[3,128,1024]{2,1,0:T(8,128)(2,1)} %bitcast.8, bf16[1024,256]{1,0:T(8,128)(2,1)} %constant.6.clone.table_hbm, s32[16,128]{1,0:T(8,128)} %first_hbm.1, s32[16,128]{1,0:T(8,128)} %second_hbm.1, s32[16,128]{1,0:T(8,128)} %mask_hbm.1, ...), custom_call_target="tpu_custom_call" | custom-call | flops 2000000000 | bytes 3000000 | tf_op jit(solution)/shard_map/exchange/pallas_call | solution.py:451
  27.8 0.0 copy-done
  27.8 0.0 copy-done.1
  27.9 0.0 copy-start.2
  27.9 1.0 %copy-done.2 = f32[3,128,256]{2,1,0:T(8,128)S(1)} copy-done((f32[3,128,256]{2,1,0:T(8,128)S(1)}, f32[3,128,256]{2,1,0:T(8,128)}, u32[]{:S(2)}) %copy-start.2) | copy-done | bytes 393240
  28.9 1.7 %finish.1 = f32[384,1024]{1,0:T(8,128)} custom-call(f32[3,128,256]{2,1,0:T(8,128)S(1)} %copy-done.2, bf16[256,1024]{1,0:T(8,128)(2,1)S(1)} %copy-done.1, bf16[256,1024]{1,0:T(8,128)(2,1)S(1)} %copy-done), custom_call_target="tpu_custom_call" | custom-call | flops 700000000 | bytes 3000000 | tf_op jit(solution)/shard_map/finish/pallas_call | solution.py:531
Async XLA Ops:
  0.0 27.8 %copy-start = (bf16[256,1024]{1,0:T(8,128)(2,1)S(1)}, bf16[256,1024]{1,0:T(8,128)(2,1)}, u32[]{:S(2)}) copy-start(bf16[256,1024]{1,0:T(8,128)(2,1)} %constant.8.clone.table_low) | copy-start | bytes 1572868
  0.0 27.8 %copy-start.1 = (bf16[256,1024]{1,0:T(8,128)(2,1)S(1)}, bf16[256,1024]{1,0:T(8,128)(2,1)}, u32[]{:S(2)}) copy-start(bf16[256,1024]{1,0:T(8,128)(2,1)} %constant.7.clone.table_high) | copy-start | bytes 1572868
  27.9 1.0 %copy-start.2 = (f32[3,128,256]{2,1,0:T(8,128)S(1)}, f32[3,128,256]{2,1,0:T(8,128)}, u32[]{:S(2)}) copy-start(f32[3,128,256]{2,1,0:T(8,128)} %exchange.1.summed) | copy-start | bytes 1179652

commit v2 on v1

--- a/solution.py
+++ b/solution.py
@@ -12,6 +12,7 @@
 MESH = pl.DeviceIdType.MESH
 NF = 128
 BLOCK = 64
+TILE = 16
 F32 = jnp.float32
 BF16 = jnp.bfloat16
 
@@ -115,14 +116,10 @@
     list_over,
     lists,
     lists_prev,
-    near_out,
-    near_labels,
-    label_out,
-    labels,
-    group_out,
-    group_in,
-    far_out,
-    far_in,
+    wide,
+    outgoing,
+    received,
+    wide_in,
     load_sems,
     list_send,
     list_recv,
@@ -130,22 +127,15 @@
     over_recv,
     halo_send,
     halo_recv,
-    near_send,
-    near_recv,
-    label_send,
-    label_recv,
-    group_send,
-    group_recv,
-    far_send,
-    far_recv,
+    joined,
+    all_send,
+    all_recv,
 ):
     devices = blks * subs
     blk, sub = lax.axis_index("blk"), lax.axis_index("sub")
     me = blk * subs + sub
     rows = spec.shape[1]
     blocks = first.shape[0]
-    group_rows, far_rows = 2 * blks, 2 * subs
-
     def around(at, step, size):
         there = at + step
         return jnp.where(there >= size, there - size, there)
@@ -229,6 +219,8 @@
     transform(0)
 
     pl.semaphore_wait(barrier, subs + blks - 1)
+    for there in subs_there:
+        pl.semaphore_signal(joined, inc=1, device_id=(blk, there), device_id_type=MESH)
 
     def halo_copies(c):
         q = pl.ds(2 * c, 2)
@@ -284,35 +276,18 @@
     lane = lax.broadcasted_iota(jnp.int32, (rows, rows), 1)
     line = lax.broadcasted_iota(jnp.int32, (rows, rows), 0)
     owner_row = owner[...]
-
-    def column(row):
-        return jnp.sum(jnp.where(lane == line, row, 0), axis=1, keepdims=True)
-
-    owner_column, element_column = column(owner_row), column(element[...]).astype(F32)
-    same = owner_column == owner_row
-    rank_row = jnp.sum(jnp.where(same & (line < lane), 1, 0), axis=0, keepdims=True)
-    rank_column = jnp.sum(jnp.where(same & (lane < line), 1, 0), axis=1, keepdims=True)
-    label_rows = []
+    owner_column = jnp.sum(jnp.where(lane == line, owner_row, 0), axis=1, keepdims=True)
+    rank_row = jnp.sum(
+        jnp.where((owner_column == owner_row) & (line < lane), 1, 0), axis=0, keepdims=True
+    )
+    slot = lax.broadcasted_iota(jnp.int32, (2 * devices, rows), 0)
+    chosen = (slot == rank_row * devices + owner_row).astype(F32)
+    placement = chosen.astype(BF16)
+    label = jnp.sum(chosen * (element[...].astype(F32) - rows), axis=1, keepdims=True) + rows
     for k in range(2):
-        chosen = ((owner_column == lane) & (rank_column == k)).astype(F32)
-        label_rows.append(
-            jnp.sum(chosen * (element_column - rows), axis=0, keepdims=True) + float(rows)
-        )
-    near_out[...] = jnp.concatenate(label_rows + [zero_row] * 6, axis=0)
-    near_labels[sub] = near_out[...]
-    for there in subs_there:
-        pltpu.make_async_remote_copy(
-            src_ref=near_out,
-            dst_ref=near_labels.at[sub],
-            send_sem=near_send,
-            recv_sem=near_recv,
-            device_id=(blk, there),
-            device_id_type=MESH,
-        ).start()
-    sub_bits, blk_bits = subs.bit_length() - 1, blks.bit_length() - 1
-    target = (owner_row & (subs - 1)) * group_rows + rank_row * blks + (owner_row >> sub_bits)
-    slot = lax.broadcasted_iota(jnp.int32, (2 * devices, rows), 0)
-    placement = (slot == target).astype(F32).astype(BF16)
+        mine = label[k * devices : (k + 1) * devices]
+        wide[pl.ds(8 * k + 6, devices, stride=TILE), :] = jnp.broadcast_to(mine, (devices, NF))
+        wide[pl.ds(8 * k + 7, devices, stride=TILE), :] = jnp.zeros((devices, NF), F32)
 
     def stations(c):
         return (spec[2 * c], spec[2 * c + 1])
@@ -350,29 +325,6 @@
     link_halo = for_features(jnp.concatenate([to_prev, jnp.where(half, lower, 0.0)], axis=0))
     inner = [linked(link_own, own[c]) for c in range(3)]
 
-    pltpu.make_async_copy(near_labels.at[others], near_labels.at[others], near_recv).wait()
-    group_labels = jnp.concatenate([near_labels[:, 0, :], near_labels[:, 1, :]], axis=0)
-    label_out[...] = group_labels
-    labels[blk] = group_labels
-    for there in blks_there:
-        pltpu.make_async_remote_copy(
-            src_ref=label_out,
-            dst_ref=labels.at[blk],
-            send_sem=label_send,
-            recv_sem=label_recv,
-            device_id=(there, sub),
-            device_id_type=MESH,
-        ).start()
-
-    row_out = lax.broadcasted_iota(jnp.int32, (2 * devices, 2 * devices), 0)
-    row_in = lax.broadcasted_iota(jnp.int32, (2 * devices, 2 * devices), 1)
-    wanted = (
-        ((row_out & (subs - 1)) << (blk_bits + 1))
-        + (((row_out >> sub_bits) & 1) << blk_bits)
-        + (row_out >> (sub_bits + 1))
-    )
-    turned = (row_in == wanted).astype(F32).astype(BF16)
-
     for c in range(3):
         for copy in halos[c]:
             copy.wait_recv()
@@ -384,62 +336,66 @@
         real = (xr * g1r - xi * g1i) + (dr * g2r - di * g2i)
         imag = (xr * g1i + xi * g1r) + (dr * g2i + di * g2r)
         adjoint = jnp.concatenate([real, imag], axis=1).astype(BF16)
-        group_out[c] = dot_plain(placement, adjoint).astype(BF16)
-        mine = pl.ds(pl.multiple_of(sub * group_rows, group_rows), group_rows)
-        group_in[c, mine] = group_out[c, mine]
-        for there in subs_there:
-            theirs = pl.ds(pl.multiple_of(there * group_rows, group_rows), group_rows)
-            pltpu.make_async_remote_copy(
-                src_ref=group_out.at[c, theirs],
-                dst_ref=group_in.at[c, mine],
-                send_sem=group_send.at[c],
-                recv_sem=group_recv.at[c],
-                device_id=(blk, there),
-                device_id_type=MESH,
-            ).start()
-
-    some = pl.ds(0, blks - 1)
-    pltpu.make_async_copy(labels.at[some], labels.at[some], label_recv).wait()
-    table_of_labels = labels[...].reshape(2 * devices, NF)
-    row_lane = lax.broadcasted_iota(jnp.int32, (2 * devices, NF), 1)
-    label = jnp.sum(jnp.where(row_lane == me, table_of_labels, 0.0), axis=1, keepdims=True)
-    collect = (label == row_lane.astype(F32)).astype(F32).T.astype(BF16)
-
-    part = pl.ds(0, (subs - 1) * group_rows)
-    here = pl.ds(pl.multiple_of(blk * far_rows, far_rows), far_rows)
+        moved = dot_plain(placement, adjoint)
+        for k in range(2):
+            for i in range(2):
+                wide[pl.ds(8 * k + 2 * c + i, devices, stride=TILE), :] = moved[
+                    k * devices : (k + 1) * devices, i * NF : (i + 1) * NF
+                ]
+    outgoing[...] = wide[...].astype(BF16).reshape(outgoing.shape)
+    received[me] = outgoing[me]
+
+    pl.semaphore_wait(joined, subs - 1)
+
+    def deliver(blk_to, sub_to):
+        to = blk_to * subs + sub_to
+        pltpu.make_async_remote_copy(
+            src_ref=outgoing.at[to],
+            dst_ref=received.at[me],
+            send_sem=all_send,
+            recv_sem=all_recv,
+            device_id=(blk_to, sub_to),
+            device_id_type=MESH,
+        ).start()
+
+    def deliver_far(step, carry):
+        there = around(blk, step, blks)
+        for sub_to in [sub] + subs_there:
+            deliver(there, sub_to)
+        return carry
+
+    lax.fori_loop(1, blks, deliver_far, 0)
+    for there in subs_there:
+        deliver(blk, there)
+
+    most = pl.ds(0, devices - 1)
+    pltpu.make_async_copy(received.at[most], received.at[most], all_recv).wait()
+    wide_in[...] = received[...].astype(F32).reshape(wide_in.shape)
+
+    def picked(row):
+        return wide_in[pl.ds(row, devices, stride=TILE), :]
+
+    labels = jnp.concatenate([picked(6), picked(14)], axis=0)
+    element_lane = lax.broadcasted_iota(jnp.int32, (2 * devices, NF), 1).astype(F32)
+    collect = (labels == element_lane).astype(F32).astype(BF16)
     for c in range(3):
-        pltpu.make_async_copy(group_in.at[c, part], group_in.at[c, part], group_recv.at[c]).wait()
-        far_out[c] = dot_plain(turned, group_in[c]).astype(BF16)
-        far_in[c, here] = far_out[c, here]
-        for there in blks_there:
-            theirs = pl.ds(pl.multiple_of(there * far_rows, far_rows), far_rows)
-            pltpu.make_async_remote_copy(
-                src_ref=far_out.at[c, theirs],
-                dst_ref=far_in.at[c, here],
-                send_sem=far_send.at[c],
-                recv_sem=far_recv.at[c],
-                device_id=(there, sub),
-                device_id_type=MESH,
-            ).start()
-
-    far_part = pl.ds(0, (blks - 1) * far_rows)
-    for c in range(3):
-        pltpu.make_async_copy(far_in.at[c, far_part], far_in.at[c, far_part], far_recv.at[c]).wait()
-        summed[c] = dot_plain(collect, far_in[c])
+        values = jnp.concatenate(
+            [
+                jnp.concatenate([picked(8 * k + 2 * c), picked(8 * k + 2 * c + 1)], axis=1)
+                for k in range(2)
+            ],
+            axis=0,
+        ).astype(BF16)
+        summed[c] = lax.dot_general(
+            collect, values, (((0,), (0,)), ((), ())), preferred_element_type=F32
+        )
 
     for c in range(3):
         for copy in halos[c]:
             copy.wait_send()
-        pltpu.make_async_copy(
-            group_out.at[c, part], group_out.at[c, part], group_send.at[c]
-        ).wait()
-        pltpu.make_async_copy(
-            far_out.at[c, far_part], far_out.at[c, far_part], far_send.at[c]
-        ).wait()
     pltpu.make_async_copy(list_out.at[others], list_out.at[others], list_send).wait()
-    pltpu.make_async_copy(near_labels.at[others], near_labels.at[others], near_send).wait()
-    pltpu.make_async_copy(labels.at[some], labels.at[some], label_send).wait()
     over.wait_send()
+    pltpu.make_async_copy(outgoing.at[most], outgoing.at[most], all_send).wait()
 
 
 def exchange(blks, subs, syn, obs, table, first, second, mask, weight, owner, element):
@@ -447,7 +403,6 @@
     samples, rows = syn.shape[2], syn.shape[1]
     in_hbm = pl.BlockSpec(memory_space=pltpu.HBM)
     dma = pltpu.SemaphoreType.DMA
-    moved = pltpu.VMEM((3, 2 * devices, 2 * NF), BF16)
     return pl.pallas_call(
         functools.partial(exchange_kernel, blks, subs),
         out_shape=jax.ShapeDtypeStruct((3, rows, 2 * NF), F32),
@@ -468,14 +423,10 @@
             pltpu.VMEM((8, NF), F32),
             pltpu.VMEM((subs, 8, NF), F32),
             pltpu.VMEM((subs, 8, NF), F32),
-            pltpu.VMEM((8, NF), F32),
-            pltpu.VMEM((subs, 8, NF), F32),
-            pltpu.VMEM((2 * subs, NF), F32),
-            pltpu.VMEM((blks, 2 * subs, NF), F32),
-            moved,
-            moved,
-            moved,
-            moved,
+            pltpu.VMEM((devices * TILE, NF), F32),
+            pltpu.VMEM((devices, TILE, NF), BF16),
+            pltpu.VMEM((devices, TILE, NF), BF16),
+            pltpu.VMEM((devices * TILE, NF), F32),
             dma((13,)),
             dma,
             dma,
@@ -483,14 +434,9 @@
             dma,
             dma((2, 3)),
             dma((2, 3)),
+            pltpu.SemaphoreType.REGULAR,
             dma,
             dma,
-            dma,
-            dma,
-            dma((3,)),
-            dma((3,)),
-            dma((3,)),
-            dma((3,)),
         ],
         compiler_params=pltpu.CompilerParams(
             collective_id=0, has_side_effects=True, vmem_limit_bytes=60 * 2**20

time: 30.9 us -> 28.1 us (0.909)
  Pallas kernels: 29.5 us -> 26.9 us
    pallas_call x1, Pallas kernels: 27.8 us -> 25.2 us  [exchange(): pl.pallas_call(functools.partial(exchange_kernel, blks, subs), out_shape=...]
where the time goes in v2:
time: 28.1 us; the launch traced here: 27.9 us
  Pallas kernels  26.9 us (96%)
  local copies, waits for them, and re-layouts  1 us (4%)
    pallas_call x1, Pallas kernels, exchange(): pl.pallas_call(functools.partial(exchange_kernel, blks, subs), out_shape=...  25.2 us
    pallas_call x1, Pallas kernels, finish(): pl.pallas_call(finish_kernel, out_shape=jax.ShapeDtypeStruct((components...  1.73 us
    unnamed x6, local copies, waits for them, and re-layouts  1 us

profile of v2, /device:TPU:1, one launch (start us, length us, event | category | flops | bytes accessed | tf_op | source)
XLA Modules:
  0.0 27.9 jit_solution(1436535462088347186)
XLA Ops:
  0.0 0.0 copy-start
  0.0 0.0 copy-start.1
  0.0 25.2 %exchange.1.summed = f32[3,128,256]{2,1,0:T(8,128)} custom-call(bf16[3,128,1024]{2,1,0:T(8,128)(2,1)} %bitcast.7, bf16[3,128,1024]{2,1,0:T(8,128)(2,1)} %bitcast.8, bf16[1024,256]{1,0:T(8,128)(2,1)} %constant.6.clone.table_hbm, s32[16,128]{1,0:T(8,128)} %first_hbm.1, s32[16,128]{1,0:T(8,128)} %second_hbm.1, s32[16,128]{1,0:T(8,128)} %mask_hbm.1, ...), custom_call_target="tpu_custom_call" | custom-call | flops 2000000000 | bytes 3000000 | tf_op jit(solution)/shard_map/exchange/pallas_call | solution.py:406
  25.2 0.0 copy-done
  25.2 0.0 copy-done.1
  25.2 0.0 copy-start.2
  25.2 1.0 %copy-done.2 = f32[3,128,256]{2,1,0:T(8,128)S(1)} copy-done((f32[3,128,256]{2,1,0:T(8,128)S(1)}, f32[3,128,256]{2,1,0:T(8,128)}, u32[]{:S(2)}) %copy-start.2) | copy-done | bytes 393240
  26.2 1.7 %finish.1 = f32[384,1024]{1,0:T(8,128)} custom-call(f32[3,128,256]{2,1,0:T(8,128)S(1)} %copy-done.2, bf16[256,1024]{1,0:T(8,128)(2,1)S(1)} %copy-done.1, bf16[256,1024]{1,0:T(8,128)(2,1)S(1)} %copy-done), custom_call_target="tpu_custom_call" | custom-call | flops 700000000 | bytes 3000000 | tf_op jit(solution)/shard_map/finish/pallas_call | solution.py:477
Async XLA Ops:
  0.0 25.2 %copy-start = (bf16[256,1024]{1,0:T(8,128)(2,1)S(1)}, bf16[256,1024]{1,0:T(8,128)(2,1)}, u32[]{:S(2)}) copy-start(bf16[256,1024]{1,0:T(8,128)(2,1)} %constant.8.clone.table_low) | copy-start | bytes 1572868
  0.0 25.2 %copy-start.1 = (bf16[256,1024]{1,0:T(8,128)(2,1)S(1)}, bf16[256,1024]{1,0:T(8,128)(2,1)}, u32[]{:S(2)}) copy-start(bf16[256,1024]{1,0:T(8,128)(2,1)} %constant.7.clone.table_high) | copy-start | bytes 1572868
  25.2 1.0 %copy-start.2 = (f32[3,128,256]{2,1,0:T(8,128)S(1)}, f32[3,128,256]{2,1,0:T(8,128)}, u32[]{:S(2)}) copy-start(f32[3,128,256]{2,1,0:T(8,128)} %exchange.1.summed) | copy-start | bytes 1179652

commit v3 on v2

--- a/solution.py
+++ b/solution.py
@@ -1,4 +1,5 @@
 import functools
+import itertools
 import math
 
 import jax
@@ -25,7 +26,7 @@
     forward = np.concatenate([cosine, -sine], axis=1).astype(np.float32)
     doubled = np.where(np.arange(freqs) == 0, 1.0, 2.0)[:, None]
     inverse = np.concatenate([cosine.T * doubled, -sine.T * doubled], axis=0)
-    return forward.astype(jnp.bfloat16), inverse.astype(np.float32)
+    return forward.astype(jnp.bfloat16), inverse.astype(np.float32).astype(jnp.bfloat16)
 
 
 def in_two(x):
@@ -87,6 +88,22 @@
             )
         )
     return jnp.concatenate(parts, axis=0)
+
+
+def spread_order():
+    left = list(itertools.product(range(4), range(4), range(4), range(2)))[1:]
+    ways = {0: (0.0, 0.0), 1: (1.0, 0.0), 2: (1.0, 1.0), 3: (0.0, 1.0)}
+
+    def links(step):
+        return np.array([way for axis in step[:3] for way in ways[axis]])
+
+    used, order = np.zeros(6), []
+    while left:
+        step = min(left, key=lambda t: (np.max(used + links(t)), -np.sum(links(t)), t))
+        left.remove(step)
+        used = used + links(step)
+        order.append(step)
+    return order
 
 
 def exchange_kernel(
@@ -209,6 +226,26 @@
     )
     lists[sub] = list_out[sub]
 
+    pl.semaphore_wait(barrier, subs + blks - 1)
+    for there in subs_there:
+        pltpu.make_async_remote_copy(
+            src_ref=list_out.at[there],
+            dst_ref=lists.at[sub],
+            send_sem=list_send,
+            recv_sem=list_recv,
+            device_id=(blk, there),
+            device_id_type=MESH,
+        ).start()
+    over = pltpu.make_async_remote_copy(
+        src_ref=list_over,
+        dst_ref=lists_prev.at[sub],
+        send_sem=over_send,
+        recv_sem=over_recv,
+        device_id=(blk_after, 0),
+        device_id_type=MESH,
+    )
+    over.start()
+
     def transform(c):
         both = dot_plain(traces[c], table[...]).astype(BF16)
         spec[2 * c] = both[:rows]
@@ -217,10 +254,6 @@
     for i in range(4, 7):
         loads[i].wait()
     transform(0)
-
-    pl.semaphore_wait(barrier, subs + blks - 1)
-    for there in subs_there:
-        pl.semaphore_signal(joined, inc=1, device_id=(blk, there), device_id_type=MESH)
 
     def halo_copies(c):
         q = pl.ds(2 * c, 2)
@@ -244,24 +277,6 @@
         ]
 
     halos = [halo_copies(c) for c in range(3)]
-    for there in subs_there:
-        pltpu.make_async_remote_copy(
-            src_ref=list_out.at[there],
-            dst_ref=lists.at[sub],
-            send_sem=list_send,
-            recv_sem=list_recv,
-            device_id=(blk, there),
-            device_id_type=MESH,
-        ).start()
-    over = pltpu.make_async_remote_copy(
-        src_ref=list_over,
-        dst_ref=lists_prev.at[sub],
-        send_sem=over_send,
-        recv_sem=over_recv,
-        device_id=(blk_after, 0),
-        device_id_type=MESH,
-    )
-    over.start()
     for copy in halos[0]:
         copy.start()
     for c in (1, 2):
@@ -270,6 +285,9 @@
         transform(c)
         for copy in halos[c]:
             copy.start()
+
+    for there in subs_there:
+        pl.semaphore_signal(joined, inc=1, device_id=(blk, there), device_id_type=MESH)
 
     loads[11].wait()
     loads[12].wait()
@@ -347,26 +365,21 @@
 
     pl.semaphore_wait(joined, subs - 1)
 
-    def deliver(blk_to, sub_to):
-        to = blk_to * subs + sub_to
+    def turns(at, size):
+        return [at] + [around(at, step, size) for step in range(1, size)]
+
+    z_to, y_to = turns(lax.div(blk, 4), 4), turns(lax.rem(blk, 4), 4)
+    x_to, core_to = turns(lax.div(sub, 2), 4), turns(lax.rem(sub, 2), 2)
+    for dz, dy, dx, core in spread_order():
+        blk_to, sub_to = z_to[dz] * 4 + y_to[dy], x_to[dx] * 2 + core_to[core]
         pltpu.make_async_remote_copy(
-            src_ref=outgoing.at[to],
+            src_ref=outgoing.at[blk_to * subs + sub_to],
             dst_ref=received.at[me],
             send_sem=all_send,
             recv_sem=all_recv,
             device_id=(blk_to, sub_to),
             device_id_type=MESH,
         ).start()
-
-    def deliver_far(step, carry):
-        there = around(blk, step, blks)
-        for sub_to in [sub] + subs_there:
-            deliver(there, sub_to)
-        return carry
-
-    lax.fori_loop(1, blks, deliver_far, 0)
-    for there in subs_there:
-        deliver(blk, there)
 
     most = pl.ds(0, devices - 1)
     pltpu.make_async_copy(received.at[most], received.at[most], all_recv).wait()
@@ -405,7 +418,7 @@
     dma = pltpu.SemaphoreType.DMA
     return pl.pallas_call(
         functools.partial(exchange_kernel, blks, subs),
-        out_shape=jax.ShapeDtypeStruct((3, rows, 2 * NF), F32),
+        out_shape=pltpu.VMEM((3, rows, 2 * NF), F32),
         in_specs=[in_hbm] * 9,
         out_specs=pl.BlockSpec(memory_space=pltpu.VMEM),
         scratch_shapes=[
@@ -448,20 +461,16 @@
     )(syn, obs, table, first, second, mask, weight, owner, element)
 
 
-def finish_kernel(summed, table_high, table_low, out, result, sems):
+def finish_kernel(summed, table, out, result, sems):
     components, elements, width = summed.shape
     count = components * elements
     samples = result.shape[1]
     chunk = samples // sems.shape[0]
-    high, low = in_two(summed[...].reshape(count, width))
-    parts = jnp.concatenate([high, low], axis=0)
+    values = summed[...].reshape(count, width).astype(BF16)
     copies = []
     for n in range(sems.shape[0]):
         columns = pl.ds(n * chunk, chunk)
-        both = dot_plain(parts, table_high[:, columns])
-        result[:, columns] = both[:count] + (
-            both[count:] + dot_plain(high, table_low[:, columns])
-        )
+        result[:, columns] = dot_plain(values, table[:, columns])
         copies.append(
             pltpu.make_async_copy(result.at[:, columns], out.at[:, columns], sems.at[n])
         )
@@ -470,14 +479,14 @@
         copy.wait()
 
 
-def finish(summed, table_high, table_low):
+def finish(summed, table):
     components, elements, width = summed.shape
-    samples = table_high.shape[1]
+    samples = table.shape[1]
     in_vmem = pl.BlockSpec(memory_space=pltpu.VMEM)
     out = pl.pallas_call(
         finish_kernel,
         out_shape=jax.ShapeDtypeStruct((components * elements, samples), F32),
-        in_specs=[in_vmem] * 3,
+        in_specs=[in_vmem] * 2,
         out_specs=pl.BlockSpec(memory_space=pl.ANY),
         scratch_shapes=[
             pltpu.VMEM((components * elements, samples), F32),
@@ -488,7 +497,7 @@
             flops=7 * 10**8, bytes_accessed=3 * 10**6, transcendentals=0
         ),
         name="finish",
-    )(summed, table_high, table_low)
+    )(summed, table)
     return out.reshape(components, elements, samples)
 
 
@@ -506,8 +515,6 @@
 ):
     rows, _, samples = synthetic.shape
     forward, inverse = dft_tables(samples, NF)
-    inverse_high = inverse.astype(jnp.bfloat16)
-    inverse_low = (inverse - inverse_high.astype(np.float32)).astype(jnp.bfloat16)
     summed = exchange(
         blks,
         subs,
@@ -521,7 +528,7 @@
         station_owner.reshape(1, rows),
         station_element.reshape(1, rows),
     )
-    out = finish(summed, jnp.asarray(inverse_high), jnp.asarray(inverse_low))
+    out = finish(summed, jnp.asarray(inverse))
     return jnp.transpose(out, (1, 0, 2))
 
 

time: 28.1 us -> 26.2 us (0.932)
  local copies, waits for them, and re-layouts: 1 us -> 0.01 us
  Pallas kernels: 26.9 us -> 26.1 us
    unnamed x6 -> x2, local copies, waits for them, and re-layouts: 1 us -> 0.01 us
    pallas_call x1, Pallas kernels: 25.2 us -> 24.7 us  [exchange(): pl.pallas_call(functools.partial(exchange_kernel, blks, subs), out_shape=...]
    pallas_call x1, Pallas kernels: 1.73 us -> 1.44 us  [finish(): pl.pallas_call(finish_kernel, out_shape=jax.ShapeDtypeStruct((components...]
where the time goes in v3:
time: 26.2 us; the launch traced here: 26.1 us
  Pallas kernels  26.1 us (100%)
    pallas_call x1, Pallas kernels, exchange(): pl.pallas_call(functools.partial(exchange_kernel, blks, subs), out_shape=...  24.7 us
    pallas_call x1, Pallas kernels, finish(): pl.pallas_call(finish_kernel, out_shape=jax.ShapeDtypeStruct((components...  1.44 us

profile of v3, /device:TPU:1, one launch (start us, length us, event | category | flops | bytes accessed | tf_op | source)
XLA Modules:
  0.0 26.1 jit_solution(13941211435817847339)
XLA Ops:
  0.0 0.0 copy-start
  0.0 24.7 %exchange.1.summed = f32[3,128,256]{2,1,0:T(8,128)S(1)} custom-call(bf16[3,128,1024]{2,1,0:T(8,128)(2,1)} %bitcast.7, bf16[3,128,1024]{2,1,0:T(8,128)(2,1)} %bitcast.8, bf16[1024,256]{1,0:T(8,128)(2,1)} %constant.4.clone.table_hbm, s32[16,128]{1,0:T(8,128)} %first_hbm.1, s32[16,128]{1,0:T(8,128)} %second_hbm.1, s32[16,128]{1,0:T(8,128)} %mask_hbm.1, ...), custom_call_target="tpu_custom_call" | custom-call | flops 2000000000 | bytes 3000000 | tf_op jit(solution)/shard_map/exchange/pallas_call | solution.py:419
  24.7 0.0 copy-done
  24.7 1.4 %finish.1 = f32[384,1024]{1,0:T(8,128)} custom-call(f32[3,128,256]{2,1,0:T(8,128)S(1)} %exchange.1.summed, bf16[256,1024]{1,0:T(8,128)(2,1)S(1)} %copy-done), custom_call_target="tpu_custom_call" | custom-call | flops 700000000 | bytes 3000000 | tf_op jit(solution)/shard_map/finish/pallas_call | solution.py:486
Async XLA Ops:
  0.0 24.7 %copy-start = (bf16[256,1024]{1,0:T(8,128)(2,1)S(1)}, bf16[256,1024]{1,0:T(8,128)(2,1)}, u32[]{:S(2)}) copy-start(bf16[256,1024]{1,0:T(8,128)(2,1)} %constant.5.clone.table) | copy-start | bytes 1572868

commit v4 on v3

--- a/solution.py
+++ b/solution.py
@@ -13,7 +13,6 @@
 MESH = pl.DeviceIdType.MESH
 NF = 128
 BLOCK = 64
-TILE = 16
 F32 = jnp.float32
 BF16 = jnp.bfloat16
 
@@ -133,10 +132,12 @@
     list_over,
     lists,
     lists_prev,
-    wide,
+    near_out,
+    near_labels,
+    far_out,
+    labels,
     outgoing,
     received,
-    wide_in,
     load_sems,
     list_send,
     list_recv,
@@ -145,6 +146,10 @@
     halo_send,
     halo_recv,
     joined,
+    near_send,
+    near_recv,
+    far_send,
+    far_recv,
     all_send,
     all_recv,
 ):
@@ -294,18 +299,35 @@
     lane = lax.broadcasted_iota(jnp.int32, (rows, rows), 1)
     line = lax.broadcasted_iota(jnp.int32, (rows, rows), 0)
     owner_row = owner[...]
-    owner_column = jnp.sum(jnp.where(lane == line, owner_row, 0), axis=1, keepdims=True)
-    rank_row = jnp.sum(
-        jnp.where((owner_column == owner_row) & (line < lane), 1, 0), axis=0, keepdims=True
-    )
-    slot = lax.broadcasted_iota(jnp.int32, (2 * devices, rows), 0)
-    chosen = (slot == rank_row * devices + owner_row).astype(F32)
-    placement = chosen.astype(BF16)
-    label = jnp.sum(chosen * (element[...].astype(F32) - rows), axis=1, keepdims=True) + rows
+
+    def column(row):
+        return jnp.sum(jnp.where(lane == line, row, 0), axis=1, keepdims=True)
+
+    owner_column, element_column = column(owner_row), column(element[...]).astype(F32)
+    same = owner_column == owner_row
+    rank_column = jnp.sum(jnp.where(same & (lane < line), 1, 0), axis=1, keepdims=True)
+    label_rows = []
     for k in range(2):
-        mine = label[k * devices : (k + 1) * devices]
-        wide[pl.ds(8 * k + 6, devices, stride=TILE), :] = jnp.broadcast_to(mine, (devices, NF))
-        wide[pl.ds(8 * k + 7, devices, stride=TILE), :] = jnp.zeros((devices, NF), F32)
+        chosen = ((owner_column == lane) & (rank_column == k)).astype(F32)
+        label_rows.append(
+            jnp.sum(chosen * (element_column - rows), axis=0, keepdims=True) + float(rows)
+        )
+    near_out[...] = jnp.concatenate(label_rows + [zero_row] * 6, axis=0)
+    near_labels[sub] = near_out[...]
+    for there in subs_there:
+        pltpu.make_async_remote_copy(
+            src_ref=near_out,
+            dst_ref=near_labels.at[sub],
+            send_sem=near_send,
+            recv_sem=near_recv,
+            device_id=(blk, there),
+            device_id_type=MESH,
+        ).start()
+
+    rank_row = jnp.sum(jnp.where(same & (line < lane), 1, 0), axis=0, keepdims=True)
+    target = owner_row * 4 + rank_row * 2
+    slot = lax.broadcasted_iota(jnp.int32, (4 * devices, 2 * rows), 0)
+    placement = (slot == jnp.concatenate([target, target + 1], axis=1)).astype(F32).astype(BF16)
 
     def stations(c):
         return (spec[2 * c], spec[2 * c + 1])
@@ -343,6 +365,21 @@
     link_halo = for_features(jnp.concatenate([to_prev, jnp.where(half, lower, 0.0)], axis=0))
     inner = [linked(link_own, own[c]) for c in range(3)]
 
+    pltpu.make_async_copy(near_labels.at[others], near_labels.at[others], near_recv).wait()
+    far_out[...] = jnp.concatenate(
+        [near_labels[:, 0, :], near_labels[:, 1, :]], axis=0
+    ).astype(BF16)
+    labels[blk] = far_out[...]
+    for there in blks_there:
+        pltpu.make_async_remote_copy(
+            src_ref=far_out,
+            dst_ref=labels.at[blk],
+            send_sem=far_send,
+            recv_sem=far_recv,
+            device_id=(there, sub),
+            device_id_type=MESH,
+        ).start()
+
     for c in range(3):
         for copy in halos[c]:
             copy.wait_recv()
@@ -353,14 +390,8 @@
         dr, di = xr - o[:, :NF].astype(F32), xi - o[:, NF:].astype(F32)
         real = (xr * g1r - xi * g1i) + (dr * g2r - di * g2i)
         imag = (xr * g1i + xi * g1r) + (dr * g2i + di * g2r)
-        adjoint = jnp.concatenate([real, imag], axis=1).astype(BF16)
-        moved = dot_plain(placement, adjoint)
-        for k in range(2):
-            for i in range(2):
-                wide[pl.ds(8 * k + 2 * c + i, devices, stride=TILE), :] = moved[
-                    k * devices : (k + 1) * devices, i * NF : (i + 1) * NF
-                ]
-    outgoing[...] = wide[...].astype(BF16).reshape(outgoing.shape)
+        adjoint = jnp.concatenate([real, imag], axis=0).astype(BF16)
+        outgoing[:, c] = dot_plain(placement, adjoint).astype(BF16).reshape(devices, 4, NF)
     received[me] = outgoing[me]
 
     pl.semaphore_wait(joined, subs - 1)
@@ -381,33 +412,46 @@
             device_id_type=MESH,
         ).start()
 
+    some = pl.ds(0, blks - 1)
+    pltpu.make_async_copy(labels.at[some], labels.at[some], far_recv).wait()
+    by_owner = labels[...].reshape(2 * devices, NF)
+    arrived = lax.broadcasted_iota(jnp.int32, (2 * devices, 4 * devices), 1)
+    held = lax.broadcasted_iota(jnp.int32, (2 * devices, 4 * devices), 0)
+    sub_bits = subs.bit_length() - 1
+    wanted = (
+        ((arrived >> (sub_bits + 2)) << (sub_bits + 1))
+        + (((arrived >> 1) & 1) << sub_bits)
+        + ((arrived >> 2) & (subs - 1))
+    )
+    repeated = lax.dot_general(
+        by_owner,
+        (held == wanted).astype(F32).astype(BF16),
+        (((0,), (0,)), ((), ())),
+        preferred_element_type=F32,
+    )
+    owner_line = lax.broadcasted_iota(jnp.int32, repeated.shape, 0)
+    label = jnp.sum(jnp.where(owner_line == me, repeated, 0.0), axis=0, keepdims=True)
+    collect = jnp.concatenate(
+        [
+            ((label == owner_line.astype(F32)) & ((arrived[:rows] & 1) == i)).astype(F32)
+            for i in range(2)
+        ],
+        axis=0,
+    ).astype(BF16)
     most = pl.ds(0, devices - 1)
     pltpu.make_async_copy(received.at[most], received.at[most], all_recv).wait()
-    wide_in[...] = received[...].astype(F32).reshape(wide_in.shape)
-
-    def picked(row):
-        return wide_in[pl.ds(row, devices, stride=TILE), :]
-
-    labels = jnp.concatenate([picked(6), picked(14)], axis=0)
-    element_lane = lax.broadcasted_iota(jnp.int32, (2 * devices, NF), 1).astype(F32)
-    collect = (labels == element_lane).astype(F32).astype(BF16)
     for c in range(3):
-        values = jnp.concatenate(
-            [
-                jnp.concatenate([picked(8 * k + 2 * c), picked(8 * k + 2 * c + 1)], axis=1)
-                for k in range(2)
-            ],
-            axis=0,
-        ).astype(BF16)
-        summed[c] = lax.dot_general(
-            collect, values, (((0,), (0,)), ((), ())), preferred_element_type=F32
-        )
+        sums = dot_plain(collect, received[:, c].reshape(4 * devices, NF)).astype(BF16)
+        summed[c * rows : (c + 1) * rows, :NF] = sums[:rows]
+        summed[c * rows : (c + 1) * rows, NF:] = sums[rows:]
 
     for c in range(3):
         for copy in halos[c]:
             copy.wait_send()
     pltpu.make_async_copy(list_out.at[others], list_out.at[others], list_send).wait()
     over.wait_send()
+    pltpu.make_async_copy(near_labels.at[others], near_labels.at[others], near_send).wait()
+    pltpu.make_async_copy(labels.at[some], labels.at[some], far_send).wait()
     pltpu.make_async_copy(outgoing.at[most], outgoing.at[most], all_send).wait()
 
 
@@ -418,7 +462,7 @@
     dma = pltpu.SemaphoreType.DMA
     return pl.pallas_call(
         functools.partial(exchange_kernel, blks, subs),
-        out_shape=pltpu.VMEM((3, rows, 2 * NF), F32),
+        out_shape=pltpu.VMEM((3 * rows, 2 * NF), BF16),
         in_specs=[in_hbm] * 9,
         out_specs=pl.BlockSpec(memory_space=pltpu.VMEM),
         scratch_shapes=[
@@ -436,10 +480,12 @@
             pltpu.VMEM((8, NF), F32),
             pltpu.VMEM((subs, 8, NF), F32),
             pltpu.VMEM((subs, 8, NF), F32),
-            pltpu.VMEM((devices * TILE, NF), F32),
-            pltpu.VMEM((devices, TILE, NF), BF16),
-            pltpu.VMEM((devices, TILE, NF), BF16),
-            pltpu.VMEM((devices * TILE, NF), F32),
+            pltpu.VMEM((8, NF), F32),
+            pltpu.VMEM((subs, 8, NF), F32),
+            pltpu.VMEM((2 * subs, NF), BF16),
+            pltpu.VMEM((blks, 2 * subs, NF), BF16),
+            pltpu.VMEM((devices, 3, 4, NF), BF16),
+            pltpu.VMEM((devices, 3, 4, NF), BF16),
             dma((13,)),
             dma,
             dma,
@@ -448,6 +494,10 @@
             dma((2, 3)),
             dma((2, 3)),
             pltpu.SemaphoreType.REGULAR,
+            dma,
+            dma,
+            dma,
+            dma,
             dma,
             dma,
         ],
@@ -462,15 +512,12 @@
 
 
 def finish_kernel(summed, table, out, result, sems):
-    components, elements, width = summed.shape
-    count = components * elements
     samples = result.shape[1]
     chunk = samples // sems.shape[0]
-    values = summed[...].reshape(count, width).astype(BF16)
     copies = []
     for n in range(sems.shape[0]):
         columns = pl.ds(n * chunk, chunk)
-        result[:, columns] = dot_plain(values, table[:, columns])
+        result[:, columns] = dot_plain(summed[...], table[:, columns])
         copies.append(
             pltpu.make_async_copy(result.at[:, columns], out.at[:, columns], sems.at[n])
         )
@@ -480,16 +527,15 @@
 
 
 def finish(summed, table):
-    components, elements, width = summed.shape
-    samples = table.shape[1]
+    count, samples = summed.shape[0], table.shape[1]
     in_vmem = pl.BlockSpec(memory_space=pltpu.VMEM)
     out = pl.pallas_call(
         finish_kernel,
-        out_shape=jax.ShapeDtypeStruct((components * elements, samples), F32),
+        out_shape=jax.ShapeDtypeStruct((count, samples), F32),
         in_specs=[in_vmem] * 2,
         out_specs=pl.BlockSpec(memory_space=pl.ANY),
         scratch_shapes=[
-            pltpu.VMEM((components * elements, samples), F32),
+            pltpu.VMEM((count, samples), F32),
             pltpu.SemaphoreType.DMA((4,)),
         ],
         compiler_params=pltpu.CompilerParams(vmem_limit_bytes=40 * 2**20),
@@ -498,7 +544,7 @@
         ),
         name="finish",
     )(summed, table)
-    return out.reshape(components, elements, samples)
+    return out.reshape(3, count // 3, samples)
 
 
 def on_device(

time: 26.2 us -> 26.4 us (level)
  no operation moved by 1% of the time
where the time goes in v4:
time: 26.4 us; the launch traced here: 26.3 us
  Pallas kernels  26.3 us (100%)
    pallas_call x1, Pallas kernels, exchange(): pl.pallas_call(functools.partial(exchange_kernel, blks, subs), out_shape=...  24.8 us
    pallas_call x1, Pallas kernels, finish(): pl.pallas_call(finish_kernel, out_shape=jax.ShapeDtypeStruct((count, samp...  1.44 us

profile of v4, /device:TPU:1, one launch (start us, length us, event | category | flops | bytes accessed | tf_op | source)
XLA Modules:
  0.0 26.3 jit_solution(160947097139187074)
XLA Ops:
  0.0 0.0 copy-start
  0.0 24.8 %exchange.1.summed = bf16[384,256]{1,0:T(8,128)(2,1)S(1)} custom-call(bf16[3,128,1024]{2,1,0:T(8,128)(2,1)} %bitcast.7, bf16[3,128,1024]{2,1,0:T(8,128)(2,1)} %bitcast.8, bf16[1024,256]{1,0:T(8,128)(2,1)} %constant.4.clone.table_hbm, s32[16,128]{1,0:T(8,128)} %first_hbm.1, s32[16,128]{1,0:T(8,128)} %second_hbm.1, s32[16,128]{1,0:T(8,128)} %mask_hbm.1, ...), custom_call_target="tpu_custom_call" | custom-call | flops 2000000000 | bytes 3000000 | tf_op jit(solution)/shard_map/exchange/pallas_call | solution.py:463
  24.9 0.0 copy-done
  24.9 1.4 %finish.1 = f32[384,1024]{1,0:T(8,128)} custom-call(bf16[384,256]{1,0:T(8,128)(2,1)S(1)} %exchange.1.summed, bf16[256,1024]{1,0:T(8,128)(2,1)S(1)} %copy-done), custom_call_target="tpu_custom_call" | custom-call | flops 700000000 | bytes 3000000 | tf_op jit(solution)/shard_map/finish/pallas_call | solution.py:532
Async XLA Ops:
  0.0 24.9 %copy-start = (bf16[256,1024]{1,0:T(8,128)(2,1)S(1)}, bf16[256,1024]{1,0:T(8,128)(2,1)}, u32[]{:S(2)}) copy-start(bf16[256,1024]{1,0:T(8,128)(2,1)} %constant.5.clone.table) | copy-start | bytes 1572868

commit v5 on v4

--- a/solution.py
+++ b/solution.py
@@ -132,9 +132,6 @@
     list_over,
     lists,
     lists_prev,
-    near_out,
-    near_labels,
-    far_out,
     labels,
     outgoing,
     received,
@@ -146,10 +143,10 @@
     halo_send,
     halo_recv,
     joined,
-    near_send,
-    near_recv,
-    far_send,
-    far_recv,
+    y_send,
+    y_recv,
+    z_send,
+    z_recv,
     all_send,
     all_recv,
 ):
@@ -169,6 +166,8 @@
     before = (jnp.where(sub == 0, blk_before, blk), subs_there[-1])
 
     pairs = [
+        (owner_hbm, owner),
+        (element_hbm, element),
         (first_hbm, first),
         (second_hbm, second),
         (mask_hbm, mask),
@@ -180,8 +179,6 @@
         (obs_hbm.at[1], traces.at[1, pl.ds(rows, rows)]),
         (syn_hbm.at[2], traces.at[2, pl.ds(0, rows)]),
         (obs_hbm.at[2], traces.at[2, pl.ds(rows, rows)]),
-        (owner_hbm, owner),
-        (element_hbm, element),
     ]
     loads = [
         pltpu.make_async_copy(src, dst, load_sems.at[i]) for i, (src, dst) in enumerate(pairs)
@@ -208,7 +205,26 @@
     def _():
         greet((blk_after, 0))
 
-    for i in range(4):
+    for i in range(2):
+        loads[i].wait()
+    lane = lax.broadcasted_iota(jnp.int32, (rows, rows), 1)
+    line = lax.broadcasted_iota(jnp.int32, (rows, rows), 0)
+    owner_row = owner[...]
+
+    def column(row):
+        return jnp.sum(jnp.where(lane == line, row, 0), axis=1, keepdims=True)
+
+    owner_column, element_column = column(owner_row), column(element[...]).astype(F32)
+    same = owner_column == owner_row
+    rank_column = jnp.sum(jnp.where(same & (lane < line), 1, 0), axis=1, keepdims=True)
+    label_rows = []
+    for k in range(2):
+        chosen = ((owner_column == lane) & (rank_column == k)).astype(F32)
+        label_rows.append(
+            jnp.sum(chosen * (element_column - rows), axis=0, keepdims=True) + float(rows)
+        )
+
+    for i in range(2, 6):
         loads[i].wait()
     base = (blk * blocks + lax.broadcasted_iota(jnp.int32, (blocks, NF), 0)) * BLOCK
     code = ((first[...] - base) * (2 * BLOCK) + (second[...] - base)).astype(F32)
@@ -219,7 +235,7 @@
         list_out[s] = jnp.concatenate(
             [code[i : i + 1] for i in lines]
             + [slot_weight[i : i + 1] for i in lines]
-            + [zero_row] * 2,
+            + label_rows,
             axis=0,
         )
     list_over[...] = jnp.concatenate(
@@ -256,7 +272,7 @@
         spec[2 * c] = both[:rows]
         spec[2 * c + 1] = both[rows:]
 
-    for i in range(4, 7):
+    for i in range(6, 9):
         loads[i].wait()
     transform(0)
 
@@ -285,44 +301,14 @@
     for copy in halos[0]:
         copy.start()
     for c in (1, 2):
-        loads[5 + 2 * c].wait()
-        loads[6 + 2 * c].wait()
+        loads[7 + 2 * c].wait()
+        loads[8 + 2 * c].wait()
         transform(c)
         for copy in halos[c]:
             copy.start()
 
     for there in subs_there:
         pl.semaphore_signal(joined, inc=1, device_id=(blk, there), device_id_type=MESH)
-
-    loads[11].wait()
-    loads[12].wait()
-    lane = lax.broadcasted_iota(jnp.int32, (rows, rows), 1)
-    line = lax.broadcasted_iota(jnp.int32, (rows, rows), 0)
-    owner_row = owner[...]
-
-    def column(row):
-        return jnp.sum(jnp.where(lane == line, row, 0), axis=1, keepdims=True)
-
-    owner_column, element_column = column(owner_row), column(element[...]).astype(F32)
-    same = owner_column == owner_row
-    rank_column = jnp.sum(jnp.where(same & (lane < line), 1, 0), axis=1, keepdims=True)
-    label_rows = []
-    for k in range(2):
-        chosen = ((owner_column == lane) & (rank_column == k)).astype(F32)
-        label_rows.append(
-            jnp.sum(chosen * (element_column - rows), axis=0, keepdims=True) + float(rows)
-        )
-    near_out[...] = jnp.concatenate(label_rows + [zero_row] * 6, axis=0)
-    near_labels[sub] = near_out[...]
-    for there in subs_there:
-        pltpu.make_async_remote_copy(
-            src_ref=near_out,
-            dst_ref=near_labels.at[sub],
-            send_sem=near_send,
-            recv_sem=near_recv,
-            device_id=(blk, there),
-            device_id_type=MESH,
-        ).start()
 
     rank_row = jnp.sum(jnp.where(same & (line < lane), 1, 0), axis=0, keepdims=True)
     target = owner_row * 4 + rank_row * 2
@@ -336,6 +322,18 @@
 
     others = pl.ds(0, subs - 1)
     pltpu.make_async_copy(lists.at[others], lists.at[others], list_recv).wait()
+
+    z, y = lax.div(blk, 4), lax.rem(blk, 4)
+    labels[z, y] = jnp.concatenate([lists[:, 6, :], lists[:, 7, :]], axis=0).astype(BF16)
+    for step in range(1, 4):
+        pltpu.make_async_remote_copy(
+            src_ref=labels.at[z, y],
+            dst_ref=labels.at[z, y],
+            send_sem=y_send,
+            recv_sem=y_recv,
+            device_id=(z * 4 + around(y, step, 4), sub),
+            device_id_type=MESH,
+        ).start()
 
     @pl.when(sub == 0)
     def _():
@@ -365,18 +363,15 @@
     link_halo = for_features(jnp.concatenate([to_prev, jnp.where(half, lower, 0.0)], axis=0))
     inner = [linked(link_own, own[c]) for c in range(3)]
 
-    pltpu.make_async_copy(near_labels.at[others], near_labels.at[others], near_recv).wait()
-    far_out[...] = jnp.concatenate(
-        [near_labels[:, 0, :], near_labels[:, 1, :]], axis=0
-    ).astype(BF16)
-    labels[blk] = far_out[...]
-    for there in blks_there:
+    some = pl.ds(0, 3)
+    pltpu.make_async_copy(labels.at[0, some], labels.at[0, some], y_recv).wait()
+    for step in range(1, 4):
         pltpu.make_async_remote_copy(
-            src_ref=far_out,
-            dst_ref=labels.at[blk],
-            send_sem=far_send,
-            recv_sem=far_recv,
-            device_id=(there, sub),
+            src_ref=labels.at[z],
+            dst_ref=labels.at[z],
+            send_sem=z_send,
+            recv_sem=z_recv,
+            device_id=(around(z, step, 4) * 4 + y, sub),
             device_id_type=MESH,
         ).start()
 
@@ -399,7 +394,7 @@
     def turns(at, size):
         return [at] + [around(at, step, size) for step in range(1, size)]
 
-    z_to, y_to = turns(lax.div(blk, 4), 4), turns(lax.rem(blk, 4), 4)
+    z_to, y_to = turns(z, 4), turns(y, 4)
     x_to, core_to = turns(lax.div(sub, 2), 4), turns(lax.rem(sub, 2), 2)
     for dz, dy, dx, core in spread_order():
         blk_to, sub_to = z_to[dz] * 4 + y_to[dy], x_to[dx] * 2 + core_to[core]
@@ -412,8 +407,7 @@
             device_id_type=MESH,
         ).start()
 
-    some = pl.ds(0, blks - 1)
-    pltpu.make_async_copy(labels.at[some], labels.at[some], far_recv).wait()
+    pltpu.make_async_copy(labels.at[some], labels.at[some], z_recv).wait()
     by_owner = labels[...].reshape(2 * devices, NF)
     arrived = lax.broadcasted_iota(jnp.int32, (2 * devices, 4 * devices), 1)
     held = lax.broadcasted_iota(jnp.int32, (2 * devices, 4 * devices), 0)
@@ -450,8 +444,8 @@
             copy.wait_send()
     pltpu.make_async_copy(list_out.at[others], list_out.at[others], list_send).wait()
     over.wait_send()
-    pltpu.make_async_copy(near_labels.at[others], near_labels.at[others], near_send).wait()
-    pltpu.make_async_copy(labels.at[some], labels.at[some], far_send).wait()
+    pltpu.make_async_copy(labels.at[0, some], labels.at[0, some], y_send).wait()
+    pltpu.make_async_copy(labels.at[some], labels.at[some], z_send).wait()
     pltpu.make_async_copy(outgoing.at[most], outgoing.at[most], all_send).wait()
 
 
@@ -480,10 +474,7 @@
             pltpu.VMEM((8, NF), F32),
             pltpu.VMEM((subs, 8, NF), F32),
             pltpu.VMEM((subs, 8, NF), F32),
-            pltpu.VMEM((8, NF), F32),
-            pltpu.VMEM((subs, 8, NF), F32),
-            pltpu.VMEM((2 * subs, NF), BF16),
-            pltpu.VMEM((blks, 2 * subs, NF), BF16),
+            pltpu.VMEM((4, blks // 4, 2 * subs, NF), BF16),
             pltpu.VMEM((devices, 3, 4, NF), BF16),
             pltpu.VMEM((devices, 3, 4, NF), BF16),
             dma((13,)),

time: 26.4 us -> 27.2 us (1.030)
  Pallas kernels: 26.3 us -> 27.1 us
    pallas_call x1, Pallas kernels: 24.8 us -> 25.7 us  [exchange(): pl.pallas_call(functools.partial(exchange_kernel, blks, subs), out_shape=...]
where the time goes in v5:
time: 27.2 us; the launch traced here: 27.1 us
  Pallas kernels  27.1 us (100%)
    pallas_call x1, Pallas kernels, exchange(): pl.pallas_call(functools.partial(exchange_kernel, blks, subs), out_shape=...  25.7 us
    pallas_call x1, Pallas kernels, finish(): pl.pallas_call(finish_kernel, out_shape=jax.ShapeDtypeStruct((count, samp...  1.44 us

profile of v5, /device:TPU:1, one launch (start us, length us, event | category | flops | bytes accessed | tf_op | source)
XLA Modules:
  0.0 27.1 jit_solution(5922896270834052376)
XLA Ops:
  0.0 0.0 copy-start
  0.0 25.7 %exchange.1.summed = bf16[384,256]{1,0:T(8,128)(2,1)S(1)} custom-call(bf16[3,128,1024]{2,1,0:T(8,128)(2,1)} %bitcast.7, bf16[3,128,1024]{2,1,0:T(8,128)(2,1)} %bitcast.8, bf16[1024,256]{1,0:T(8,128)(2,1)} %constant.4.clone.table_hbm, s32[16,128]{1,0:T(8,128)} %first_hbm.1, s32[16,128]{1,0:T(8,128)} %second_hbm.1, s32[16,128]{1,0:T(8,128)} %mask_hbm.1, ...), custom_call_target="tpu_custom_call" | custom-call | flops 2000000000 | bytes 3000000 | tf_op jit(solution)/shard_map/exchange/pallas_call | solution.py:457
  25.7 0.0 copy-done
  25.7 1.4 %finish.1 = f32[384,1024]{1,0:T(8,128)} custom-call(bf16[384,256]{1,0:T(8,128)(2,1)S(1)} %exchange.1.summed, bf16[256,1024]{1,0:T(8,128)(2,1)S(1)} %copy-done), custom_call_target="tpu_custom_call" | custom-call | flops 700000000 | bytes 3000000 | tf_op jit(solution)/shard_map/finish/pallas_call | solution.py:523
Async XLA Ops:
  0.0 25.7 %copy-start = (bf16[256,1024]{1,0:T(8,128)(2,1)S(1)}, bf16[256,1024]{1,0:T(8,128)(2,1)}, u32[]{:S(2)}) copy-start(bf16[256,1024]{1,0:T(8,128)(2,1)} %constant.5.clone.table) | copy-start | bytes 1572868

commit v6 on v5

--- a/solution.py
+++ b/solution.py
@@ -90,7 +90,7 @@
 
 
 def spread_order():
-    left = list(itertools.product(range(4), range(4), range(4), range(2)))[1:]
+    left = list(itertools.product(range(2), range(4), range(4), range(2)))[1:]
     ways = {0: (0.0, 0.0), 1: (1.0, 0.0), 2: (1.0, 1.0), 3: (0.0, 1.0)}
 
     def links(step):
@@ -134,6 +134,7 @@
     lists_prev,
     labels,
     outgoing,
+    gathered,
     received,
     load_sems,
     list_send,
@@ -147,12 +148,16 @@
     y_recv,
     z_send,
     z_recv,
+    sibling_send,
+    sibling_recv,
     all_send,
     all_recv,
 ):
     devices = blks * subs
     blk, sub = lax.axis_index("blk"), lax.axis_index("sub")
     me = blk * subs + sub
+    core, served = lax.rem(sub, 2), devices // 2
+    sibling = sub + 1 - 2 * core
     rows = spec.shape[1]
     blocks = first.shape[0]
     def around(at, step, size):
@@ -311,9 +316,24 @@
         pl.semaphore_signal(joined, inc=1, device_id=(blk, there), device_id_type=MESH)
 
     rank_row = jnp.sum(jnp.where(same & (line < lane), 1, 0), axis=0, keepdims=True)
-    target = owner_row * 4 + rank_row * 2
+    target = (owner_row ^ (core * served)) * 4 + rank_row * 2
     slot = lax.broadcasted_iota(jnp.int32, (4 * devices, 2 * rows), 0)
     placement = (slot == jnp.concatenate([target, target + 1], axis=1)).astype(F32).astype(BF16)
+
+    def sort_out(c, values):
+        tiles = values.astype(BF16).reshape(2, served, 4, NF)
+        gathered[:, core, c] = tiles[0]
+        outgoing[c] = tiles[1]
+        copy = pltpu.make_async_remote_copy(
+            src_ref=outgoing.at[c],
+            dst_ref=gathered.at[:, core, c],
+            send_sem=sibling_send.at[c],
+            recv_sem=sibling_recv.at[c],
+            device_id=(blk, sibling),
+            device_id_type=MESH,
+        )
+        copy.start()
+        return copy
 
     def stations(c):
         return (spec[2 * c], spec[2 * c + 1])
@@ -375,6 +395,7 @@
             device_id_type=MESH,
         ).start()
 
+    sorted_out = []
     for c in range(3):
         for copy in halos[c]:
             copy.wait_recv()
@@ -386,26 +407,50 @@
         real = (xr * g1r - xi * g1i) + (dr * g2r - di * g2i)
         imag = (xr * g1i + xi * g1r) + (dr * g2i + di * g2r)
         adjoint = jnp.concatenate([real, imag], axis=0).astype(BF16)
-        outgoing[:, c] = dot_plain(placement, adjoint).astype(BF16).reshape(devices, 4, NF)
-    received[me] = outgoing[me]
+        sorted_out.append(sort_out(c, dot_plain(placement, adjoint)))
 
     pl.semaphore_wait(joined, subs - 1)
+    for copy in sorted_out:
+        copy.wait_recv()
 
     def turns(at, size):
         return [at] + [around(at, step, size) for step in range(1, size)]
 
-    z_to, y_to = turns(z, 4), turns(y, 4)
-    x_to, core_to = turns(lax.div(sub, 2), 4), turns(lax.rem(sub, 2), 2)
-    for dz, dy, dx, core in spread_order():
-        blk_to, sub_to = z_to[dz] * 4 + y_to[dy], x_to[dx] * 2 + core_to[core]
+    x = lax.div(sub, 2)
+    z_near = lax.rem(z, 2)
+    near_to, y_to, x_to, core_to = [z_near, 1 - z_near], turns(y, 4), turns(x, 4), turns(core, 2)
+    home = lax.div(z, 2) == core
+    chip = lax.div(me, 2)
+
+    def deliver(step):
+        dz, dy, dx, dcore = step
+        blk_to, sub_to = near_to[dz] * 4 + y_to[dy], x_to[dx] * 2 + core_to[dcore]
+        return gathered.at[blk_to * subs + sub_to], (core * 8 + blk_to, sub_to)
+
+    def deliver_away(step):
+        tile, there = deliver(step)
         pltpu.make_async_remote_copy(
-            src_ref=outgoing.at[blk_to * subs + sub_to],
-            dst_ref=received.at[me],
+            src_ref=tile,
+            dst_ref=received.at[chip],
             send_sem=all_send,
             recv_sem=all_recv,
-            device_id=(blk_to, sub_to),
+            device_id=there,
             device_id_type=MESH,
         ).start()
+
+    for step in spread_order():
+        deliver_away(step)
+
+    @pl.when(home)
+    def _():
+        tile, _ = deliver((0, 0, 0, 0))
+        kept = pltpu.make_async_copy(tile, received.at[chip], load_sems.at[0])
+        kept.start()
+        kept.wait()
+
+    @pl.when(jnp.logical_not(home))
+    def _():
+        deliver_away((0, 0, 0, 0))
 
     pltpu.make_async_copy(labels.at[some], labels.at[some], z_recv).wait()
     by_owner = labels[...].reshape(2 * devices, NF)
@@ -432,10 +477,20 @@
         ],
         axis=0,
     ).astype(BF16)
-    most = pl.ds(0, devices - 1)
-    pltpu.make_async_copy(received.at[most], received.at[most], all_recv).wait()
+    most = pl.ds(0, served - 1)
+
+    def wait_for(ref, sem):
+        @pl.when(home)
+        def _():
+            pltpu.make_async_copy(ref.at[most], ref.at[most], sem).wait()
+
+        @pl.when(jnp.logical_not(home))
+        def _():
+            pltpu.make_async_copy(ref, ref, sem).wait()
+
+    wait_for(received, all_recv)
     for c in range(3):
-        sums = dot_plain(collect, received[:, c].reshape(4 * devices, NF)).astype(BF16)
+        sums = dot_plain(collect, received[:, :, c].reshape(4 * devices, NF)).astype(BF16)
         summed[c * rows : (c + 1) * rows, :NF] = sums[:rows]
         summed[c * rows : (c + 1) * rows, NF:] = sums[rows:]
 
@@ -446,7 +501,9 @@
     over.wait_send()
     pltpu.make_async_copy(labels.at[0, some], labels.at[0, some], y_send).wait()
     pltpu.make_async_copy(labels.at[some], labels.at[some], z_send).wait()
-    pltpu.make_async_copy(outgoing.at[most], outgoing.at[most], all_send).wait()
+    for copy in sorted_out:
+        copy.wait_send()
+    wait_for(gathered, all_send)
 
 
 def exchange(blks, subs, syn, obs, table, first, second, mask, weight, owner, element):
@@ -475,8 +532,9 @@
             pltpu.VMEM((subs, 8, NF), F32),
             pltpu.VMEM((subs, 8, NF), F32),
             pltpu.VMEM((4, blks // 4, 2 * subs, NF), BF16),
-            pltpu.VMEM((devices, 3, 4, NF), BF16),
-            pltpu.VMEM((devices, 3, 4, NF), BF16),
+            pltpu.VMEM((3, devices // 2, 4, NF), BF16),
+            pltpu.VMEM((devices // 2, 2, 3, 4, NF), BF16),
+            pltpu.VMEM((devices // 2, 2, 3, 4, NF), BF16),
             dma((13,)),
             dma,
             dma,
@@ -489,6 +547,8 @@
             dma,
             dma,
             dma,
+            dma((3,)),
+            dma((3,)),
             dma,
             dma,
         ],

time: 27.2 us -> 28.6 us (1.051)
  Pallas kernels: 27.1 us -> 28.5 us
    pallas_call x1, Pallas kernels: 25.7 us -> 27 us  [exchange(): pl.pallas_call(functools.partial(exchange_kernel, blks, subs), out_shape=...]
where the time goes in v6:
time: 28.6 us; the launch traced here: 28.5 us
  Pallas kernels  28.5 us (100%)
    pallas_call x1, Pallas kernels, exchange(): pl.pallas_call(functools.partial(exchange_kernel, blks, subs), out_shape=...  27 us
    pallas_call x1, Pallas kernels, finish(): pl.pallas_call(finish_kernel, out_shape=jax.ShapeDtypeStruct((count, samp...  1.44 us

profile of v6, /device:TPU:1, one launch (start us, length us, event | category | flops | bytes accessed | tf_op | source)
XLA Modules:
  0.0 28.5 jit_solution(15873503520631831005)
XLA Ops:
  0.0 0.0 copy-start
  0.0 27.0 %exchange.1.summed = bf16[384,256]{1,0:T(8,128)(2,1)S(1)} custom-call(bf16[3,128,1024]{2,1,0:T(8,128)(2,1)} %bitcast.7, bf16[3,128,1024]{2,1,0:T(8,128)(2,1)} %bitcast.8, bf16[1024,256]{1,0:T(8,128)(2,1)} %constant.4.clone.table_hbm, s32[16,128]{1,0:T(8,128)} %first_hbm.1, s32[16,128]{1,0:T(8,128)} %second_hbm.1, s32[16,128]{1,0:T(8,128)} %mask_hbm.1, ...), custom_call_target="tpu_custom_call" | custom-call | flops 2000000000 | bytes 3000000 | tf_op jit(solution)/shard_map/exchange/pallas_call | solution.py:514
  27.0 0.0 copy-done
  27.1 1.4 %finish.1 = f32[384,1024]{1,0:T(8,128)} custom-call(bf16[384,256]{1,0:T(8,128)(2,1)S(1)} %exchange.1.summed, bf16[256,1024]{1,0:T(8,128)(2,1)S(1)} %copy-done), custom_call_target="tpu_custom_call" | custom-call | flops 700000000 | bytes 3000000 | tf_op jit(solution)/shard_map/finish/pallas_call | solution.py:583
Async XLA Ops:
  0.0 27.0 %copy-start = (bf16[256,1024]{1,0:T(8,128)(2,1)S(1)}, bf16[256,1024]{1,0:T(8,128)(2,1)}, u32[]{:S(2)}) copy-start(bf16[256,1024]{1,0:T(8,128)(2,1)} %constant.5.clone.table) | copy-start | bytes 1572868

commit v7 on v5

--- a/solution.py
+++ b/solution.py
@@ -363,18 +363,6 @@
     link_halo = for_features(jnp.concatenate([to_prev, jnp.where(half, lower, 0.0)], axis=0))
     inner = [linked(link_own, own[c]) for c in range(3)]
 
-    some = pl.ds(0, 3)
-    pltpu.make_async_copy(labels.at[0, some], labels.at[0, some], y_recv).wait()
-    for step in range(1, 4):
-        pltpu.make_async_remote_copy(
-            src_ref=labels.at[z],
-            dst_ref=labels.at[z],
-            send_sem=z_send,
-            recv_sem=z_recv,
-            device_id=(around(z, step, 4) * 4 + y, sub),
-            device_id_type=MESH,
-        ).start()
-
     for c in range(3):
         for copy in halos[c]:
             copy.wait_recv()
@@ -396,7 +384,8 @@
 
     z_to, y_to = turns(z, 4), turns(y, 4)
     x_to, core_to = turns(lax.div(sub, 2), 4), turns(lax.rem(sub, 2), 2)
-    for dz, dy, dx, core in spread_order():
+    def deliver(step):
+        dz, dy, dx, core = step
         blk_to, sub_to = z_to[dz] * 4 + y_to[dy], x_to[dx] * 2 + core_to[core]
         pltpu.make_async_remote_copy(
             src_ref=outgoing.at[blk_to * subs + sub_to],
@@ -406,6 +395,24 @@
             device_id=(blk_to, sub_to),
             device_id_type=MESH,
         ).start()
+
+    order = spread_order()
+    for step in order[:32]:
+        deliver(step)
+    some = pl.ds(0, 3)
+    pltpu.make_async_copy(labels.at[0, some], labels.at[0, some], y_recv).wait()
+    for step in range(1, 4):
+        pltpu.make_async_remote_copy(
+            src_ref=labels.at[z],
+            dst_ref=labels.at[z],
+            send_sem=z_send,
+            recv_sem=z_recv,
+            device_id=(around(z, step, 4) * 4 + y, sub),
+            device_id_type=MESH,
+        ).start()
+
+    for step in order[32:]:
+        deliver(step)
 
     pltpu.make_async_copy(labels.at[some], labels.at[some], z_recv).wait()
     by_owner = labels[...].reshape(2 * devices, NF)

time: 27.2 us -> 25.5 us (0.938)
  Pallas kernels: 27.1 us -> 25.3 us
    pallas_call x1, Pallas kernels: 25.7 us -> 23.9 us  [exchange(): pl.pallas_call(functools.partial(exchange_kernel, blks, subs), out_shape=...]
where the time goes in v7:
time: 25.5 us; the launch traced here: 25.4 us
  Pallas kernels  25.3 us (99%)
    pallas_call x1, Pallas kernels, exchange(): pl.pallas_call(functools.partial(exchange_kernel, blks, subs), out_shape=...  23.9 us
    pallas_call x1, Pallas kernels, finish(): pl.pallas_call(finish_kernel, out_shape=jax.ShapeDtypeStruct((count, samp...  1.44 us

profile of v7, /device:TPU:1, one launch (start us, length us, event | category | flops | bytes accessed | tf_op | source)
XLA Modules:
  0.0 25.4 jit_solution(12467465031392013920)
XLA Ops:
  0.0 0.0 copy-start
  0.0 23.9 %exchange.1.summed = bf16[384,256]{1,0:T(8,128)(2,1)S(1)} custom-call(bf16[3,128,1024]{2,1,0:T(8,128)(2,1)} %bitcast.7, bf16[3,128,1024]{2,1,0:T(8,128)(2,1)} %bitcast.8, bf16[1024,256]{1,0:T(8,128)(2,1)} %constant.4.clone.table_hbm, s32[16,128]{1,0:T(8,128)} %first_hbm.1, s32[16,128]{1,0:T(8,128)} %second_hbm.1, s32[16,128]{1,0:T(8,128)} %mask_hbm.1, ...), custom_call_target="tpu_custom_call" | custom-call | flops 2000000000 | bytes 3000000 | tf_op jit(solution)/shard_map/exchange/pallas_call | solution.py:464
  23.9 0.0 copy-done
  23.9 1.4 %finish.1 = f32[384,1024]{1,0:T(8,128)} custom-call(bf16[384,256]{1,0:T(8,128)(2,1)S(1)} %exchange.1.summed, bf16[256,1024]{1,0:T(8,128)(2,1)S(1)} %copy-done), custom_call_target="tpu_custom_call" | custom-call | flops 700000000 | bytes 3000000 | tf_op jit(solution)/shard_map/finish/pallas_call | solution.py:530
Async XLA Ops:
  0.0 23.9 %copy-start = (bf16[256,1024]{1,0:T(8,128)(2,1)S(1)}, bf16[256,1024]{1,0:T(8,128)(2,1)}, u32[]{:S(2)}) copy-start(bf16[256,1024]{1,0:T(8,128)(2,1)} %constant.5.clone.table) | copy-start | bytes 1572868

commit v8 on v7

--- a/solution.py
+++ b/solution.py
@@ -89,8 +89,8 @@
     return jnp.concatenate(parts, axis=0)
 
 
-def spread_order():
-    left = list(itertools.product(range(4), range(4), range(4), range(2)))[1:]
+def spread_order(core):
+    left = [step + (core,) for step in itertools.product(range(4), range(4), range(4))]
     ways = {0: (0.0, 0.0), 1: (1.0, 0.0), 2: (1.0, 1.0), 3: (0.0, 1.0)}
 
     def links(step):
@@ -351,11 +351,9 @@
     first1, second1, weight1 = unpacked(lists, 1)
     first2, second2, weight2 = unpacked(lists, 2)
     to_prev = dot_rows(spread_weights(second0, weight0, BLOCK, BLOCK), spread(first0, rows, 0))
-    upper = dot_rows(spread(first1, BLOCK, 0), spread_weights(second1, weight1, rows, 0))
-    lower = dot_rows(spread(first2, BLOCK, 0), spread_weights(second2, weight2, rows, 0))
-    to_prev = to_prev[:BLOCK] + to_prev[BLOCK:]
-    upper = upper[:, :rows] + upper[:, rows:]
-    lower = lower[:, :rows] + lower[:, rows:]
+    upper = dot_rows(spread_weights(first1, weight1, BLOCK, 0), spread(second1, rows, 0))
+    lower = dot_rows(spread_weights(first2, weight2, BLOCK, 0), spread(second2, rows, 0))
+    to_prev, upper, lower = (both[:BLOCK] + both[BLOCK:] for both in (to_prev, upper, lower))
     half = lax.broadcasted_iota(jnp.int32, (BLOCK, rows), 1) >= BLOCK
     inside = jnp.where(half, pltpu.roll(lower, BLOCK, 1), 0.0)
     one_way = jnp.concatenate([upper, inside], axis=0)
@@ -375,28 +373,33 @@
         imag = (xr * g1i + xi * g1r) + (dr * g2i + di * g2r)
         adjoint = jnp.concatenate([real, imag], axis=0).astype(BF16)
         outgoing[:, c] = dot_plain(placement, adjoint).astype(BF16).reshape(devices, 4, NF)
-    received[me] = outgoing[me]
 
     pl.semaphore_wait(joined, subs - 1)
 
+    core = lax.rem(sub, 2)
+
     def turns(at, size):
-        return [at] + [around(at, step, size) for step in range(1, size)]
-
-    z_to, y_to = turns(z, 4), turns(y, 4)
-    x_to, core_to = turns(lax.div(sub, 2), 4), turns(lax.rem(sub, 2), 2)
+        up = [around(at, step, size) for step in range(1, size)]
+        return [at] + [jnp.where(core == 0, up[i], up[-1 - i]) for i in range(size - 1)]
+
+    chip = lax.div(me, 2)
+    z_to, y_to, x_to = turns(z, 4), turns(y, 4), turns(lax.div(sub, 2), 4)
+    core_to = [core, 1 - core]
+    received[core, chip] = outgoing[me]
+
     def deliver(step):
-        dz, dy, dx, core = step
-        blk_to, sub_to = z_to[dz] * 4 + y_to[dy], x_to[dx] * 2 + core_to[core]
+        dz, dy, dx, other = step
+        blk_to, sub_to = z_to[dz] * 4 + y_to[dy], x_to[dx] * 2 + core_to[other]
         pltpu.make_async_remote_copy(
             src_ref=outgoing.at[blk_to * subs + sub_to],
-            dst_ref=received.at[me],
+            dst_ref=received.at[core, chip],
             send_sem=all_send,
-            recv_sem=all_recv,
+            recv_sem=all_recv.at[other],
             device_id=(blk_to, sub_to),
             device_id_type=MESH,
         ).start()
 
-    order = spread_order()
+    order = spread_order(1) + spread_order(0)[1:]
     for step in order[:32]:
         deliver(step)
     some = pl.ds(0, 3)
@@ -416,35 +419,45 @@
 
     pltpu.make_async_copy(labels.at[some], labels.at[some], z_recv).wait()
     by_owner = labels[...].reshape(2 * devices, NF)
-    arrived = lax.broadcasted_iota(jnp.int32, (2 * devices, 4 * devices), 1)
-    held = lax.broadcasted_iota(jnp.int32, (2 * devices, 4 * devices), 0)
+    arrived = lax.broadcasted_iota(jnp.int32, (2 * devices, 2 * devices), 1)
+    held = lax.broadcasted_iota(jnp.int32, (2 * devices, 2 * devices), 0)
     sub_bits = subs.bit_length() - 1
     wanted = (
-        ((arrived >> (sub_bits + 2)) << (sub_bits + 1))
+        ((arrived >> (sub_bits + 1)) << (sub_bits + 1))
         + (((arrived >> 1) & 1) << sub_bits)
-        + ((arrived >> 2) & (subs - 1))
-    )
-    repeated = lax.dot_general(
-        by_owner,
-        (held == wanted).astype(F32).astype(BF16),
-        (((0,), (0,)), ((), ())),
-        preferred_element_type=F32,
-    )
-    owner_line = lax.broadcasted_iota(jnp.int32, repeated.shape, 0)
-    label = jnp.sum(jnp.where(owner_line == me, repeated, 0.0), axis=0, keepdims=True)
-    collect = jnp.concatenate(
-        [
-            ((label == owner_line.astype(F32)) & ((arrived[:rows] & 1) == i)).astype(F32)
-            for i in range(2)
-        ],
-        axis=0,
-    ).astype(BF16)
-    most = pl.ds(0, devices - 1)
-    pltpu.make_async_copy(received.at[most], received.at[most], all_recv).wait()
+        + (((arrived >> 2) & (subs // 2 - 1)) << 1)
+    )
+    owner_line = lax.broadcasted_iota(jnp.int32, (rows, 2 * devices), 0)
+
+    def collector(source_core):
+        repeated = lax.dot_general(
+            by_owner,
+            (held == wanted + source_core).astype(F32).astype(BF16),
+            (((0,), (0,)), ((), ())),
+            preferred_element_type=F32,
+        )
+        label = jnp.sum(jnp.where(owner_line == me, repeated, 0.0), axis=0, keepdims=True)
+        return jnp.concatenate(
+            [
+                ((label == owner_line.astype(F32)) & ((arrived[:rows] & 1) == i)).astype(F32)
+                for i in range(2)
+            ],
+            axis=0,
+        ).astype(BF16)
+
+    collect_other, collect_same = collector(1 - core), collector(core)
+
+    def sums(collect, source_core, c):
+        return dot_plain(collect, received[source_core, :, c].reshape(2 * devices, NF))
+
+    pltpu.make_async_copy(received.at[0], received.at[0], all_recv.at[1]).wait()
+    first_sums = [sums(collect_other, 1 - core, c) for c in range(3)]
+    most = pl.ds(0, devices // 2 - 1)
+    pltpu.make_async_copy(received.at[0, most], received.at[0, most], all_recv.at[0]).wait()
     for c in range(3):
-        sums = dot_plain(collect, received[:, c].reshape(4 * devices, NF)).astype(BF16)
-        summed[c * rows : (c + 1) * rows, :NF] = sums[:rows]
-        summed[c * rows : (c + 1) * rows, NF:] = sums[rows:]
+        total = (first_sums[c] + sums(collect_same, core, c)).astype(BF16)
+        summed[c * rows : (c + 1) * rows, :NF] = total[:rows]
+        summed[c * rows : (c + 1) * rows, NF:] = total[rows:]
 
     for c in range(3):
         for copy in halos[c]:
@@ -453,6 +466,7 @@
     over.wait_send()
     pltpu.make_async_copy(labels.at[0, some], labels.at[0, some], y_send).wait()
     pltpu.make_async_copy(labels.at[some], labels.at[some], z_send).wait()
+    most = pl.ds(0, devices - 1)
     pltpu.make_async_copy(outgoing.at[most], outgoing.at[most], all_send).wait()
 
 
@@ -483,7 +497,7 @@
             pltpu.VMEM((subs, 8, NF), F32),
             pltpu.VMEM((4, blks // 4, 2 * subs, NF), BF16),
             pltpu.VMEM((devices, 3, 4, NF), BF16),
-            pltpu.VMEM((devices, 3, 4, NF), BF16),
+            pltpu.VMEM((2, devices // 2, 3, 4, NF), BF16),
             dma((13,)),
             dma,
             dma,
@@ -497,7 +511,7 @@
             dma,
             dma,
             dma,
-            dma,
+            dma((2,)),
         ],
         compiler_params=pltpu.CompilerParams(
             collective_id=0, has_side_effects=True, vmem_limit_bytes=60 * 2**20

time: 25.5 us -> 25.6 us (level)
  no operation moved by 1% of the time
where the time goes in v8:
time: 25.6 us; the launch traced here: 25.5 us
  Pallas kernels  25.4 us (99%)
    pallas_call x1, Pallas kernels, exchange(): pl.pallas_call(functools.partial(exchange_kernel, blks, subs), out_shape=...  24 us
    pallas_call x1, Pallas kernels, finish(): pl.pallas_call(finish_kernel, out_shape=jax.ShapeDtypeStruct((count, samp...  1.44 us

profile of v8, /device:TPU:1, one launch (start us, length us, event | category | flops | bytes accessed | tf_op | source)
XLA Modules:
  0.0 25.5 jit_solution(17285208752284184904)
XLA Ops:
  0.0 0.0 copy-start
  0.0 24.0 %exchange.1.summed = bf16[384,256]{1,0:T(8,128)(2,1)S(1)} custom-call(bf16[3,128,1024]{2,1,0:T(8,128)(2,1)} %bitcast.7, bf16[3,128,1024]{2,1,0:T(8,128)(2,1)} %bitcast.8, bf16[1024,256]{1,0:T(8,128)(2,1)} %constant.4.clone.table_hbm, s32[16,128]{1,0:T(8,128)} %first_hbm.1, s32[16,128]{1,0:T(8,128)} %second_hbm.1, s32[16,128]{1,0:T(8,128)} %mask_hbm.1, ...), custom_call_target="tpu_custom_call" | custom-call | flops 2000000000 | bytes 3000000 | tf_op jit(solution)/shard_map/exchange/pallas_call | solution.py:478
  24.0 0.0 copy-done
  24.0 1.4 %finish.1 = f32[384,1024]{1,0:T(8,128)} custom-call(bf16[384,256]{1,0:T(8,128)(2,1)S(1)} %exchange.1.summed, bf16[256,1024]{1,0:T(8,128)(2,1)S(1)} %copy-done), custom_call_target="tpu_custom_call" | custom-call | flops 700000000 | bytes 3000000 | tf_op jit(solution)/shard_map/finish/pallas_call | solution.py:544
Async XLA Ops:
  0.0 24.0 %copy-start = (bf16[256,1024]{1,0:T(8,128)(2,1)S(1)}, bf16[256,1024]{1,0:T(8,128)(2,1)}, u32[]{:S(2)}) copy-start(bf16[256,1024]{1,0:T(8,128)(2,1)} %constant.5.clone.table) | copy-start | bytes 1572868

commit v9 on v8

--- a/solution.py
+++ b/solution.py
@@ -132,6 +132,8 @@
     list_over,
     lists,
     lists_prev,
+    near_out,
+    near_labels,
     labels,
     outgoing,
     received,
@@ -143,6 +145,8 @@
     halo_send,
     halo_recv,
     joined,
+    near_send,
+    near_recv,
     y_send,
     y_recv,
     z_send,
@@ -166,19 +170,19 @@
     before = (jnp.where(sub == 0, blk_before, blk), subs_there[-1])
 
     pairs = [
-        (owner_hbm, owner),
-        (element_hbm, element),
+        (table_hbm, table),
+        (syn_hbm.at[0], traces.at[0, pl.ds(0, rows)]),
+        (obs_hbm.at[0], traces.at[0, pl.ds(rows, rows)]),
         (first_hbm, first),
         (second_hbm, second),
         (mask_hbm, mask),
         (weight_hbm, weight),
-        (table_hbm, table),
-        (syn_hbm.at[0], traces.at[0, pl.ds(0, rows)]),
-        (obs_hbm.at[0], traces.at[0, pl.ds(rows, rows)]),
         (syn_hbm.at[1], traces.at[1, pl.ds(0, rows)]),
         (obs_hbm.at[1], traces.at[1, pl.ds(rows, rows)]),
         (syn_hbm.at[2], traces.at[2, pl.ds(0, rows)]),
         (obs_hbm.at[2], traces.at[2, pl.ds(rows, rows)]),
+        (owner_hbm, owner),
+        (element_hbm, element),
     ]
     loads = [
         pltpu.make_async_copy(src, dst, load_sems.at[i]) for i, (src, dst) in enumerate(pairs)
@@ -205,76 +209,16 @@
     def _():
         greet((blk_after, 0))
 
-    for i in range(2):
-        loads[i].wait()
-    lane = lax.broadcasted_iota(jnp.int32, (rows, rows), 1)
-    line = lax.broadcasted_iota(jnp.int32, (rows, rows), 0)
-    owner_row = owner[...]
-
-    def column(row):
-        return jnp.sum(jnp.where(lane == line, row, 0), axis=1, keepdims=True)
-
-    owner_column, element_column = column(owner_row), column(element[...]).astype(F32)
-    same = owner_column == owner_row
-    rank_column = jnp.sum(jnp.where(same & (lane < line), 1, 0), axis=1, keepdims=True)
-    label_rows = []
-    for k in range(2):
-        chosen = ((owner_column == lane) & (rank_column == k)).astype(F32)
-        label_rows.append(
-            jnp.sum(chosen * (element_column - rows), axis=0, keepdims=True) + float(rows)
-        )
-
-    for i in range(2, 6):
-        loads[i].wait()
-    base = (blk * blocks + lax.broadcasted_iota(jnp.int32, (blocks, NF), 0)) * BLOCK
-    code = ((first[...] - base) * (2 * BLOCK) + (second[...] - base)).astype(F32)
-    slot_weight = weight[...] * mask[...].astype(F32)
-    zero_row = jnp.zeros((1, NF), F32)
-    for s in range(subs):
-        lines = [max(2 * s - 1, 0), 2 * s, 2 * s + 1]
-        list_out[s] = jnp.concatenate(
-            [code[i : i + 1] for i in lines]
-            + [slot_weight[i : i + 1] for i in lines]
-            + label_rows,
-            axis=0,
-        )
-    list_over[...] = jnp.concatenate(
-        [code[blocks - 1 : blocks]]
-        + [zero_row] * 2
-        + [slot_weight[blocks - 1 : blocks]]
-        + [zero_row] * 4,
-        axis=0,
-    )
-    lists[sub] = list_out[sub]
-
-    pl.semaphore_wait(barrier, subs + blks - 1)
-    for there in subs_there:
-        pltpu.make_async_remote_copy(
-            src_ref=list_out.at[there],
-            dst_ref=lists.at[sub],
-            send_sem=list_send,
-            recv_sem=list_recv,
-            device_id=(blk, there),
-            device_id_type=MESH,
-        ).start()
-    over = pltpu.make_async_remote_copy(
-        src_ref=list_over,
-        dst_ref=lists_prev.at[sub],
-        send_sem=over_send,
-        recv_sem=over_recv,
-        device_id=(blk_after, 0),
-        device_id_type=MESH,
-    )
-    over.start()
-
     def transform(c):
         both = dot_plain(traces[c], table[...]).astype(BF16)
         spec[2 * c] = both[:rows]
         spec[2 * c + 1] = both[rows:]
 
-    for i in range(6, 9):
+    for i in range(3):
         loads[i].wait()
     transform(0)
+
+    pl.semaphore_wait(barrier, subs + blks - 1)
 
     def halo_copies(c):
         q = pl.ds(2 * c, 2)
@@ -300,15 +244,89 @@
     halos = [halo_copies(c) for c in range(3)]
     for copy in halos[0]:
         copy.start()
+
+    for i in range(3, 7):
+        loads[i].wait()
+    base = (blk * blocks + lax.broadcasted_iota(jnp.int32, (blocks, NF), 0)) * BLOCK
+    code = ((first[...] - base) * (2 * BLOCK) + (second[...] - base)).astype(F32)
+    slot_weight = weight[...] * mask[...].astype(F32)
+    zero_row = jnp.zeros((1, NF), F32)
+    for s in range(subs):
+        lines = [max(2 * s - 1, 0), 2 * s, 2 * s + 1]
+        list_out[s] = jnp.concatenate(
+            [code[i : i + 1] for i in lines]
+            + [slot_weight[i : i + 1] for i in lines]
+            + [zero_row] * 2,
+            axis=0,
+        )
+    list_over[...] = jnp.concatenate(
+        [code[blocks - 1 : blocks]]
+        + [zero_row] * 2
+        + [slot_weight[blocks - 1 : blocks]]
+        + [zero_row] * 4,
+        axis=0,
+    )
+    lists[sub] = list_out[sub]
+
+    for there in subs_there:
+        pltpu.make_async_remote_copy(
+            src_ref=list_out.at[there],
+            dst_ref=lists.at[sub],
+            send_sem=list_send,
+            recv_sem=list_recv,
+            device_id=(blk, there),
+            device_id_type=MESH,
+        ).start()
+    over = pltpu.make_async_remote_copy(
+        src_ref=list_over,
+        dst_ref=lists_prev.at[sub],
+        send_sem=over_send,
+        recv_sem=over_recv,
+        device_id=(blk_after, 0),
+        device_id_type=MESH,
+    )
+    over.start()
+
     for c in (1, 2):
-        loads[7 + 2 * c].wait()
-        loads[8 + 2 * c].wait()
+        loads[5 + 2 * c].wait()
+        loads[6 + 2 * c].wait()
         transform(c)
         for copy in halos[c]:
             copy.start()
 
     for there in subs_there:
         pl.semaphore_signal(joined, inc=1, device_id=(blk, there), device_id_type=MESH)
+
+    loads[11].wait()
+    loads[12].wait()
+    lane = lax.broadcasted_iota(jnp.int32, (rows, rows), 1)
+    line = lax.broadcasted_iota(jnp.int32, (rows, rows), 0)
+    owner_row = owner[...]
+
+    def column(row):
+        return jnp.sum(jnp.where(lane == line, row, 0), axis=1, keepdims=True)
+
+    owner_column, element_column = column(owner_row), column(element[...]).astype(F32)
+    same = owner_column == owner_row
+    rank_column = jnp.sum(jnp.where(same & (lane < line), 1, 0), axis=1, keepdims=True)
+    label_rows = []
+    for k in range(2):
+        chosen = ((owner_column == lane) & (rank_column == k)).astype(F32)
+        label_rows.append(
+            jnp.sum(chosen * (element_column - rows), axis=0, keepdims=True) + float(rows)
+        )
+
+    near_out[...] = jnp.concatenate(label_rows + [zero_row] * 6, axis=0)
+    near_labels[sub] = near_out[...]
+    for there in subs_there:
+        pltpu.make_async_remote_copy(
+            src_ref=near_out,
+            dst_ref=near_labels.at[sub],
+            send_sem=near_send,
+            recv_sem=near_recv,
+            device_id=(blk, there),
+            device_id_type=MESH,
+        ).start()
 
     rank_row = jnp.sum(jnp.where(same & (line < lane), 1, 0), axis=0, keepdims=True)
     target = owner_row * 4 + rank_row * 2
@@ -322,18 +340,6 @@
 
     others = pl.ds(0, subs - 1)
     pltpu.make_async_copy(lists.at[others], lists.at[others], list_recv).wait()
-
-    z, y = lax.div(blk, 4), lax.rem(blk, 4)
-    labels[z, y] = jnp.concatenate([lists[:, 6, :], lists[:, 7, :]], axis=0).astype(BF16)
-    for step in range(1, 4):
-        pltpu.make_async_remote_copy(
-            src_ref=labels.at[z, y],
-            dst_ref=labels.at[z, y],
-            send_sem=y_send,
-            recv_sem=y_recv,
-            device_id=(z * 4 + around(y, step, 4), sub),
-            device_id_type=MESH,
-        ).start()
 
     @pl.when(sub == 0)
     def _():
@@ -360,6 +366,21 @@
     link_own = for_features(one_way + one_way.T)
     link_halo = for_features(jnp.concatenate([to_prev, jnp.where(half, lower, 0.0)], axis=0))
     inner = [linked(link_own, own[c]) for c in range(3)]
+
+    z, y = lax.div(blk, 4), lax.rem(blk, 4)
+    pltpu.make_async_copy(near_labels.at[others], near_labels.at[others], near_recv).wait()
+    labels[z, y] = jnp.concatenate(
+        [near_labels[:, 0, :], near_labels[:, 1, :]], axis=0
+    ).astype(BF16)
+    for step in range(1, 4):
+        pltpu.make_async_remote_copy(
+            src_ref=labels.at[z, y],
+            dst_ref=labels.at[z, y],
+            send_sem=y_send,
+            recv_sem=y_recv,
+            device_id=(z * 4 + around(y, step, 4), sub),
+            device_id_type=MESH,
+        ).start()
 
     for c in range(3):
         for copy in halos[c]:
@@ -464,6 +485,7 @@
             copy.wait_send()
     pltpu.make_async_copy(list_out.at[others], list_out.at[others], list_send).wait()
     over.wait_send()
+    pltpu.make_async_copy(near_labels.at[others], near_labels.at[others], near_send).wait()
     pltpu.make_async_copy(labels.at[0, some], labels.at[0, some], y_send).wait()
     pltpu.make_async_copy(labels.at[some], labels.at[some], z_send).wait()
     most = pl.ds(0, devices - 1)
@@ -495,6 +517,8 @@
             pltpu.VMEM((8, NF), F32),
             pltpu.VMEM((subs, 8, NF), F32),
             pltpu.VMEM((subs, 8, NF), F32),
+            pltpu.VMEM((8, NF), F32),
+            pltpu.VMEM((subs, 8, NF), F32),
             pltpu.VMEM((4, blks // 4, 2 * subs, NF), BF16),
             pltpu.VMEM((devices, 3, 4, NF), BF16),
             pltpu.VMEM((2, devices // 2, 3, 4, NF), BF16),
@@ -506,6 +530,8 @@
             dma((2, 3)),
             dma((2, 3)),
             pltpu.SemaphoreType.REGULAR,
+            dma,
+            dma,
             dma,
             dma,
             dma,

time: 25.6 us -> 27 us (1.055)
  Pallas kernels: 25.4 us -> 26.8 us
    pallas_call x1, Pallas kernels: 24 us -> 25.4 us  [exchange(): pl.pallas_call(functools.partial(exchange_kernel, blks, subs), out_shape=...]
where the time goes in v9:
time: 27 us; the launch traced here: 26.9 us
  Pallas kernels  26.8 us (99%)
    pallas_call x1, Pallas kernels, exchange(): pl.pallas_call(functools.partial(exchange_kernel, blks, subs), out_shape=...  25.4 us
    pallas_call x1, Pallas kernels, finish(): pl.pallas_call(finish_kernel, out_shape=jax.ShapeDtypeStruct((count, samp...  1.44 us

profile of v9, /device:TPU:1, one launch (start us, length us, event | category | flops | bytes accessed | tf_op | source)
XLA Modules:
  0.0 26.9 jit_solution(16018146976238739117)
XLA Ops:
  0.0 0.0 copy-start
  0.0 25.4 %exchange.1.summed = bf16[384,256]{1,0:T(8,128)(2,1)S(1)} custom-call(bf16[3,128,1024]{2,1,0:T(8,128)(2,1)} %bitcast.7, bf16[3,128,1024]{2,1,0:T(8,128)(2,1)} %bitcast.8, bf16[1024,256]{1,0:T(8,128)(2,1)} %constant.4.clone.table_hbm, s32[16,128]{1,0:T(8,128)} %first_hbm.1, s32[16,128]{1,0:T(8,128)} %second_hbm.1, s32[16,128]{1,0:T(8,128)} %mask_hbm.1, ...), custom_call_target="tpu_custom_call" | custom-call | flops 2000000000 | bytes 3000000 | tf_op jit(solution)/shard_map/exchange/pallas_call | solution.py:500
  25.4 0.0 copy-done
  25.4 1.4 %finish.1 = f32[384,1024]{1,0:T(8,128)} custom-call(bf16[384,256]{1,0:T(8,128)(2,1)S(1)} %exchange.1.summed, bf16[256,1024]{1,0:T(8,128)(2,1)S(1)} %copy-done), custom_call_target="tpu_custom_call" | custom-call | flops 700000000 | bytes 3000000 | tf_op jit(solution)/shard_map/finish/pallas_call | solution.py:570
Async XLA Ops:
  0.0 25.4 %copy-start = (bf16[256,1024]{1,0:T(8,128)(2,1)S(1)}, bf16[256,1024]{1,0:T(8,128)(2,1)}, u32[]{:S(2)}) copy-start(bf16[256,1024]{1,0:T(8,128)(2,1)} %constant.5.clone.table) | copy-start | bytes 1572868

commit v10 on v8

--- a/solution.py
+++ b/solution.py
@@ -53,16 +53,7 @@
 
 
 def for_features(links):
-    high, low = in_two(links)
-    return jnp.concatenate(
-        [jnp.concatenate([high, high], axis=1), jnp.concatenate([low, low], axis=1)], axis=0
-    )
-
-
-def linked(links, values):
-    rows = links.shape[0] // 2
-    both = dot_plain(links, values)
-    return both[:rows] + both[rows:]
+    return jnp.concatenate([links.astype(BF16)] * 2, axis=1)
 
 
 def spread(rows, count, shift):
@@ -74,19 +65,13 @@
 
 def spread_weights(rows, weights, count, shift):
     index = lax.broadcasted_iota(jnp.int32, (count, NF), 0) + shift
-    parts = []
-    for part in in_two(weights):
-        wide = part.astype(F32)
-        parts.append(
-            jnp.concatenate(
-                [
-                    jnp.where(index == rows[s : s + 1], wide[s : s + 1], 0.0).astype(BF16)
-                    for s in range(rows.shape[0])
-                ],
-                axis=1,
-            )
-        )
-    return jnp.concatenate(parts, axis=0)
+    return jnp.concatenate(
+        [
+            jnp.where(index == rows[s : s + 1], weights[s : s + 1], 0.0).astype(BF16)
+            for s in range(rows.shape[0])
+        ],
+        axis=1,
+    )
 
 
 def spread_order(core):
@@ -132,6 +117,8 @@
     list_over,
     lists,
     lists_prev,
+    near_out,
+    near_labels,
     labels,
     outgoing,
     received,
@@ -143,6 +130,8 @@
     halo_send,
     halo_recv,
     joined,
+    near_send,
+    near_recv,
     y_send,
     y_recv,
     z_send,
@@ -166,8 +155,6 @@
     before = (jnp.where(sub == 0, blk_before, blk), subs_there[-1])
 
     pairs = [
-        (owner_hbm, owner),
-        (element_hbm, element),
         (first_hbm, first),
         (second_hbm, second),
         (mask_hbm, mask),
@@ -179,6 +166,8 @@
         (obs_hbm.at[1], traces.at[1, pl.ds(rows, rows)]),
         (syn_hbm.at[2], traces.at[2, pl.ds(0, rows)]),
         (obs_hbm.at[2], traces.at[2, pl.ds(rows, rows)]),
+        (owner_hbm, owner),
+        (element_hbm, element),
     ]
     loads = [
         pltpu.make_async_copy(src, dst, load_sems.at[i]) for i, (src, dst) in enumerate(pairs)
@@ -205,26 +194,7 @@
     def _():
         greet((blk_after, 0))
 
-    for i in range(2):
-        loads[i].wait()
-    lane = lax.broadcasted_iota(jnp.int32, (rows, rows), 1)
-    line = lax.broadcasted_iota(jnp.int32, (rows, rows), 0)
-    owner_row = owner[...]
-
-    def column(row):
-        return jnp.sum(jnp.where(lane == line, row, 0), axis=1, keepdims=True)
-
-    owner_column, element_column = column(owner_row), column(element[...]).astype(F32)
-    same = owner_column == owner_row
-    rank_column = jnp.sum(jnp.where(same & (lane < line), 1, 0), axis=1, keepdims=True)
-    label_rows = []
-    for k in range(2):
-        chosen = ((owner_column == lane) & (rank_column == k)).astype(F32)
-        label_rows.append(
-            jnp.sum(chosen * (element_column - rows), axis=0, keepdims=True) + float(rows)
-        )
-
-    for i in range(2, 6):
+    for i in range(4):
         loads[i].wait()
     base = (blk * blocks + lax.broadcasted_iota(jnp.int32, (blocks, NF), 0)) * BLOCK
     code = ((first[...] - base) * (2 * BLOCK) + (second[...] - base)).astype(F32)
@@ -235,7 +205,7 @@
         list_out[s] = jnp.concatenate(
             [code[i : i + 1] for i in lines]
             + [slot_weight[i : i + 1] for i in lines]
-            + label_rows,
+            + [zero_row] * 2,
             axis=0,
         )
     list_over[...] = jnp.concatenate(
@@ -272,7 +242,7 @@
         spec[2 * c] = both[:rows]
         spec[2 * c + 1] = both[rows:]
 
-    for i in range(6, 9):
+    for i in range(4, 7):
         loads[i].wait()
     transform(0)
 
@@ -300,15 +270,47 @@
     halos = [halo_copies(c) for c in range(3)]
     for copy in halos[0]:
         copy.start()
+
     for c in (1, 2):
-        loads[7 + 2 * c].wait()
-        loads[8 + 2 * c].wait()
+        loads[5 + 2 * c].wait()
+        loads[6 + 2 * c].wait()
         transform(c)
         for copy in halos[c]:
             copy.start()
 
     for there in subs_there:
         pl.semaphore_signal(joined, inc=1, device_id=(blk, there), device_id_type=MESH)
+
+    loads[11].wait()
+    loads[12].wait()
+    lane = lax.broadcasted_iota(jnp.int32, (rows, rows), 1)
+    line = lax.broadcasted_iota(jnp.int32, (rows, rows), 0)
+    owner_row = owner[...]
+
+    def column(row):
+        return jnp.sum(jnp.where(lane == line, row, 0), axis=1, keepdims=True)
+
+    owner_column, element_column = column(owner_row), column(element[...]).astype(F32)
+    same = owner_column == owner_row
+    rank_column = jnp.sum(jnp.where(same & (lane < line), 1, 0), axis=1, keepdims=True)
+    label_rows = []
+    for k in range(2):
+        chosen = ((owner_column == lane) & (rank_column == k)).astype(F32)
+        label_rows.append(
+            jnp.sum(chosen * (element_column - rows), axis=0, keepdims=True) + float(rows)
+        )
+
+    near_out[...] = jnp.concatenate(label_rows + [zero_row] * 6, axis=0)
+    near_labels[sub] = near_out[...]
+    for there in subs_there:
+        pltpu.make_async_remote_copy(
+            src_ref=near_out,
+            dst_ref=near_labels.at[sub],
+            send_sem=near_send,
+            recv_sem=near_recv,
+            device_id=(blk, there),
+            device_id_type=MESH,
+        ).start()
 
     rank_row = jnp.sum(jnp.where(same & (line < lane), 1, 0), axis=0, keepdims=True)
     target = owner_row * 4 + rank_row * 2
@@ -323,8 +325,49 @@
     others = pl.ds(0, subs - 1)
     pltpu.make_async_copy(lists.at[others], lists.at[others], list_recv).wait()
 
+    @pl.when(sub == 0)
+    def _():
+        pltpu.make_async_copy(lists_prev, lists_prev, over_recv).wait()
+
+    @pl.when(sub != 0)
+    def _():
+        lists_prev[...] = lists[...]
+
+    def unpacked(ref, k):
+        codes = ref[:, k, :].astype(jnp.int32)
+        return codes >> 7, codes & 127, ref[:, 3 + k, :]
+
+    first0, second0, weight0 = unpacked(lists_prev, 0)
+    first1, second1, weight1 = unpacked(lists, 1)
+    first2, second2, weight2 = unpacked(lists, 2)
+    to_prev = dot_rows(spread_weights(second0, weight0, BLOCK, BLOCK), spread(first0, rows, 0))
+    upper = dot_rows(spread_weights(first1, weight1, BLOCK, 0), spread(second1, rows, 0))
+    lower = dot_rows(spread_weights(first2, weight2, BLOCK, 0), spread(second2, rows, 0))
+    half = lax.broadcasted_iota(jnp.int32, (BLOCK, rows), 1) >= BLOCK
+    inside = jnp.where(half, pltpu.roll(lower, BLOCK, 1), 0.0)
+    one_way = jnp.concatenate([upper, inside], axis=0)
+    link_own = for_features(one_way + one_way.T)
+    link_halo = for_features(jnp.concatenate([to_prev, jnp.where(half, lower, 0.0)], axis=0))
+    inner = [dot_plain(link_own, own[c]) for c in range(3)]
+
+    for c in range(3):
+        for copy in halos[c]:
+            copy.wait_recv()
+        sums = inner[c] + dot_plain(link_halo, features((halo[2 * c], halo[2 * c + 1])))
+        g1r, g1i, g2r, g2i = (sums[:, i * NF : (i + 1) * NF] for i in range(4))
+        x, o = stations(c)
+        xr, xi = x[:, :NF].astype(F32), x[:, NF:].astype(F32)
+        dr, di = xr - o[:, :NF].astype(F32), xi - o[:, NF:].astype(F32)
+        real = (xr * g1r - xi * g1i) + (dr * g2r - di * g2i)
+        imag = (xr * g1i + xi * g1r) + (dr * g2i + di * g2r)
+        adjoint = jnp.concatenate([real, imag], axis=0).astype(BF16)
+        outgoing[:, c] = dot_plain(placement, adjoint).astype(BF16).reshape(devices, 4, NF)
+
     z, y = lax.div(blk, 4), lax.rem(blk, 4)
-    labels[z, y] = jnp.concatenate([lists[:, 6, :], lists[:, 7, :]], axis=0).astype(BF16)
+    pltpu.make_async_copy(near_labels.at[others], near_labels.at[others], near_recv).wait()
+    labels[z, y] = jnp.concatenate(
+        [near_labels[:, 0, :], near_labels[:, 1, :]], axis=0
+    ).astype(BF16)
     for step in range(1, 4):
         pltpu.make_async_remote_copy(
             src_ref=labels.at[z, y],
@@ -334,45 +377,6 @@
             device_id=(z * 4 + around(y, step, 4), sub),
             device_id_type=MESH,
         ).start()
-
-    @pl.when(sub == 0)
-    def _():
-        pltpu.make_async_copy(lists_prev, lists_prev, over_recv).wait()
-
-    @pl.when(sub != 0)
-    def _():
-        lists_prev[...] = lists[...]
-
-    def unpacked(ref, k):
-        codes = ref[:, k, :].astype(jnp.int32)
-        return codes >> 7, codes & 127, ref[:, 3 + k, :]
-
-    first0, second0, weight0 = unpacked(lists_prev, 0)
-    first1, second1, weight1 = unpacked(lists, 1)
-    first2, second2, weight2 = unpacked(lists, 2)
-    to_prev = dot_rows(spread_weights(second0, weight0, BLOCK, BLOCK), spread(first0, rows, 0))
-    upper = dot_rows(spread_weights(first1, weight1, BLOCK, 0), spread(second1, rows, 0))
-    lower = dot_rows(spread_weights(first2, weight2, BLOCK, 0), spread(second2, rows, 0))
-    to_prev, upper, lower = (both[:BLOCK] + both[BLOCK:] for both in (to_prev, upper, lower))
-    half = lax.broadcasted_iota(jnp.int32, (BLOCK, rows), 1) >= BLOCK
-    inside = jnp.where(half, pltpu.roll(lower, BLOCK, 1), 0.0)
-    one_way = jnp.concatenate([upper, inside], axis=0)
-    link_own = for_features(one_way + one_way.T)
-    link_halo = for_features(jnp.concatenate([to_prev, jnp.where(half, lower, 0.0)], axis=0))
-    inner = [linked(link_own, own[c]) for c in range(3)]
-
-    for c in range(3):
-        for copy in halos[c]:
-            copy.wait_recv()
-        sums = inner[c] + linked(link_halo, features((halo[2 * c], halo[2 * c + 1])))
-        g1r, g1i, g2r, g2i = (sums[:, i * NF : (i + 1) * NF] for i in range(4))
-        x, o = stations(c)
-        xr, xi = x[:, :NF].astype(F32), x[:, NF:].astype(F32)
-        dr, di = xr - o[:, :NF].astype(F32), xi - o[:, NF:].astype(F32)
-        real = (xr * g1r - xi * g1i) + (dr * g2r - di * g2i)
-        imag = (xr * g1i + xi * g1r) + (dr * g2i + di * g2r)
-        adjoint = jnp.concatenate([real, imag], axis=0).astype(BF16)
-        outgoing[:, c] = dot_plain(placement, adjoint).astype(BF16).reshape(devices, 4, NF)
 
     pl.semaphore_wait(joined, subs - 1)
 
@@ -400,7 +404,7 @@
         ).start()
 
     order = spread_order(1) + spread_order(0)[1:]
-    for step in order[:32]:
+    for step in order[:56]:
         deliver(step)
     some = pl.ds(0, 3)
     pltpu.make_async_copy(labels.at[0, some], labels.at[0, some], y_recv).wait()
@@ -414,7 +418,7 @@
             device_id_type=MESH,
         ).start()
 
-    for step in order[32:]:
+    for step in order[56:]:
         deliver(step)
 
     pltpu.make_async_copy(labels.at[some], labels.at[some], z_recv).wait()
@@ -464,6 +468,7 @@
             copy.wait_send()
     pltpu.make_async_copy(list_out.at[others], list_out.at[others], list_send).wait()
     over.wait_send()
+    pltpu.make_async_copy(near_labels.at[others], near_labels.at[others], near_send).wait()
     pltpu.make_async_copy(labels.at[0, some], labels.at[0, some], y_send).wait()
     pltpu.make_async_copy(labels.at[some], labels.at[some], z_send).wait()
     most = pl.ds(0, devices - 1)
@@ -495,6 +500,8 @@
             pltpu.VMEM((8, NF), F32),
             pltpu.VMEM((subs, 8, NF), F32),
             pltpu.VMEM((subs, 8, NF), F32),
+            pltpu.VMEM((8, NF), F32),
+            pltpu.VMEM((subs, 8, NF), F32),
             pltpu.VMEM((4, blks // 4, 2 * subs, NF), BF16),
             pltpu.VMEM((devices, 3, 4, NF), BF16),
             pltpu.VMEM((2, devices // 2, 3, 4, NF), BF16),
@@ -506,6 +513,8 @@
             dma((2, 3)),
             dma((2, 3)),
             pltpu.SemaphoreType.REGULAR,
+            dma,
+            dma,
             dma,
             dma,
             dma,

time: 25.6 us -> 27.3 us (1.066)
  Pallas kernels: 25.4 us -> 27.1 us
    pallas_call x1, Pallas kernels: 24 us -> 25.7 us  [exchange(): pl.pallas_call(functools.partial(exchange_kernel, blks, subs), out_shape=...]
where the time goes in v10:
time: 27.3 us; the launch traced here: 27.1 us
  Pallas kernels  27.1 us (99%)
    pallas_call x1, Pallas kernels, exchange(): pl.pallas_call(functools.partial(exchange_kernel, blks, subs), out_shape=...  25.7 us
    pallas_call x1, Pallas kernels, finish(): pl.pallas_call(finish_kernel, out_shape=jax.ShapeDtypeStruct((count, samp...  1.44 us

profile of v10, /device:TPU:1, one launch (start us, length us, event | category | flops | bytes accessed | tf_op | source)
XLA Modules:
  0.0 27.1 jit_solution(7825460235045300527)
XLA Ops:
  0.0 0.0 copy-start
  0.0 25.7 %exchange.1.summed = bf16[384,256]{1,0:T(8,128)(2,1)S(1)} custom-call(bf16[3,128,1024]{2,1,0:T(8,128)(2,1)} %bitcast.7, bf16[3,128,1024]{2,1,0:T(8,128)(2,1)} %bitcast.8, bf16[1024,256]{1,0:T(8,128)(2,1)} %constant.4.clone.table_hbm, s32[16,128]{1,0:T(8,128)} %first_hbm.1, s32[16,128]{1,0:T(8,128)} %second_hbm.1, s32[16,128]{1,0:T(8,128)} %mask_hbm.1, ...), custom_call_target="tpu_custom_call" | custom-call | flops 2000000000 | bytes 3000000 | tf_op jit(solution)/shard_map/exchange/pallas_call | solution.py:483
  25.7 0.0 copy-done
  25.7 1.4 %finish.1 = f32[384,1024]{1,0:T(8,128)} custom-call(bf16[384,256]{1,0:T(8,128)(2,1)S(1)} %exchange.1.summed, bf16[256,1024]{1,0:T(8,128)(2,1)S(1)} %copy-done), custom_call_target="tpu_custom_call" | custom-call | flops 700000000 | bytes 3000000 | tf_op jit(solution)/shard_map/finish/pallas_call | solution.py:553
Async XLA Ops:
  0.0 25.7 %copy-start = (bf16[256,1024]{1,0:T(8,128)(2,1)S(1)}, bf16[256,1024]{1,0:T(8,128)(2,1)}, u32[]{:S(2)}) copy-start(bf16[256,1024]{1,0:T(8,128)(2,1)} %constant.5.clone.table) | copy-start | bytes 1572868

commit v11 on v8

--- a/solution.py
+++ b/solution.py
@@ -53,16 +53,7 @@
 
 
 def for_features(links):
-    high, low = in_two(links)
-    return jnp.concatenate(
-        [jnp.concatenate([high, high], axis=1), jnp.concatenate([low, low], axis=1)], axis=0
-    )
-
-
-def linked(links, values):
-    rows = links.shape[0] // 2
-    both = dot_plain(links, values)
-    return both[:rows] + both[rows:]
+    return jnp.concatenate([links.astype(BF16)] * 2, axis=1)
 
 
 def spread(rows, count, shift):
@@ -74,19 +65,13 @@
 
 def spread_weights(rows, weights, count, shift):
     index = lax.broadcasted_iota(jnp.int32, (count, NF), 0) + shift
-    parts = []
-    for part in in_two(weights):
-        wide = part.astype(F32)
-        parts.append(
-            jnp.concatenate(
-                [
-                    jnp.where(index == rows[s : s + 1], wide[s : s + 1], 0.0).astype(BF16)
-                    for s in range(rows.shape[0])
-                ],
-                axis=1,
-            )
-        )
-    return jnp.concatenate(parts, axis=0)
+    return jnp.concatenate(
+        [
+            jnp.where(index == rows[s : s + 1], weights[s : s + 1], 0.0).astype(BF16)
+            for s in range(rows.shape[0])
+        ],
+        axis=1,
+    )
 
 
 def spread_order(core):
@@ -353,18 +338,17 @@
     to_prev = dot_rows(spread_weights(second0, weight0, BLOCK, BLOCK), spread(first0, rows, 0))
     upper = dot_rows(spread_weights(first1, weight1, BLOCK, 0), spread(second1, rows, 0))
     lower = dot_rows(spread_weights(first2, weight2, BLOCK, 0), spread(second2, rows, 0))
-    to_prev, upper, lower = (both[:BLOCK] + both[BLOCK:] for both in (to_prev, upper, lower))
     half = lax.broadcasted_iota(jnp.int32, (BLOCK, rows), 1) >= BLOCK
     inside = jnp.where(half, pltpu.roll(lower, BLOCK, 1), 0.0)
     one_way = jnp.concatenate([upper, inside], axis=0)
     link_own = for_features(one_way + one_way.T)
     link_halo = for_features(jnp.concatenate([to_prev, jnp.where(half, lower, 0.0)], axis=0))
-    inner = [linked(link_own, own[c]) for c in range(3)]
+    inner = [dot_plain(link_own, own[c]) for c in range(3)]
 
     for c in range(3):
         for copy in halos[c]:
             copy.wait_recv()
-        sums = inner[c] + linked(link_halo, features((halo[2 * c], halo[2 * c + 1])))
+        sums = inner[c] + dot_plain(link_halo, features((halo[2 * c], halo[2 * c + 1])))
         g1r, g1i, g2r, g2i = (sums[:, i * NF : (i + 1) * NF] for i in range(4))
         x, o = stations(c)
         xr, xi = x[:, :NF].astype(F32), x[:, NF:].astype(F32)
@@ -400,7 +384,7 @@
         ).start()
 
     order = spread_order(1) + spread_order(0)[1:]
-    for step in order[:32]:
+    for step in order[:48]:
         deliver(step)
     some = pl.ds(0, 3)
     pltpu.make_async_copy(labels.at[0, some], labels.at[0, some], y_recv).wait()
@@ -414,7 +398,7 @@
             device_id_type=MESH,
         ).start()
 
-    for step in order[32:]:
+    for step in order[48:]:
         deliver(step)
 
     pltpu.make_async_copy(labels.at[some], labels.at[some], z_recv).wait()

time: 25.6 us -> 25.6 us (level)
  no operation moved by 1% of the time
where the time goes in v11:
time: 25.6 us; the launch traced here: 25.4 us
  Pallas kernels  25.4 us (99%)
    pallas_call x1, Pallas kernels, exchange(): pl.pallas_call(functools.partial(exchange_kernel, blks, subs), out_shape=...  24 us
    pallas_call x1, Pallas kernels, finish(): pl.pallas_call(finish_kernel, out_shape=jax.ShapeDtypeStruct((count, samp...  1.44 us

profile of v11, /device:TPU:1, one launch (start us, length us, event | category | flops | bytes accessed | tf_op | source)
XLA Modules:
  0.0 25.4 jit_solution(8254422539422245851)
XLA Ops:
  0.0 0.0 copy-start
  0.0 24.0 %exchange.1.summed = bf16[384,256]{1,0:T(8,128)(2,1)S(1)} custom-call(bf16[3,128,1024]{2,1,0:T(8,128)(2,1)} %bitcast.7, bf16[3,128,1024]{2,1,0:T(8,128)(2,1)} %bitcast.8, bf16[1024,256]{1,0:T(8,128)(2,1)} %constant.4.clone.table_hbm, s32[16,128]{1,0:T(8,128)} %first_hbm.1, s32[16,128]{1,0:T(8,128)} %second_hbm.1, s32[16,128]{1,0:T(8,128)} %mask_hbm.1, ...), custom_call_target="tpu_custom_call" | custom-call | flops 2000000000 | bytes 3000000 | tf_op jit(solution)/shard_map/exchange/pallas_call | solution.py:462
  24.0 0.0 copy-done
  24.0 1.4 %finish.1 = f32[384,1024]{1,0:T(8,128)} custom-call(bf16[384,256]{1,0:T(8,128)(2,1)S(1)} %exchange.1.summed, bf16[256,1024]{1,0:T(8,128)(2,1)S(1)} %copy-done), custom_call_target="tpu_custom_call" | custom-call | flops 700000000 | bytes 3000000 | tf_op jit(solution)/shard_map/finish/pallas_call | solution.py:528
Async XLA Ops:
  0.0 24.0 %copy-start = (bf16[256,1024]{1,0:T(8,128)(2,1)S(1)}, bf16[256,1024]{1,0:T(8,128)(2,1)}, u32[]{:S(2)}) copy-start(bf16[256,1024]{1,0:T(8,128)(2,1)} %constant.5.clone.table) | copy-start | bytes 1572868

commit v12 on v11

--- a/solution.py
+++ b/solution.py
@@ -151,15 +151,15 @@
     before = (jnp.where(sub == 0, blk_before, blk), subs_there[-1])
 
     pairs = [
+        (table_hbm, table),
+        (syn_hbm.at[0], traces.at[0, pl.ds(0, rows)]),
+        (obs_hbm.at[0], traces.at[0, pl.ds(rows, rows)]),
         (owner_hbm, owner),
         (element_hbm, element),
         (first_hbm, first),
         (second_hbm, second),
         (mask_hbm, mask),
         (weight_hbm, weight),
-        (table_hbm, table),
-        (syn_hbm.at[0], traces.at[0, pl.ds(0, rows)]),
-        (obs_hbm.at[0], traces.at[0, pl.ds(rows, rows)]),
         (syn_hbm.at[1], traces.at[1, pl.ds(0, rows)]),
         (obs_hbm.at[1], traces.at[1, pl.ds(rows, rows)]),
         (syn_hbm.at[2], traces.at[2, pl.ds(0, rows)]),
@@ -190,76 +190,16 @@
     def _():
         greet((blk_after, 0))
 
-    for i in range(2):
-        loads[i].wait()
-    lane = lax.broadcasted_iota(jnp.int32, (rows, rows), 1)
-    line = lax.broadcasted_iota(jnp.int32, (rows, rows), 0)
-    owner_row = owner[...]
-
-    def column(row):
-        return jnp.sum(jnp.where(lane == line, row, 0), axis=1, keepdims=True)
-
-    owner_column, element_column = column(owner_row), column(element[...]).astype(F32)
-    same = owner_column == owner_row
-    rank_column = jnp.sum(jnp.where(same & (lane < line), 1, 0), axis=1, keepdims=True)
-    label_rows = []
-    for k in range(2):
-        chosen = ((owner_column == lane) & (rank_column == k)).astype(F32)
-        label_rows.append(
-            jnp.sum(chosen * (element_column - rows), axis=0, keepdims=True) + float(rows)
-        )
-
-    for i in range(2, 6):
-        loads[i].wait()
-    base = (blk * blocks + lax.broadcasted_iota(jnp.int32, (blocks, NF), 0)) * BLOCK
-    code = ((first[...] - base) * (2 * BLOCK) + (second[...] - base)).astype(F32)
-    slot_weight = weight[...] * mask[...].astype(F32)
-    zero_row = jnp.zeros((1, NF), F32)
-    for s in range(subs):
-        lines = [max(2 * s - 1, 0), 2 * s, 2 * s + 1]
-        list_out[s] = jnp.concatenate(
-            [code[i : i + 1] for i in lines]
-            + [slot_weight[i : i + 1] for i in lines]
-            + label_rows,
-            axis=0,
-        )
-    list_over[...] = jnp.concatenate(
-        [code[blocks - 1 : blocks]]
-        + [zero_row] * 2
-        + [slot_weight[blocks - 1 : blocks]]
-        + [zero_row] * 4,
-        axis=0,
-    )
-    lists[sub] = list_out[sub]
-
-    pl.semaphore_wait(barrier, subs + blks - 1)
-    for there in subs_there:
-        pltpu.make_async_remote_copy(
-            src_ref=list_out.at[there],
-            dst_ref=lists.at[sub],
-            send_sem=list_send,
-            recv_sem=list_recv,
-            device_id=(blk, there),
-            device_id_type=MESH,
-        ).start()
-    over = pltpu.make_async_remote_copy(
-        src_ref=list_over,
-        dst_ref=lists_prev.at[sub],
-        send_sem=over_send,
-        recv_sem=over_recv,
-        device_id=(blk_after, 0),
-        device_id_type=MESH,
-    )
-    over.start()
-
     def transform(c):
         both = dot_plain(traces[c], table[...]).astype(BF16)
         spec[2 * c] = both[:rows]
         spec[2 * c + 1] = both[rows:]
 
-    for i in range(6, 9):
+    for i in range(3):
         loads[i].wait()
     transform(0)
+
+    pl.semaphore_wait(barrier, subs + blks - 1)
 
     def halo_copies(c):
         q = pl.ds(2 * c, 2)
@@ -285,6 +225,68 @@
     halos = [halo_copies(c) for c in range(3)]
     for copy in halos[0]:
         copy.start()
+
+    for i in range(3, 5):
+        loads[i].wait()
+    lane = lax.broadcasted_iota(jnp.int32, (rows, rows), 1)
+    line = lax.broadcasted_iota(jnp.int32, (rows, rows), 0)
+    owner_row = owner[...]
+
+    def column(row):
+        return jnp.sum(jnp.where(lane == line, row, 0), axis=1, keepdims=True)
+
+    owner_column, element_column = column(owner_row), column(element[...]).astype(F32)
+    same = owner_column == owner_row
+    rank_column = jnp.sum(jnp.where(same & (lane < line), 1, 0), axis=1, keepdims=True)
+    label_rows = []
+    for k in range(2):
+        chosen = ((owner_column == lane) & (rank_column == k)).astype(F32)
+        label_rows.append(
+            jnp.sum(chosen * (element_column - rows), axis=0, keepdims=True) + float(rows)
+        )
+
+    for i in range(5, 9):
+        loads[i].wait()
+    base = (blk * blocks + lax.broadcasted_iota(jnp.int32, (blocks, NF), 0)) * BLOCK
+    code = ((first[...] - base) * (2 * BLOCK) + (second[...] - base)).astype(F32)
+    slot_weight = weight[...] * mask[...].astype(F32)
+    zero_row = jnp.zeros((1, NF), F32)
+    for s in range(subs):
+        lines = [max(2 * s - 1, 0), 2 * s, 2 * s + 1]
+        list_out[s] = jnp.concatenate(
+            [code[i : i + 1] for i in lines]
+            + [slot_weight[i : i + 1] for i in lines]
+            + label_rows,
+            axis=0,
+        )
+    list_over[...] = jnp.concatenate(
+        [code[blocks - 1 : blocks]]
+        + [zero_row] * 2
+        + [slot_weight[blocks - 1 : blocks]]
+        + [zero_row] * 4,
+        axis=0,
+    )
+    lists[sub] = list_out[sub]
+
+    for there in subs_there:
+        pltpu.make_async_remote_copy(
+            src_ref=list_out.at[there],
+            dst_ref=lists.at[sub],
+            send_sem=list_send,
+            recv_sem=list_recv,
+            device_id=(blk, there),
+            device_id_type=MESH,
+        ).start()
+    over = pltpu.make_async_remote_copy(
+        src_ref=list_over,
+        dst_ref=lists_prev.at[sub],
+        send_sem=over_send,
+        recv_sem=over_recv,
+        device_id=(blk_after, 0),
+        device_id_type=MESH,
+    )
+    over.start()
+
     for c in (1, 2):
         loads[7 + 2 * c].wait()
         loads[8 + 2 * c].wait()

time: 25.6 us -> 25.5 us (level)
  no operation moved by 1% of the time
where the time goes in v12:
time: 25.5 us; the launch traced here: 25.4 us
  Pallas kernels  25.3 us (99%)
    pallas_call x1, Pallas kernels, exchange(): pl.pallas_call(functools.partial(exchange_kernel, blks, subs), out_shape=...  23.9 us
    pallas_call x1, Pallas kernels, finish(): pl.pallas_call(finish_kernel, out_shape=jax.ShapeDtypeStruct((count, samp...  1.44 us

profile of v12, /device:TPU:1, one launch (start us, length us, event | category | flops | bytes accessed | tf_op | source)
XLA Modules:
  0.0 25.4 jit_solution(1415233299996000674)
XLA Ops:
  0.0 0.0 copy-start
  0.0 23.9 %exchange.1.summed = bf16[384,256]{1,0:T(8,128)(2,1)S(1)} custom-call(bf16[3,128,1024]{2,1,0:T(8,128)(2,1)} %bitcast.7, bf16[3,128,1024]{2,1,0:T(8,128)(2,1)} %bitcast.8, bf16[1024,256]{1,0:T(8,128)(2,1)} %constant.4.clone.table_hbm, s32[16,128]{1,0:T(8,128)} %first_hbm.1, s32[16,128]{1,0:T(8,128)} %second_hbm.1, s32[16,128]{1,0:T(8,128)} %mask_hbm.1, ...), custom_call_target="tpu_custom_call" | custom-call | flops 2000000000 | bytes 3000000 | tf_op jit(solution)/shard_map/exchange/pallas_call | solution.py:464
  23.9 0.0 copy-done
  23.9 1.4 %finish.1 = f32[384,1024]{1,0:T(8,128)} custom-call(bf16[384,256]{1,0:T(8,128)(2,1)S(1)} %exchange.1.summed, bf16[256,1024]{1,0:T(8,128)(2,1)S(1)} %copy-done), custom_call_target="tpu_custom_call" | custom-call | flops 700000000 | bytes 3000000 | tf_op jit(solution)/shard_map/finish/pallas_call | solution.py:530
Async XLA Ops:
  0.0 23.9 %copy-start = (bf16[256,1024]{1,0:T(8,128)(2,1)S(1)}, bf16[256,1024]{1,0:T(8,128)(2,1)}, u32[]{:S(2)}) copy-start(bf16[256,1024]{1,0:T(8,128)(2,1)} %constant.5.clone.table) | copy-start | bytes 1572868

commit v13 on v12

--- a/solution.py
+++ b/solution.py
@@ -360,6 +360,18 @@
         adjoint = jnp.concatenate([real, imag], axis=0).astype(BF16)
         outgoing[:, c] = dot_plain(placement, adjoint).astype(BF16).reshape(devices, 4, NF)
 
+    some = pl.ds(0, 3)
+    pltpu.make_async_copy(labels.at[0, some], labels.at[0, some], y_recv).wait()
+    for step in range(1, 4):
+        pltpu.make_async_remote_copy(
+            src_ref=labels.at[z],
+            dst_ref=labels.at[z],
+            send_sem=z_send,
+            recv_sem=z_recv,
+            device_id=(around(z, step, 4) * 4 + y, sub),
+            device_id_type=MESH,
+        ).start()
+
     pl.semaphore_wait(joined, subs - 1)
 
     core = lax.rem(sub, 2)
@@ -385,22 +397,7 @@
             device_id_type=MESH,
         ).start()
 
-    order = spread_order(1) + spread_order(0)[1:]
-    for step in order[:48]:
-        deliver(step)
-    some = pl.ds(0, 3)
-    pltpu.make_async_copy(labels.at[0, some], labels.at[0, some], y_recv).wait()
-    for step in range(1, 4):
-        pltpu.make_async_remote_copy(
-            src_ref=labels.at[z],
-            dst_ref=labels.at[z],
-            send_sem=z_send,
-            recv_sem=z_recv,
-            device_id=(around(z, step, 4) * 4 + y, sub),
-            device_id_type=MESH,
-        ).start()
-
-    for step in order[48:]:
+    for step in spread_order(1) + spread_order(0)[1:]:
         deliver(step)
 
     pltpu.make_async_copy(labels.at[some], labels.at[some], z_recv).wait()

time: 25.5 us -> 26.2 us (1.027)
  Pallas kernels: 25.3 us -> 26 us
    pallas_call x1, Pallas kernels: 23.9 us -> 24.6 us  [exchange(): pl.pallas_call(functools.partial(exchange_kernel, blks, subs), out_shape=...]
where the time goes in v13:
time: 26.2 us; the launch traced here: 26.1 us
  Pallas kernels  26 us (99%)
    pallas_call x1, Pallas kernels, exchange(): pl.pallas_call(functools.partial(exchange_kernel, blks, subs), out_shape=...  24.6 us
    pallas_call x1, Pallas kernels, finish(): pl.pallas_call(finish_kernel, out_shape=jax.ShapeDtypeStruct((count, samp...  1.44 us

profile of v13, /device:TPU:1, one launch (start us, length us, event | category | flops | bytes accessed | tf_op | source)
XLA Modules:
  0.0 26.1 jit_solution(8790282905547041663)
XLA Ops:
  0.0 0.0 copy-start
  0.0 24.6 %exchange.1.summed = bf16[384,256]{1,0:T(8,128)(2,1)S(1)} custom-call(bf16[3,128,1024]{2,1,0:T(8,128)(2,1)} %bitcast.7, bf16[3,128,1024]{2,1,0:T(8,128)(2,1)} %bitcast.8, bf16[1024,256]{1,0:T(8,128)(2,1)} %constant.4.clone.table_hbm, s32[16,128]{1,0:T(8,128)} %first_hbm.1, s32[16,128]{1,0:T(8,128)} %second_hbm.1, s32[16,128]{1,0:T(8,128)} %mask_hbm.1, ...), custom_call_target="tpu_custom_call" | custom-call | flops 2000000000 | bytes 3000000 | tf_op jit(solution)/shard_map/exchange/pallas_call | solution.py:461
  24.6 0.0 copy-done
  24.6 1.4 %finish.1 = f32[384,1024]{1,0:T(8,128)} custom-call(bf16[384,256]{1,0:T(8,128)(2,1)S(1)} %exchange.1.summed, bf16[256,1024]{1,0:T(8,128)(2,1)S(1)} %copy-done), custom_call_target="tpu_custom_call" | custom-call | flops 700000000 | bytes 3000000 | tf_op jit(solution)/shard_map/finish/pallas_call | solution.py:527
Async XLA Ops:
  0.0 24.6 %copy-start = (bf16[256,1024]{1,0:T(8,128)(2,1)S(1)}, bf16[256,1024]{1,0:T(8,128)(2,1)}, u32[]{:S(2)}) copy-start(bf16[256,1024]{1,0:T(8,128)(2,1)} %constant.5.clone.table) | copy-start | bytes 1572868

commit v14 on v12

--- a/solution.py
+++ b/solution.py
@@ -1,5 +1,4 @@
 import functools
-import itertools
 import math
 
 import jax
@@ -72,22 +71,6 @@
         ],
         axis=1,
     )
-
-
-def spread_order(core):
-    left = [step + (core,) for step in itertools.product(range(4), range(4), range(4))]
-    ways = {0: (0.0, 0.0), 1: (1.0, 0.0), 2: (1.0, 1.0), 3: (0.0, 1.0)}
-
-    def links(step):
-        return np.array([way for axis in step[:3] for way in ways[axis]])
-
-    used, order = np.zeros(6), []
-    while left:
-        step = min(left, key=lambda t: (np.max(used + links(t)), -np.sum(links(t)), t))
-        left.remove(step)
-        used = used + links(step)
-        order.append(step)
-    return order
 
 
 def exchange_kernel(
@@ -362,20 +345,17 @@
 
     pl.semaphore_wait(joined, subs - 1)
 
-    core = lax.rem(sub, 2)
-
-    def turns(at, size):
-        up = [around(at, step, size) for step in range(1, size)]
-        return [at] + [jnp.where(core == 0, up[i], up[-1 - i]) for i in range(size - 1)]
-
-    chip = lax.div(me, 2)
-    z_to, y_to, x_to = turns(z, 4), turns(y, 4), turns(lax.div(sub, 2), 4)
-    core_to = [core, 1 - core]
+    core, chip, x = lax.rem(sub, 2), lax.div(me, 2), lax.div(sub, 2)
     received[core, chip] = outgoing[me]
 
-    def deliver(step):
-        dz, dy, dx, other = step
-        blk_to, sub_to = z_to[dz] * 4 + y_to[dy], x_to[dx] * 2 + core_to[other]
+    def stepped(at, step):
+        step = jnp.where(step >= 4, step - 4, step)
+        step = jnp.where((core == 1) & (step > 0), 4 - step, step)
+        return around(at, step, 4)
+
+    def deliver(a, b, j, other):
+        blk_to = stepped(z, j) * 4 + stepped(y, a + j)
+        sub_to = stepped(x, b + j) * 2 + (1 - core if other else core)
         pltpu.make_async_remote_copy(
             src_ref=outgoing.at[blk_to * subs + sub_to],
             dst_ref=received.at[core, chip],
@@ -385,9 +365,12 @@
             device_id_type=MESH,
         ).start()
 
-    order = spread_order(1) + spread_order(0)[1:]
-    for step in order[:48]:
-        deliver(step)
+    def turn(other, i, carry):
+        for j in (2, 1, 3, 0):
+            deliver(lax.div(i, 4), lax.rem(i, 4), j, other)
+        return carry
+
+    lax.fori_loop(0, blks, functools.partial(turn, 1), 0)
     some = pl.ds(0, 3)
     pltpu.make_async_copy(labels.at[0, some], labels.at[0, some], y_recv).wait()
     for step in range(1, 4):
@@ -400,8 +383,9 @@
             device_id_type=MESH,
         ).start()
 
-    for step in order[48:]:
-        deliver(step)
+    for j in (2, 1, 3):
+        deliver(0, 0, j, 0)
+    lax.fori_loop(1, blks, functools.partial(turn, 0), 0)
 
     pltpu.make_async_copy(labels.at[some], labels.at[some], z_recv).wait()
     by_owner = labels[...].reshape(2 * devices, NF)

time: 25.5 us -> 25.6 us (level)
  no operation moved by 1% of the time
where the time goes in v14:
time: 25.6 us; the launch traced here: 25.5 us
  Pallas kernels  25.5 us (100%)
    pallas_call x1, Pallas kernels, exchange(): pl.pallas_call(functools.partial(exchange_kernel, blks, subs), out_shape=...  24 us
    pallas_call x1, Pallas kernels, finish(): pl.pallas_call(finish_kernel, out_shape=jax.ShapeDtypeStruct((count, samp...  1.44 us

profile of v14, /device:TPU:1, one launch (start us, length us, event | category | flops | bytes accessed | tf_op | source)
XLA Modules:
  0.0 25.5 jit_solution(12749199616904294243)
XLA Ops:
  0.0 0.0 copy-start
  0.0 24.0 %exchange.1.summed = bf16[384,256]{1,0:T(8,128)(2,1)S(1)} custom-call(bf16[3,128,1024]{2,1,0:T(8,128)(2,1)} %bitcast.7, bf16[3,128,1024]{2,1,0:T(8,128)(2,1)} %bitcast.8, bf16[1024,256]{1,0:T(8,128)(2,1)} %constant.4.clone.table_hbm, s32[16,128]{1,0:T(8,128)} %first_hbm.1, s32[16,128]{1,0:T(8,128)} %second_hbm.1, s32[16,128]{1,0:T(8,128)} %mask_hbm.1, ...), custom_call_target="tpu_custom_call" | custom-call | flops 2000000000 | bytes 3000000 | tf_op jit(solution)/shard_map/exchange/pallas_call | solution.py:448
  24.0 0.0 copy-done
  24.0 1.4 %finish.1 = f32[384,1024]{1,0:T(8,128)} custom-call(bf16[384,256]{1,0:T(8,128)(2,1)S(1)} %exchange.1.summed, bf16[256,1024]{1,0:T(8,128)(2,1)S(1)} %copy-done), custom_call_target="tpu_custom_call" | custom-call | flops 700000000 | bytes 3000000 | tf_op jit(solution)/shard_map/finish/pallas_call | solution.py:514
Async XLA Ops:
  0.0 24.0 %copy-start = (bf16[256,1024]{1,0:T(8,128)(2,1)S(1)}, bf16[256,1024]{1,0:T(8,128)(2,1)}, u32[]{:S(2)}) copy-start(bf16[256,1024]{1,0:T(8,128)(2,1)} %constant.5.clone.table) | copy-start | bytes 1572868

commit v15 on v12

--- a/solution.py
+++ b/solution.py
@@ -74,8 +74,8 @@
     )
 
 
-def spread_order(core):
-    left = [step + (core,) for step in itertools.product(range(4), range(4), range(4))]
+def spread_order():
+    left = list(itertools.product(range(4), range(4), range(4), range(2)))[1:]
     ways = {0: (0.0, 0.0), 1: (1.0, 0.0), 2: (1.0, 1.0), 3: (0.0, 1.0)}
 
     def links(step):
@@ -83,7 +83,7 @@
 
     used, order = np.zeros(6), []
     while left:
-        step = min(left, key=lambda t: (np.max(used + links(t)), -np.sum(links(t)), t))
+        step = min(left, key=lambda t: (-np.sum(links(t)), np.max(used + links(t)), t))
         left.remove(step)
         used = used + links(step)
         order.append(step)
@@ -385,7 +385,7 @@
             device_id_type=MESH,
         ).start()
 
-    order = spread_order(1) + spread_order(0)[1:]
+    order = spread_order()
     for step in order[:48]:
         deliver(step)
     some = pl.ds(0, 3)

time: 25.5 us -> 25.6 us (level)
  no operation moved by 1% of the time
where the time goes in v15:
time: 25.6 us; the launch traced here: 25.5 us
  Pallas kernels  25.5 us (100%)
    pallas_call x1, Pallas kernels, exchange(): pl.pallas_call(functools.partial(exchange_kernel, blks, subs), out_shape=...  24 us
    pallas_call x1, Pallas kernels, finish(): pl.pallas_call(finish_kernel, out_shape=jax.ShapeDtypeStruct((count, samp...  1.44 us

profile of v15, /device:TPU:1, one launch (start us, length us, event | category | flops | bytes accessed | tf_op | source)
XLA Modules:
  0.0 25.5 jit_solution(7923229120873692947)
XLA Ops:
  0.0 0.0 copy-start
  0.0 24.0 %exchange.1.summed = bf16[384,256]{1,0:T(8,128)(2,1)S(1)} custom-call(bf16[3,128,1024]{2,1,0:T(8,128)(2,1)} %bitcast.7, bf16[3,128,1024]{2,1,0:T(8,128)(2,1)} %bitcast.8, bf16[1024,256]{1,0:T(8,128)(2,1)} %constant.4.clone.table_hbm, s32[16,128]{1,0:T(8,128)} %first_hbm.1, s32[16,128]{1,0:T(8,128)} %second_hbm.1, s32[16,128]{1,0:T(8,128)} %mask_hbm.1, ...), custom_call_target="tpu_custom_call" | custom-call | flops 2000000000 | bytes 3000000 | tf_op jit(solution)/shard_map/exchange/pallas_call | solution.py:464
  24.1 0.0 copy-done
  24.1 1.4 %finish.1 = f32[384,1024]{1,0:T(8,128)} custom-call(bf16[384,256]{1,0:T(8,128)(2,1)S(1)} %exchange.1.summed, bf16[256,1024]{1,0:T(8,128)(2,1)S(1)} %copy-done), custom_call_target="tpu_custom_call" | custom-call | flops 700000000 | bytes 3000000 | tf_op jit(solution)/shard_map/finish/pallas_call | solution.py:530
Async XLA Ops:
  0.0 24.1 %copy-start = (bf16[256,1024]{1,0:T(8,128)(2,1)S(1)}, bf16[256,1024]{1,0:T(8,128)(2,1)}, u32[]{:S(2)}) copy-start(bf16[256,1024]{1,0:T(8,128)(2,1)} %constant.5.clone.table) | copy-start | bytes 1572868

commit v16 on v15

--- a/solution.py
+++ b/solution.py
@@ -77,13 +77,23 @@
 def spread_order():
     left = list(itertools.product(range(4), range(4), range(4), range(2)))[1:]
     ways = {0: (0.0, 0.0), 1: (1.0, 0.0), 2: (1.0, 1.0), 3: (0.0, 1.0)}
+    entered = ((0.0, 1.1, 2.0, 2.5), (0.0, 0.65, 1.1, 1.5), (0.0, 0.8, 1.2, 1.25))
 
     def links(step):
         return np.array([way for axis in step[:3] for way in ways[axis]])
 
+    def lead(step):
+        return sum(
+            max(at[source] - at[(source + by) % 4] for source in range(4))
+            for at, by in zip(entered, step)
+        )
+
     used, order = np.zeros(6), []
     while left:
-        step = min(left, key=lambda t: (-np.sum(links(t)), np.max(used + links(t)), t))
+        if len(order) % 2 == 0:
+            step = max(left, key=lambda t: (lead(t), t))
+        else:
+            step = min(left, key=lambda t: (np.max(used + links(t)), -lead(t), t))
         left.remove(step)
         used = used + links(step)
         order.append(step)
@@ -362,13 +372,10 @@
 
     pl.semaphore_wait(joined, subs - 1)
 
-    core = lax.rem(sub, 2)
-
     def turns(at, size):
-        up = [around(at, step, size) for step in range(1, size)]
-        return [at] + [jnp.where(core == 0, up[i], up[-1 - i]) for i in range(size - 1)]
-
-    chip = lax.div(me, 2)
+        return [at] + [around(at, step, size) for step in range(1, size)]
+
+    core, chip = lax.rem(sub, 2), lax.div(me, 2)
     z_to, y_to, x_to = turns(z, 4), turns(y, 4), turns(lax.div(sub, 2), 4)
     core_to = [core, 1 - core]
     received[core, chip] = outgoing[me]

time: 25.6 us -> 25.6 us (level)
  no operation moved by 1% of the time
where the time goes in v16:
time: 25.6 us; the launch traced here: 25.5 us
  Pallas kernels  25.5 us (100%)
    pallas_call x1, Pallas kernels, exchange(): pl.pallas_call(functools.partial(exchange_kernel, blks, subs), out_shape=...  24.1 us
    pallas_call x1, Pallas kernels, finish(): pl.pallas_call(finish_kernel, out_shape=jax.ShapeDtypeStruct((count, samp...  1.44 us

profile of v16, /device:TPU:1, one launch (start us, length us, event | category | flops | bytes accessed | tf_op | source)
XLA Modules:
  0.0 25.5 jit_solution(421500883494524203)
XLA Ops:
  0.0 0.0 copy-start
  0.0 24.1 %exchange.1.summed = bf16[384,256]{1,0:T(8,128)(2,1)S(1)} custom-call(bf16[3,128,1024]{2,1,0:T(8,128)(2,1)} %bitcast.7, bf16[3,128,1024]{2,1,0:T(8,128)(2,1)} %bitcast.8, bf16[1024,256]{1,0:T(8,128)(2,1)} %constant.4.clone.table_hbm, s32[16,128]{1,0:T(8,128)} %first_hbm.1, s32[16,128]{1,0:T(8,128)} %second_hbm.1, s32[16,128]{1,0:T(8,128)} %mask_hbm.1, ...), custom_call_target="tpu_custom_call" | custom-call | flops 2000000000 | bytes 3000000 | tf_op jit(solution)/shard_map/exchange/pallas_call | solution.py:471
  24.1 0.0 copy-done
  24.1 1.4 %finish.1 = f32[384,1024]{1,0:T(8,128)} custom-call(bf16[384,256]{1,0:T(8,128)(2,1)S(1)} %exchange.1.summed, bf16[256,1024]{1,0:T(8,128)(2,1)S(1)} %copy-done), custom_call_target="tpu_custom_call" | custom-call | flops 700000000 | bytes 3000000 | tf_op jit(solution)/shard_map/finish/pallas_call | solution.py:537
Async XLA Ops:
  0.0 24.1 %copy-start = (bf16[256,1024]{1,0:T(8,128)(2,1)S(1)}, bf16[256,1024]{1,0:T(8,128)(2,1)}, u32[]{:S(2)}) copy-start(bf16[256,1024]{1,0:T(8,128)(2,1)} %constant.5.clone.table) | copy-start | bytes 1572868

commit v17 on v12

--- a/solution.py
+++ b/solution.py
@@ -347,9 +347,7 @@
     link_halo = for_features(jnp.concatenate([to_prev, jnp.where(half, lower, 0.0)], axis=0))
     inner = [dot_plain(link_own, own[c]) for c in range(3)]
 
-    for c in range(3):
-        for copy in halos[c]:
-            copy.wait_recv()
+    def adjoint(c):
         sums = inner[c] + dot_plain(link_halo, features((halo[2 * c], halo[2 * c + 1])))
         g1r, g1i, g2r, g2i = (sums[:, i * NF : (i + 1) * NF] for i in range(4))
         x, o = stations(c)
@@ -357,8 +355,17 @@
         dr, di = xr - o[:, :NF].astype(F32), xi - o[:, NF:].astype(F32)
         real = (xr * g1r - xi * g1i) + (dr * g2r - di * g2i)
         imag = (xr * g1i + xi * g1r) + (dr * g2i + di * g2r)
-        adjoint = jnp.concatenate([real, imag], axis=0).astype(BF16)
-        outgoing[:, c] = dot_plain(placement, adjoint).astype(BF16).reshape(devices, 4, NF)
+        return jnp.concatenate([real, imag], axis=0).astype(BF16)
+
+    for together in ((0, 1), (2,)):
+        for c in together:
+            for copy in halos[c]:
+                copy.wait_recv()
+        placed = dot_plain(placement, jnp.concatenate([adjoint(c) for c in together], axis=1))
+        for i, c in enumerate(together):
+            outgoing[:, c] = (
+                placed[:, i * NF : (i + 1) * NF].astype(BF16).reshape(devices, 4, NF)
+            )
 
     pl.semaphore_wait(joined, subs - 1)
 
@@ -433,17 +440,18 @@
 
     collect_other, collect_same = collector(1 - core), collector(core)
 
-    def sums(collect, source_core, c):
-        return dot_plain(collect, received[source_core, :, c].reshape(2 * devices, NF))
+    def sums(collect, source_core):
+        values = [received[source_core, :, c].reshape(2 * devices, NF) for c in range(3)]
+        return dot_plain(collect, jnp.concatenate(values, axis=1))
 
     pltpu.make_async_copy(received.at[0], received.at[0], all_recv.at[1]).wait()
-    first_sums = [sums(collect_other, 1 - core, c) for c in range(3)]
+    first_sums = sums(collect_other, 1 - core)
     most = pl.ds(0, devices // 2 - 1)
     pltpu.make_async_copy(received.at[0, most], received.at[0, most], all_recv.at[0]).wait()
+    total = (first_sums + sums(collect_same, core)).astype(BF16)
     for c in range(3):
-        total = (first_sums[c] + sums(collect_same, core, c)).astype(BF16)
-        summed[c * rows : (c + 1) * rows, :NF] = total[:rows]
-        summed[c * rows : (c + 1) * rows, NF:] = total[rows:]
+        summed[c * rows : (c + 1) * rows, :NF] = total[:rows, c * NF : (c + 1) * NF]
+        summed[c * rows : (c + 1) * rows, NF:] = total[rows:, c * NF : (c + 1) * NF]
 
     for c in range(3):
         for copy in halos[c]:

time: 25.5 us -> 25.2 us (0.988)
  Pallas kernels: 25.3 us -> 25 us
    pallas_call x1, Pallas kernels: 23.9 us -> 23.6 us  [exchange(): pl.pallas_call(functools.partial(exchange_kernel, blks, subs), out_shape=...]
where the time goes in v17:
time: 25.2 us; the launch traced here: 25.1 us
  Pallas kernels  25 us (99%)
    pallas_call x1, Pallas kernels, exchange(): pl.pallas_call(functools.partial(exchange_kernel, blks, subs), out_shape=...  23.6 us
    pallas_call x1, Pallas kernels, finish(): pl.pallas_call(finish_kernel, out_shape=jax.ShapeDtypeStruct((count, samp...  1.44 us

profile of v17, /device:TPU:1, one launch (start us, length us, event | category | flops | bytes accessed | tf_op | source)
XLA Modules:
  0.0 25.1 jit_solution(3884254408882275129)
XLA Ops:
  0.0 0.0 copy-start
  0.0 23.6 %exchange.1.summed = bf16[384,256]{1,0:T(8,128)(2,1)S(1)} custom-call(bf16[3,128,1024]{2,1,0:T(8,128)(2,1)} %bitcast.7, bf16[3,128,1024]{2,1,0:T(8,128)(2,1)} %bitcast.8, bf16[1024,256]{1,0:T(8,128)(2,1)} %constant.4.clone.table_hbm, s32[16,128]{1,0:T(8,128)} %first_hbm.1, s32[16,128]{1,0:T(8,128)} %second_hbm.1, s32[16,128]{1,0:T(8,128)} %mask_hbm.1, ...), custom_call_target="tpu_custom_call" | custom-call | flops 2000000000 | bytes 3000000 | tf_op jit(solution)/shard_map/exchange/pallas_call | solution.py:472
  23.6 0.0 copy-done
  23.6 1.4 %finish.1 = f32[384,1024]{1,0:T(8,128)} custom-call(bf16[384,256]{1,0:T(8,128)(2,1)S(1)} %exchange.1.summed, bf16[256,1024]{1,0:T(8,128)(2,1)S(1)} %copy-done), custom_call_target="tpu_custom_call" | custom-call | flops 700000000 | bytes 3000000 | tf_op jit(solution)/shard_map/finish/pallas_call | solution.py:538
Async XLA Ops:
  0.0 23.6 %copy-start = (bf16[256,1024]{1,0:T(8,128)(2,1)S(1)}, bf16[256,1024]{1,0:T(8,128)(2,1)}, u32[]{:S(2)}) copy-start(bf16[256,1024]{1,0:T(8,128)(2,1)} %constant.5.clone.table) | copy-start | bytes 1572868

commit v18 on v17

--- a/solution.py
+++ b/solution.py
@@ -74,14 +74,14 @@
     )
 
 
-def spread_order(core):
-    left = [step + (core,) for step in itertools.product(range(4), range(4), range(4))]
+def spread_order():
+    left = list(itertools.product(range(4), range(4), range(2)))[1:]
     ways = {0: (0.0, 0.0), 1: (1.0, 0.0), 2: (1.0, 1.0), 3: (0.0, 1.0)}
 
     def links(step):
-        return np.array([way for axis in step[:3] for way in ways[axis]])
-
-    used, order = np.zeros(6), []
+        return np.array([way for axis in step[:2] for way in ways[axis]])
+
+    used, order = np.zeros(4), []
     while left:
         step = min(left, key=lambda t: (np.max(used + links(t)), -np.sum(links(t)), t))
         left.remove(step)
@@ -127,6 +127,7 @@
     over_recv,
     halo_send,
     halo_recv,
+    entered,
     joined,
     y_send,
     y_recv,
@@ -171,24 +172,39 @@
     for load in loads:
         load.start()
 
+    z, y = lax.div(blk, 4), lax.rem(blk, 4)
+    has_before, has_after = me > 0, me < devices - 1
+    row_before, row_after = blk > 0, blk < blks - 1
     barrier = pltpu.get_barrier_semaphore()
 
     def greet(there):
         pl.semaphore_signal(barrier, inc=1, device_id=there, device_id_type=MESH)
 
+    def greet_column(there, carry):
+        greet((there, sub))
+        return carry
+
     for there in subs_there:
         greet((blk, there))
-    for there in blks_there:
-        greet((there, sub))
-
-    @pl.when(sub == 0)
-    def _():
-        for s in range(1, subs):
+    lax.fori_loop(blk + 1, blks, greet_column, 0)
+
+    @pl.when((sub == 0) & row_before)
+    def _():
+        for s in range(subs):
             greet((blk_before, s))
 
-    @pl.when(sub == subs - 1)
+    @pl.when((sub == subs - 1) & row_after)
     def _():
         greet((blk_after, 0))
+
+    for i in range(3):
+        pl.semaphore_signal(entered.at[i], inc=1)
+    greetings = (
+        (subs - 1)
+        + jnp.where(row_after, 1, 0)
+        + jnp.where((sub == 0) & row_before, 1, 0)
+        + blk
+    )
 
     def transform(c):
         both = dot_plain(traces[c], table[...]).astype(BF16)
@@ -199,7 +215,7 @@
         loads[i].wait()
     transform(0)
 
-    pl.semaphore_wait(barrier, subs + blks - 1)
+    pl.semaphore_wait(barrier, greetings)
 
     def halo_copies(c):
         q = pl.ds(2 * c, 2)
@@ -223,8 +239,17 @@
         ]
 
     halos = [halo_copies(c) for c in range(3)]
-    for copy in halos[0]:
-        copy.start()
+
+    def start_halos(c):
+        @pl.when(has_before)
+        def _():
+            halos[c][0].start()
+
+        @pl.when(has_after)
+        def _():
+            halos[c][1].start()
+
+    start_halos(0)
 
     for i in range(3, 5):
         loads[i].wait()
@@ -285,17 +310,44 @@
         device_id=(blk_after, 0),
         device_id_type=MESH,
     )
-    over.start()
+
+    @pl.when(row_after)
+    def _():
+        over.start()
+
 
     for c in (1, 2):
         loads[7 + 2 * c].wait()
         loads[8 + 2 * c].wait()
         transform(c)
-        for copy in halos[c]:
-            copy.start()
-
-    for there in subs_there:
-        pl.semaphore_signal(joined, inc=1, device_id=(blk, there), device_id_type=MESH)
+        start_halos(c)
+
+    @pl.when(jnp.logical_not(has_before))
+    def _():
+        halo[:, :BLOCK] = jnp.zeros((6, BLOCK, 2 * NF), BF16)
+
+    @pl.when(jnp.logical_not(has_after))
+    def _():
+        halo[:, BLOCK:] = jnp.zeros((6, BLOCK, 2 * NF), BF16)
+
+    def answer(there, carry):
+        kind = jnp.where(lax.div(there, 4) == z, 0, jnp.where(z == 1, 1, 2))
+        pl.semaphore_signal(
+            entered.at[kind], inc=1, device_id=(there, sub), device_id_type=MESH
+        )
+        return carry
+
+    lax.fori_loop(0, blk, answer, 0)
+
+    def tell_row(which):
+        for there in subs_there:
+            pl.semaphore_signal(
+                joined.at[which], inc=1, device_id=(blk, there), device_id_type=MESH
+            )
+
+    @pl.when(z >= 2)
+    def _():
+        tell_row(0)
 
     rank_row = jnp.sum(jnp.where(same & (line < lane), 1, 0), axis=0, keepdims=True)
     target = owner_row * 4 + rank_row * 2
@@ -310,21 +362,13 @@
     others = pl.ds(0, subs - 1)
     pltpu.make_async_copy(lists.at[others], lists.at[others], list_recv).wait()
 
-    z, y = lax.div(blk, 4), lax.rem(blk, 4)
-    labels[z, y] = jnp.concatenate([lists[:, 6, :], lists[:, 7, :]], axis=0).astype(BF16)
-    for step in range(1, 4):
-        pltpu.make_async_remote_copy(
-            src_ref=labels.at[z, y],
-            dst_ref=labels.at[z, y],
-            send_sem=y_send,
-            recv_sem=y_recv,
-            device_id=(z * 4 + around(y, step, 4), sub),
-            device_id_type=MESH,
-        ).start()
-
-    @pl.when(sub == 0)
+    @pl.when((sub == 0) & row_before)
     def _():
         pltpu.make_async_copy(lists_prev, lists_prev, over_recv).wait()
+
+    @pl.when((sub == 0) & jnp.logical_not(row_before))
+    def _():
+        lists_prev[...] = jnp.zeros(lists_prev.shape, F32)
 
     @pl.when(sub != 0)
     def _():
@@ -357,32 +401,59 @@
         imag = (xr * g1i + xi * g1r) + (dr * g2i + di * g2r)
         return jnp.concatenate([real, imag], axis=0).astype(BF16)
 
-    for together in ((0, 1), (2,)):
+    def handle(together):
         for c in together:
-            for copy in halos[c]:
-                copy.wait_recv()
+
+            @pl.when(has_after)
+            def _():
+                halos[c][0].wait_recv()
+
+            @pl.when(has_before)
+            def _():
+                halos[c][1].wait_recv()
+
         placed = dot_plain(placement, jnp.concatenate([adjoint(c) for c in together], axis=1))
         for i, c in enumerate(together):
             outgoing[:, c] = (
                 placed[:, i * NF : (i + 1) * NF].astype(BF16).reshape(devices, 4, NF)
             )
 
-    pl.semaphore_wait(joined, subs - 1)
-
-    core = lax.rem(sub, 2)
+    handle((0, 1))
+
+    pl.semaphore_wait(entered.at[0], 4 - y)
+    labels[z, y] = jnp.concatenate([lists[:, 6, :], lists[:, 7, :]], axis=0).astype(BF16)
+    for step in range(1, 4):
+        pltpu.make_async_remote_copy(
+            src_ref=labels.at[z, y],
+            dst_ref=labels.at[z, y],
+            send_sem=y_send,
+            recv_sem=y_recv,
+            device_id=(z * 4 + around(y, step, 4), sub),
+            device_id_type=MESH,
+        ).start()
+
+    pl.semaphore_wait(entered.at[1], 1 + jnp.where(z == 0, 4, 0))
+
+    @pl.when(z < 2)
+    def _():
+        tell_row(0)
+
+    handle((2,))
+
+    pl.semaphore_wait(entered.at[2], 1 + jnp.where(z < 2, 8, jnp.where(z == 2, 4, 0)))
+    tell_row(1)
 
     def turns(at, size):
-        up = [around(at, step, size) for step in range(1, size)]
-        return [at] + [jnp.where(core == 0, up[i], up[-1 - i]) for i in range(size - 1)]
-
-    chip = lax.div(me, 2)
-    z_to, y_to, x_to = turns(z, 4), turns(y, 4), turns(lax.div(sub, 2), 4)
+        return [at] + [around(at, step, size) for step in range(1, size)]
+
+    core, chip = lax.rem(sub, 2), lax.div(me, 2)
+    y_to, x_to = turns(y, 4), turns(lax.div(sub, 2), 4)
     core_to = [core, 1 - core]
     received[core, chip] = outgoing[me]
 
-    def deliver(step):
-        dz, dy, dx, other = step
-        blk_to, sub_to = z_to[dz] * 4 + y_to[dy], x_to[dx] * 2 + core_to[other]
+    def deliver(plane, step):
+        dy, dx, other = step
+        blk_to, sub_to = plane * 4 + y_to[dy], x_to[dx] * 2 + core_to[other]
         pltpu.make_async_remote_copy(
             src_ref=outgoing.at[blk_to * subs + sub_to],
             dst_ref=received.at[core, chip],
@@ -392,9 +463,16 @@
             device_id_type=MESH,
         ).start()
 
-    order = spread_order(1) + spread_order(0)[1:]
-    for step in order[:48]:
-        deliver(step)
+    def deliver_plane(plane):
+        for step in spread_order():
+            deliver(plane, step)
+
+        @pl.when(z != plane)
+        def _():
+            deliver(plane, (0, 0, 0))
+
+    pl.semaphore_wait(joined.at[0], subs - 1)
+    deliver_plane(0)
     some = pl.ds(0, 3)
     pltpu.make_async_copy(labels.at[0, some], labels.at[0, some], y_recv).wait()
     for step in range(1, 4):
@@ -407,8 +485,10 @@
             device_id_type=MESH,
         ).start()
 
-    for step in order[48:]:
-        deliver(step)
+    deliver_plane(1)
+    pl.semaphore_wait(joined.at[1], subs - 1)
+    deliver_plane(2)
+    deliver_plane(3)
 
     pltpu.make_async_copy(labels.at[some], labels.at[some], z_recv).wait()
     by_owner = labels[...].reshape(2 * devices, NF)
@@ -454,10 +534,21 @@
         summed[c * rows : (c + 1) * rows, NF:] = total[rows:, c * NF : (c + 1) * NF]
 
     for c in range(3):
-        for copy in halos[c]:
-            copy.wait_send()
+
+        @pl.when(has_before)
+        def _():
+            halos[c][0].wait_send()
+
+        @pl.when(has_after)
+        def _():
+            halos[c][1].wait_send()
+
     pltpu.make_async_copy(list_out.at[others], list_out.at[others], list_send).wait()
-    over.wait_send()
+
+    @pl.when(row_after)
+    def _():
+        over.wait_send()
+
     pltpu.make_async_copy(labels.at[0, some], labels.at[0, some], y_send).wait()
     pltpu.make_async_copy(labels.at[some], labels.at[some], z_send).wait()
     most = pl.ds(0, devices - 1)
@@ -499,7 +590,8 @@
             dma,
             dma((2, 3)),
             dma((2, 3)),
-            pltpu.SemaphoreType.REGULAR,
+            pltpu.SemaphoreType.REGULAR((3,)),
+            pltpu.SemaphoreType.REGULAR((2,)),
             dma,
             dma,
             dma,

time: 25.2 us -> 24 us (0.952)
  Pallas kernels: 25 us -> 23.9 us
    pallas_call x1, Pallas kernels: 23.6 us -> 22.4 us  [exchange(): pl.pallas_call(functools.partial(exchange_kernel, blks, subs), out_shape=...]
where the time goes in v18:
time: 24 us; the launch traced here: 23.9 us
  Pallas kernels  23.9 us (100%)
    pallas_call x1, Pallas kernels, exchange(): pl.pallas_call(functools.partial(exchange_kernel, blks, subs), out_shape=...  22.4 us
    pallas_call x1, Pallas kernels, finish(): pl.pallas_call(finish_kernel, out_shape=jax.ShapeDtypeStruct((count, samp...  1.44 us

profile of v18, /device:TPU:1, one launch (start us, length us, event | category | flops | bytes accessed | tf_op | source)
XLA Modules:
  0.0 23.9 jit_solution(16414024787375251837)
XLA Ops:
  0.0 0.0 copy-start
  0.0 22.4 %exchange.1.summed = bf16[384,256]{1,0:T(8,128)(2,1)S(1)} custom-call(bf16[3,128,1024]{2,1,0:T(8,128)(2,1)} %bitcast.7, bf16[3,128,1024]{2,1,0:T(8,128)(2,1)} %bitcast.8, bf16[1024,256]{1,0:T(8,128)(2,1)} %constant.4.clone.table_hbm, s32[16,128]{1,0:T(8,128)} %first_hbm.1, s32[16,128]{1,0:T(8,128)} %second_hbm.1, s32[16,128]{1,0:T(8,128)} %mask_hbm.1, ...), custom_call_target="tpu_custom_call" | custom-call | flops 2000000000 | bytes 3000000 | tf_op jit(solution)/shard_map/exchange/pallas_call | solution.py:563
  22.5 0.0 copy-done
  22.5 1.4 %finish.1 = f32[384,1024]{1,0:T(8,128)} custom-call(bf16[384,256]{1,0:T(8,128)(2,1)S(1)} %exchange.1.summed, bf16[256,1024]{1,0:T(8,128)(2,1)S(1)} %copy-done), custom_call_target="tpu_custom_call" | custom-call | flops 700000000 | bytes 3000000 | tf_op jit(solution)/shard_map/finish/pallas_call | solution.py:630
Async XLA Ops:
  0.0 22.5 %copy-start = (bf16[256,1024]{1,0:T(8,128)(2,1)S(1)}, bf16[256,1024]{1,0:T(8,128)(2,1)}, u32[]{:S(2)}) copy-start(bf16[256,1024]{1,0:T(8,128)(2,1)} %constant.5.clone.table) | copy-start | bytes 1572868

commit v19 on v18

--- a/solution.py
+++ b/solution.py
@@ -251,6 +251,18 @@
 
     start_halos(0)
 
+    def answer(there, carry):
+        kind = jnp.where(lax.div(there, 4) == z, 0, jnp.where(z == 1, 1, 2))
+        pl.semaphore_signal(
+            entered.at[kind], inc=1, device_id=(there, sub), device_id_type=MESH
+        )
+        return carry
+
+    @pl.when(z < 3)
+    def _():
+        lax.fori_loop(0, blk, answer, 0)
+
+
     for i in range(3, 5):
         loads[i].wait()
     lane = lax.broadcasted_iota(jnp.int32, (rows, rows), 1)
@@ -330,14 +342,9 @@
     def _():
         halo[:, BLOCK:] = jnp.zeros((6, BLOCK, 2 * NF), BF16)
 
-    def answer(there, carry):
-        kind = jnp.where(lax.div(there, 4) == z, 0, jnp.where(z == 1, 1, 2))
-        pl.semaphore_signal(
-            entered.at[kind], inc=1, device_id=(there, sub), device_id_type=MESH
-        )
-        return carry
-
-    lax.fori_loop(0, blk, answer, 0)
+    @pl.when(z == 3)
+    def _():
+        lax.fori_loop(0, blk, answer, 0)
 
     def tell_row(which):
         for there in subs_there:
@@ -440,8 +447,13 @@
 
     handle((2,))
 
-    pl.semaphore_wait(entered.at[2], 1 + jnp.where(z < 2, 8, jnp.where(z == 2, 4, 0)))
-    tell_row(1)
+    def rest_entered(answers):
+        pl.semaphore_wait(entered.at[2], 1 + answers)
+        tell_row(1)
+
+    @pl.when(z >= 2)
+    def _():
+        rest_entered(jnp.where(z == 2, 4, 0))
 
     def turns(at, size):
         return [at] + [around(at, step, size) for step in range(1, size)]
@@ -473,6 +485,11 @@
 
     pl.semaphore_wait(joined.at[0], subs - 1)
     deliver_plane(0)
+
+    @pl.when(z < 2)
+    def _():
+        rest_entered(8)
+
     some = pl.ds(0, 3)
     pltpu.make_async_copy(labels.at[0, some], labels.at[0, some], y_recv).wait()
     for step in range(1, 4):

time: 24 us -> 24 us (level)
  no operation moved by 1% of the time
where the time goes in v19:
time: 24 us; the launch traced here: 23.9 us
  Pallas kernels  23.9 us (100%)
    pallas_call x1, Pallas kernels, exchange(): pl.pallas_call(functools.partial(exchange_kernel, blks, subs), out_shape=...  22.4 us
    pallas_call x1, Pallas kernels, finish(): pl.pallas_call(finish_kernel, out_shape=jax.ShapeDtypeStruct((count, samp...  1.44 us

profile of v19, /device:TPU:1, one launch (start us, length us, event | category | flops | bytes accessed | tf_op | source)
XLA Modules:
  0.0 23.9 jit_solution(2149872690542675909)
XLA Ops:
  0.0 0.0 copy-start
  0.0 22.4 %exchange.1.summed = bf16[384,256]{1,0:T(8,128)(2,1)S(1)} custom-call(bf16[3,128,1024]{2,1,0:T(8,128)(2,1)} %bitcast.7, bf16[3,128,1024]{2,1,0:T(8,128)(2,1)} %bitcast.8, bf16[1024,256]{1,0:T(8,128)(2,1)} %constant.4.clone.table_hbm, s32[16,128]{1,0:T(8,128)} %first_hbm.1, s32[16,128]{1,0:T(8,128)} %second_hbm.1, s32[16,128]{1,0:T(8,128)} %mask_hbm.1, ...), custom_call_target="tpu_custom_call" | custom-call | flops 2000000000 | bytes 3000000 | tf_op jit(solution)/shard_map/exchange/pallas_call | solution.py:580
  22.4 0.0 copy-done
  22.4 1.4 %finish.1 = f32[384,1024]{1,0:T(8,128)} custom-call(bf16[384,256]{1,0:T(8,128)(2,1)S(1)} %exchange.1.summed, bf16[256,1024]{1,0:T(8,128)(2,1)S(1)} %copy-done), custom_call_target="tpu_custom_call" | custom-call | flops 700000000 | bytes 3000000 | tf_op jit(solution)/shard_map/finish/pallas_call | solution.py:647
Async XLA Ops:
  0.0 22.4 %copy-start = (bf16[256,1024]{1,0:T(8,128)(2,1)S(1)}, bf16[256,1024]{1,0:T(8,128)(2,1)}, u32[]{:S(2)}) copy-start(bf16[256,1024]{1,0:T(8,128)(2,1)} %constant.5.clone.table) | copy-start | bytes 1572868

commit v20 on v19

--- a/solution.py
+++ b/solution.py
@@ -197,7 +197,7 @@
     def _():
         greet((blk_after, 0))
 
-    for i in range(3):
+    for i in (0, 2):
         pl.semaphore_signal(entered.at[i], inc=1)
     greetings = (
         (subs - 1)
@@ -206,6 +206,20 @@
         + blk
     )
 
+    pl.semaphore_wait(barrier, greetings)
+
+    def answer(there, carry):
+        kind = jnp.where(lax.div(there, 4) == z, 0, jnp.where(z == 1, 1, 2))
+        pl.semaphore_signal(
+            entered.at[kind], inc=1, device_id=(there, sub), device_id_type=MESH
+        )
+        return carry
+
+    @pl.when(z < 3)
+    def _():
+        lax.fori_loop(0, blk, answer, 0)
+
+
     def transform(c):
         both = dot_plain(traces[c], table[...]).astype(BF16)
         spec[2 * c] = both[:rows]
@@ -215,7 +229,6 @@
         loads[i].wait()
     transform(0)
 
-    pl.semaphore_wait(barrier, greetings)
 
     def halo_copies(c):
         q = pl.ds(2 * c, 2)
@@ -251,18 +264,6 @@
 
     start_halos(0)
 
-    def answer(there, carry):
-        kind = jnp.where(lax.div(there, 4) == z, 0, jnp.where(z == 1, 1, 2))
-        pl.semaphore_signal(
-            entered.at[kind], inc=1, device_id=(there, sub), device_id_type=MESH
-        )
-        return carry
-
-    @pl.when(z < 3)
-    def _():
-        lax.fori_loop(0, blk, answer, 0)
-
-
     for i in range(3, 5):
         loads[i].wait()
     lane = lax.broadcasted_iota(jnp.int32, (rows, rows), 1)
@@ -352,9 +353,13 @@
                 joined.at[which], inc=1, device_id=(blk, there), device_id_type=MESH
             )
 
+    @pl.when(z >= 1)
+    def _():
+        tell_row(0)
+
     @pl.when(z >= 2)
     def _():
-        tell_row(0)
+        tell_row(1)
 
     rank_row = jnp.sum(jnp.where(same & (line < lane), 1, 0), axis=0, keepdims=True)
     target = owner_row * 4 + rank_row * 2
@@ -368,6 +373,11 @@
 
     others = pl.ds(0, subs - 1)
     pltpu.make_async_copy(lists.at[others], lists.at[others], list_recv).wait()
+
+    @pl.when(z < 2)
+    def _():
+        pl.semaphore_wait(entered.at[0], 4 - y)
+        tell_row(z)
 
     @pl.when((sub == 0) & row_before)
     def _():
@@ -427,7 +437,10 @@
 
     handle((0, 1))
 
-    pl.semaphore_wait(entered.at[0], 4 - y)
+    @pl.when(z >= 2)
+    def _():
+        pl.semaphore_wait(entered.at[0], 4 - y)
+
     labels[z, y] = jnp.concatenate([lists[:, 6, :], lists[:, 7, :]], axis=0).astype(BF16)
     for step in range(1, 4):
         pltpu.make_async_remote_copy(
@@ -439,17 +452,16 @@
             device_id_type=MESH,
         ).start()
 
-    pl.semaphore_wait(entered.at[1], 1 + jnp.where(z == 0, 4, 0))
-
-    @pl.when(z < 2)
-    def _():
-        tell_row(0)
+    @pl.when(z == 0)
+    def _():
+        pl.semaphore_wait(entered.at[1], 4)
+        tell_row(1)
 
     handle((2,))
 
     def rest_entered(answers):
         pl.semaphore_wait(entered.at[2], 1 + answers)
-        tell_row(1)
+        tell_row(2)
 
     @pl.when(z >= 2)
     def _():
@@ -502,8 +514,9 @@
             device_id_type=MESH,
         ).start()
 
+    pl.semaphore_wait(joined.at[1], subs - 1)
     deliver_plane(1)
-    pl.semaphore_wait(joined.at[1], subs - 1)
+    pl.semaphore_wait(joined.at[2], subs - 1)
     deliver_plane(2)
     deliver_plane(3)
 
@@ -608,7 +621,7 @@
             dma((2, 3)),
             dma((2, 3)),
             pltpu.SemaphoreType.REGULAR((3,)),
-            pltpu.SemaphoreType.REGULAR((2,)),
+            pltpu.SemaphoreType.REGULAR((3,)),
             dma,
             dma,
             dma,

time: 24 us -> 24.2 us (level)
    pallas_call x1, Pallas kernels: 22.4 us -> 22.7 us  [exchange(): pl.pallas_call(functools.partial(exchange_kernel, blks, subs), out_shape=...]
where the time goes in v20:
time: 24.2 us; the launch traced here: 24.1 us
  Pallas kernels  24.1 us (100%)
    pallas_call x1, Pallas kernels, exchange(): pl.pallas_call(functools.partial(exchange_kernel, blks, subs), out_shape=...  22.7 us
    pallas_call x1, Pallas kernels, finish(): pl.pallas_call(finish_kernel, out_shape=jax.ShapeDtypeStruct((count, samp...  1.44 us

profile of v20, /device:TPU:1, one launch (start us, length us, event | category | flops | bytes accessed | tf_op | source)
XLA Modules:
  0.0 24.1 jit_solution(1578815617318837448)
XLA Ops:
  0.0 0.0 copy-start
  0.0 22.7 %exchange.1.summed = bf16[384,256]{1,0:T(8,128)(2,1)S(1)} custom-call(bf16[3,128,1024]{2,1,0:T(8,128)(2,1)} %bitcast.7, bf16[3,128,1024]{2,1,0:T(8,128)(2,1)} %bitcast.8, bf16[1024,256]{1,0:T(8,128)(2,1)} %constant.4.clone.table_hbm, s32[16,128]{1,0:T(8,128)} %first_hbm.1, s32[16,128]{1,0:T(8,128)} %second_hbm.1, s32[16,128]{1,0:T(8,128)} %mask_hbm.1, ...), custom_call_target="tpu_custom_call" | custom-call | flops 2000000000 | bytes 3000000 | tf_op jit(solution)/shard_map/exchange/pallas_call | solution.py:593
  22.7 0.0 copy-done
  22.7 1.4 %finish.1 = f32[384,1024]{1,0:T(8,128)} custom-call(bf16[384,256]{1,0:T(8,128)(2,1)S(1)} %exchange.1.summed, bf16[256,1024]{1,0:T(8,128)(2,1)S(1)} %copy-done), custom_call_target="tpu_custom_call" | custom-call | flops 700000000 | bytes 3000000 | tf_op jit(solution)/shard_map/finish/pallas_call | solution.py:660
Async XLA Ops:
  0.0 22.7 %copy-start = (bf16[256,1024]{1,0:T(8,128)(2,1)S(1)}, bf16[256,1024]{1,0:T(8,128)(2,1)}, u32[]{:S(2)}) copy-start(bf16[256,1024]{1,0:T(8,128)(2,1)} %constant.5.clone.table) | copy-start | bytes 1572868

commit v21 on v19

--- a/solution.py
+++ b/solution.py
@@ -475,16 +475,20 @@
             device_id_type=MESH,
         ).start()
 
-    def deliver_plane(plane):
-        for step in spread_order():
-            deliver(plane, step)
-
-        @pl.when(z != plane)
-        def _():
-            deliver(plane, (0, 0, 0))
-
+    def deliver_planes(planes, steps):
+        for step in steps:
+            for plane in planes:
+                if step != (0, 0, 0):
+                    deliver(plane, step)
+                    continue
+
+                @pl.when(z != plane)
+                def _():
+                    deliver(plane, step)
+
+    order = spread_order() + [(0, 0, 0)]
     pl.semaphore_wait(joined.at[0], subs - 1)
-    deliver_plane(0)
+    deliver_planes((0, 1), order[:16])
 
     @pl.when(z < 2)
     def _():
@@ -502,10 +506,9 @@
             device_id_type=MESH,
         ).start()
 
-    deliver_plane(1)
+    deliver_planes((0, 1), order[16:])
     pl.semaphore_wait(joined.at[1], subs - 1)
-    deliver_plane(2)
-    deliver_plane(3)
+    deliver_planes((2, 3), order)
 
     pltpu.make_async_copy(labels.at[some], labels.at[some], z_recv).wait()
     by_owner = labels[...].reshape(2 * devices, NF)

time: 24 us -> 24.6 us (1.025)
  Pallas kernels: 23.9 us -> 24.5 us
    pallas_call x1, Pallas kernels: 22.4 us -> 23.1 us  [exchange(): pl.pallas_call(functools.partial(exchange_kernel, blks, subs), out_shape=...]
where the time goes in v21:
time: 24.6 us; the launch traced here: 24.5 us
  Pallas kernels  24.5 us (100%)
    pallas_call x1, Pallas kernels, exchange(): pl.pallas_call(functools.partial(exchange_kernel, blks, subs), out_shape=...  23.1 us
    pallas_call x1, Pallas kernels, finish(): pl.pallas_call(finish_kernel, out_shape=jax.ShapeDtypeStruct((count, samp...  1.44 us

profile of v21, /device:TPU:1, one launch (start us, length us, event | category | flops | bytes accessed | tf_op | source)
XLA Modules:
  0.0 24.5 jit_solution(2553247897197721206)
XLA Ops:
  0.0 0.0 copy-start
  0.0 23.1 %exchange.1.summed = bf16[384,256]{1,0:T(8,128)(2,1)S(1)} custom-call(bf16[3,128,1024]{2,1,0:T(8,128)(2,1)} %bitcast.7, bf16[3,128,1024]{2,1,0:T(8,128)(2,1)} %bitcast.8, bf16[1024,256]{1,0:T(8,128)(2,1)} %constant.4.clone.table_hbm, s32[16,128]{1,0:T(8,128)} %first_hbm.1, s32[16,128]{1,0:T(8,128)} %second_hbm.1, s32[16,128]{1,0:T(8,128)} %mask_hbm.1, ...), custom_call_target="tpu_custom_call" | custom-call | flops 2000000000 | bytes 3000000 | tf_op jit(solution)/shard_map/exchange/pallas_call | solution.py:583
  23.1 0.0 copy-done
  23.1 1.4 %finish.1 = f32[384,1024]{1,0:T(8,128)} custom-call(bf16[384,256]{1,0:T(8,128)(2,1)S(1)} %exchange.1.summed, bf16[256,1024]{1,0:T(8,128)(2,1)S(1)} %copy-done), custom_call_target="tpu_custom_call" | custom-call | flops 700000000 | bytes 3000000 | tf_op jit(solution)/shard_map/finish/pallas_call | solution.py:650
Async XLA Ops:
  0.0 23.1 %copy-start = (bf16[256,1024]{1,0:T(8,128)(2,1)S(1)}, bf16[256,1024]{1,0:T(8,128)(2,1)}, u32[]{:S(2)}) copy-start(bf16[256,1024]{1,0:T(8,128)(2,1)} %constant.5.clone.table) | copy-start | bytes 1572868

commit v22 on v19

--- a/solution.py
+++ b/solution.py
@@ -75,19 +75,16 @@
 
 
 def spread_order():
-    left = list(itertools.product(range(4), range(4), range(2)))[1:]
-    ways = {0: (0.0, 0.0), 1: (1.0, 0.0), 2: (1.0, 1.0), 3: (0.0, 1.0)}
-
-    def links(step):
-        return np.array([way for axis in step[:2] for way in ways[axis]])
-
-    used, order = np.zeros(4), []
-    while left:
-        step = min(left, key=lambda t: (np.max(used + links(t)), -np.sum(links(t)), t))
-        left.remove(step)
-        used = used + links(step)
-        order.append(step)
-    return order
+    entered = ((0.0, 0.65, 1.1, 1.5), (0.0, 0.8, 1.2, 1.25))
+
+    def lead(step):
+        return sum(
+            max(at[source] - at[(source + by) % 4] for source in range(4))
+            for at, by in zip(entered, step)
+        )
+
+    steps = list(itertools.product(range(4), range(4), range(2)))[1:]
+    return sorted(steps, key=lambda step: (-lead(step), step))
 
 
 def exchange_kernel(

time: 24 us -> 24.1 us (level)
  no operation moved by 1% of the time
where the time goes in v22:
time: 24.1 us; the launch traced here: 23.9 us
  Pallas kernels  23.9 us (99%)
    pallas_call x1, Pallas kernels, exchange(): pl.pallas_call(functools.partial(exchange_kernel, blks, subs), out_shape=...  22.5 us
    pallas_call x1, Pallas kernels, finish(): pl.pallas_call(finish_kernel, out_shape=jax.ShapeDtypeStruct((count, samp...  1.44 us

profile of v22, /device:TPU:1, one launch (start us, length us, event | category | flops | bytes accessed | tf_op | source)
XLA Modules:
  0.0 23.9 jit_solution(11650102967338577738)
XLA Ops:
  0.0 0.0 copy-start
  0.0 22.5 %exchange.1.summed = bf16[384,256]{1,0:T(8,128)(2,1)S(1)} custom-call(bf16[3,128,1024]{2,1,0:T(8,128)(2,1)} %bitcast.7, bf16[3,128,1024]{2,1,0:T(8,128)(2,1)} %bitcast.8, bf16[1024,256]{1,0:T(8,128)(2,1)} %constant.4.clone.table_hbm, s32[16,128]{1,0:T(8,128)} %first_hbm.1, s32[16,128]{1,0:T(8,128)} %second_hbm.1, s32[16,128]{1,0:T(8,128)} %mask_hbm.1, ...), custom_call_target="tpu_custom_call" | custom-call | flops 2000000000 | bytes 3000000 | tf_op jit(solution)/shard_map/exchange/pallas_call | solution.py:577
  22.5 0.0 copy-done
  22.5 1.4 %finish.1 = f32[384,1024]{1,0:T(8,128)} custom-call(bf16[384,256]{1,0:T(8,128)(2,1)S(1)} %exchange.1.summed, bf16[256,1024]{1,0:T(8,128)(2,1)S(1)} %copy-done), custom_call_target="tpu_custom_call" | custom-call | flops 700000000 | bytes 3000000 | tf_op jit(solution)/shard_map/finish/pallas_call | solution.py:644
Async XLA Ops:
  0.0 22.5 %copy-start = (bf16[256,1024]{1,0:T(8,128)(2,1)S(1)}, bf16[256,1024]{1,0:T(8,128)(2,1)}, u32[]{:S(2)}) copy-start(bf16[256,1024]{1,0:T(8,128)(2,1)} %constant.5.clone.table) | copy-start | bytes 1572868

commit v23 on v19

--- a/solution.py
+++ b/solution.py
@@ -369,6 +369,18 @@
     others = pl.ds(0, subs - 1)
     pltpu.make_async_copy(lists.at[others], lists.at[others], list_recv).wait()
 
+    pl.semaphore_wait(entered.at[0], 4 - y)
+    labels[z, y] = jnp.concatenate([lists[:, 6, :], lists[:, 7, :]], axis=0).astype(BF16)
+    for step in range(1, 4):
+        pltpu.make_async_remote_copy(
+            src_ref=labels.at[z, y],
+            dst_ref=labels.at[z, y],
+            send_sem=y_send,
+            recv_sem=y_recv,
+            device_id=(z * 4 + around(y, step, 4), sub),
+            device_id_type=MESH,
+        ).start()
+
     @pl.when((sub == 0) & row_before)
     def _():
         pltpu.make_async_copy(lists_prev, lists_prev, over_recv).wait()
@@ -427,18 +439,6 @@
 
     handle((0, 1))
 
-    pl.semaphore_wait(entered.at[0], 4 - y)
-    labels[z, y] = jnp.concatenate([lists[:, 6, :], lists[:, 7, :]], axis=0).astype(BF16)
-    for step in range(1, 4):
-        pltpu.make_async_remote_copy(
-            src_ref=labels.at[z, y],
-            dst_ref=labels.at[z, y],
-            send_sem=y_send,
-            recv_sem=y_recv,
-            device_id=(z * 4 + around(y, step, 4), sub),
-            device_id_type=MESH,
-        ).start()
-
     pl.semaphore_wait(entered.at[1], 1 + jnp.where(z == 0, 4, 0))
 
     @pl.when(z < 2)
@@ -475,8 +475,10 @@
             device_id_type=MESH,
         ).start()
 
-    def deliver_plane(plane):
-        for step in spread_order():
+    order = spread_order()
+
+    def deliver_plane(plane, steps):
+        for step in steps:
             deliver(plane, step)
 
         @pl.when(z != plane)
@@ -484,7 +486,8 @@
             deliver(plane, (0, 0, 0))
 
     pl.semaphore_wait(joined.at[0], subs - 1)
-    deliver_plane(0)
+    for step in order[:12]:
+        deliver(0, step)
 
     @pl.when(z < 2)
     def _():
@@ -502,13 +505,12 @@
             device_id_type=MESH,
         ).start()
 
-    deliver_plane(1)
+    deliver_plane(0, order[12:])
+    deliver_plane(1, order)
     pl.semaphore_wait(joined.at[1], subs - 1)
-    deliver_plane(2)
-    deliver_plane(3)
-
-    pltpu.make_async_copy(labels.at[some], labels.at[some], z_recv).wait()
-    by_owner = labels[...].reshape(2 * devices, NF)
+    deliver_plane(2, order)
+    deliver_plane(3, order)
+
     arrived = lax.broadcasted_iota(jnp.int32, (2 * devices, 2 * devices), 1)
     held = lax.broadcasted_iota(jnp.int32, (2 * devices, 2 * devices), 0)
     sub_bits = subs.bit_length() - 1
@@ -518,11 +520,14 @@
         + (((arrived >> 2) & (subs // 2 - 1)) << 1)
     )
     owner_line = lax.broadcasted_iota(jnp.int32, (rows, 2 * devices), 0)
-
-    def collector(source_core):
+    repeat = [(held == wanted + of).astype(F32).astype(BF16) for of in (core, 1 - core)]
+    pltpu.make_async_copy(labels.at[some], labels.at[some], z_recv).wait()
+    by_owner = labels[...].reshape(2 * devices, NF)
+
+    def collector(repeat):
         repeated = lax.dot_general(
             by_owner,
-            (held == wanted + source_core).astype(F32).astype(BF16),
+            repeat,
             (((0,), (0,)), ((), ())),
             preferred_element_type=F32,
         )
@@ -535,7 +540,7 @@
             axis=0,
         ).astype(BF16)
 
-    collect_other, collect_same = collector(1 - core), collector(core)
+    collect_other, collect_same = collector(repeat[1]), collector(repeat[0])
 
     def sums(collect, source_core):
         values = [received[source_core, :, c].reshape(2 * devices, NF) for c in range(3)]

time: 24 us -> 23.4 us (0.975)
  Pallas kernels: 23.9 us -> 23.2 us
    pallas_call x1, Pallas kernels: 22.4 us -> 21.8 us  [exchange(): pl.pallas_call(functools.partial(exchange_kernel, blks, subs), out_shape=...]
where the time goes in v23:
time: 23.4 us; the launch traced here: 23.2 us
  Pallas kernels  23.2 us (99%)
    pallas_call x1, Pallas kernels, exchange(): pl.pallas_call(functools.partial(exchange_kernel, blks, subs), out_shape=...  21.8 us
    pallas_call x1, Pallas kernels, finish(): pl.pallas_call(finish_kernel, out_shape=jax.ShapeDtypeStruct((count, samp...  1.44 us

profile of v23, /device:TPU:1, one launch (start us, length us, event | category | flops | bytes accessed | tf_op | source)
XLA Modules:
  0.0 23.2 jit_solution(12421069933901535692)
XLA Ops:
  0.0 0.0 copy-start
  0.0 21.8 %exchange.1.summed = bf16[384,256]{1,0:T(8,128)(2,1)S(1)} custom-call(bf16[3,128,1024]{2,1,0:T(8,128)(2,1)} %bitcast.7, bf16[3,128,1024]{2,1,0:T(8,128)(2,1)} %bitcast.8, bf16[1024,256]{1,0:T(8,128)(2,1)} %constant.4.clone.table_hbm, s32[16,128]{1,0:T(8,128)} %first_hbm.1, s32[16,128]{1,0:T(8,128)} %second_hbm.1, s32[16,128]{1,0:T(8,128)} %mask_hbm.1, ...), custom_call_target="tpu_custom_call" | custom-call | flops 2000000000 | bytes 3000000 | tf_op jit(solution)/shard_map/exchange/pallas_call | solution.py:585
  21.8 0.0 copy-done
  21.8 1.4 %finish.1 = f32[384,1024]{1,0:T(8,128)} custom-call(bf16[384,256]{1,0:T(8,128)(2,1)S(1)} %exchange.1.summed, bf16[256,1024]{1,0:T(8,128)(2,1)S(1)} %copy-done), custom_call_target="tpu_custom_call" | custom-call | flops 700000000 | bytes 3000000 | tf_op jit(solution)/shard_map/finish/pallas_call | solution.py:652
Async XLA Ops:
  0.0 21.8 %copy-start = (bf16[256,1024]{1,0:T(8,128)(2,1)S(1)}, bf16[256,1024]{1,0:T(8,128)(2,1)}, u32[]{:S(2)}) copy-start(bf16[256,1024]{1,0:T(8,128)(2,1)} %constant.5.clone.table) | copy-start | bytes 1572868

commit v24 on v23

--- a/solution.py
+++ b/solution.py
@@ -477,16 +477,18 @@
 
     order = spread_order()
 
-    def deliver_plane(plane, steps):
+    def deliver_planes(planes, steps):
         for step in steps:
-            deliver(plane, step)
-
-        @pl.when(z != plane)
-        def _():
-            deliver(plane, (0, 0, 0))
+            for plane in planes:
+                deliver(plane, step)
+        for plane in planes:
+
+            @pl.when(z != plane)
+            def _():
+                deliver(plane, (0, 0, 0))
 
     pl.semaphore_wait(joined.at[0], subs - 1)
-    for step in order[:12]:
+    for step in order[:20]:
         deliver(0, step)
 
     @pl.when(z < 2)
@@ -505,11 +507,10 @@
             device_id_type=MESH,
         ).start()
 
-    deliver_plane(0, order[12:])
-    deliver_plane(1, order)
+    deliver_planes((0,), order[20:])
+    deliver_planes((1,), order)
     pl.semaphore_wait(joined.at[1], subs - 1)
-    deliver_plane(2, order)
-    deliver_plane(3, order)
+    deliver_planes((2, 3), order)
 
     arrived = lax.broadcasted_iota(jnp.int32, (2 * devices, 2 * devices), 1)
     held = lax.broadcasted_iota(jnp.int32, (2 * devices, 2 * devices), 0)

time: 23.4 us -> 23.4 us (level)
  no operation moved by 1% of the time
where the time goes in v24:
time: 23.4 us; the launch traced here: 23.3 us
  Pallas kernels  23.3 us (100%)
    pallas_call x1, Pallas kernels, exchange(): pl.pallas_call(functools.partial(exchange_kernel, blks, subs), out_shape=...  21.8 us
    pallas_call x1, Pallas kernels, finish(): pl.pallas_call(finish_kernel, out_shape=jax.ShapeDtypeStruct((count, samp...  1.44 us

profile of v24, /device:TPU:1, one launch (start us, length us, event | category | flops | bytes accessed | tf_op | source)
XLA Modules:
  0.0 23.3 jit_solution(11366439507786578142)
XLA Ops:
  0.0 0.0 copy-start
  0.0 21.8 %exchange.1.summed = bf16[384,256]{1,0:T(8,128)(2,1)S(1)} custom-call(bf16[3,128,1024]{2,1,0:T(8,128)(2,1)} %bitcast.7, bf16[3,128,1024]{2,1,0:T(8,128)(2,1)} %bitcast.8, bf16[1024,256]{1,0:T(8,128)(2,1)} %constant.4.clone.table_hbm, s32[16,128]{1,0:T(8,128)} %first_hbm.1, s32[16,128]{1,0:T(8,128)} %second_hbm.1, s32[16,128]{1,0:T(8,128)} %mask_hbm.1, ...), custom_call_target="tpu_custom_call" | custom-call | flops 2000000000 | bytes 3000000 | tf_op jit(solution)/shard_map/exchange/pallas_call | solution.py:586
  21.9 0.0 copy-done
  21.9 1.4 %finish.1 = f32[384,1024]{1,0:T(8,128)} custom-call(bf16[384,256]{1,0:T(8,128)(2,1)S(1)} %exchange.1.summed, bf16[256,1024]{1,0:T(8,128)(2,1)S(1)} %copy-done), custom_call_target="tpu_custom_call" | custom-call | flops 700000000 | bytes 3000000 | tf_op jit(solution)/shard_map/finish/pallas_call | solution.py:653
Async XLA Ops:
  0.0 21.9 %copy-start = (bf16[256,1024]{1,0:T(8,128)(2,1)S(1)}, bf16[256,1024]{1,0:T(8,128)(2,1)}, u32[]{:S(2)}) copy-start(bf16[256,1024]{1,0:T(8,128)(2,1)} %constant.5.clone.table) | copy-start | bytes 1572868

commit v25 on v24

--- a/solution.py
+++ b/solution.py
@@ -488,26 +488,34 @@
                 deliver(plane, (0, 0, 0))
 
     pl.semaphore_wait(joined.at[0], subs - 1)
-    for step in order[:20]:
+    some = pl.ds(0, 3)
+
+    def labels_along_z():
+        pltpu.make_async_copy(labels.at[0, some], labels.at[0, some], y_recv).wait()
+        for step in range(1, 4):
+            pltpu.make_async_remote_copy(
+                src_ref=labels.at[z],
+                dst_ref=labels.at[z],
+                send_sem=z_send,
+                recv_sem=z_recv,
+                device_id=(around(z, step, 4) * 4 + y, sub),
+                device_id_type=MESH,
+            ).start()
+
+    for step in order[:14]:
         deliver(0, step)
 
+    @pl.when(z >= 2)
+    def _():
+        labels_along_z()
+
+    deliver_planes((0,), order[14:])
+
     @pl.when(z < 2)
     def _():
         rest_entered(8)
-
-    some = pl.ds(0, 3)
-    pltpu.make_async_copy(labels.at[0, some], labels.at[0, some], y_recv).wait()
-    for step in range(1, 4):
-        pltpu.make_async_remote_copy(
-            src_ref=labels.at[z],
-            dst_ref=labels.at[z],
-            send_sem=z_send,
-            recv_sem=z_recv,
-            device_id=(around(z, step, 4) * 4 + y, sub),
-            device_id_type=MESH,
-        ).start()
-
-    deliver_planes((0,), order[20:])
+        labels_along_z()
+
     deliver_planes((1,), order)
     pl.semaphore_wait(joined.at[1], subs - 1)
     deliver_planes((2, 3), order)

time: 23.4 us -> 23.4 us (level)
  no operation moved by 1% of the time
where the time goes in v25:
time: 23.4 us; the launch traced here: 23.3 us
  Pallas kernels  23.3 us (100%)
    pallas_call x1, Pallas kernels, exchange(): pl.pallas_call(functools.partial(exchange_kernel, blks, subs), out_shape=...  21.8 us
    pallas_call x1, Pallas kernels, finish(): pl.pallas_call(finish_kernel, out_shape=jax.ShapeDtypeStruct((count, samp...  1.44 us

profile of v25, /device:TPU:1, one launch (start us, length us, event | category | flops | bytes accessed | tf_op | source)
XLA Modules:
  0.0 23.3 jit_solution(4220027903171450662)
XLA Ops:
  0.0 0.0 copy-start
  0.0 21.8 %exchange.1.summed = bf16[384,256]{1,0:T(8,128)(2,1)S(1)} custom-call(bf16[3,128,1024]{2,1,0:T(8,128)(2,1)} %bitcast.7, bf16[3,128,1024]{2,1,0:T(8,128)(2,1)} %bitcast.8, bf16[1024,256]{1,0:T(8,128)(2,1)} %constant.4.clone.table_hbm, s32[16,128]{1,0:T(8,128)} %first_hbm.1, s32[16,128]{1,0:T(8,128)} %second_hbm.1, s32[16,128]{1,0:T(8,128)} %mask_hbm.1, ...), custom_call_target="tpu_custom_call" | custom-call | flops 2000000000 | bytes 3000000 | tf_op jit(solution)/shard_map/exchange/pallas_call | solution.py:594
  21.8 0.0 copy-done
  21.8 1.4 %finish.1 = f32[384,1024]{1,0:T(8,128)} custom-call(bf16[384,256]{1,0:T(8,128)(2,1)S(1)} %exchange.1.summed, bf16[256,1024]{1,0:T(8,128)(2,1)S(1)} %copy-done), custom_call_target="tpu_custom_call" | custom-call | flops 700000000 | bytes 3000000 | tf_op jit(solution)/shard_map/finish/pallas_call | solution.py:661
Async XLA Ops:
  0.0 21.8 %copy-start = (bf16[256,1024]{1,0:T(8,128)(2,1)S(1)}, bf16[256,1024]{1,0:T(8,128)(2,1)}, u32[]{:S(2)}) copy-start(bf16[256,1024]{1,0:T(8,128)(2,1)} %constant.5.clone.table) | copy-start | bytes 1572868
